TPU v7x, 512 devices: a whole 4x4x16 slice. The times are simulated.
512 devices in a mesh: head: 32 (over z_lo, y, core), seq: 16 (over z_hi, x).
Axes of the slice: x: 4, y: 4, z: 16 (z_hi: 4, z_lo: 4; z = z_hi * 4 + z_lo), core: 2. Of those that a mesh axis runs over, the one named last changes fastest.
Arguments:
- query_rows: bfloat16 [2048, 16384], P('seq', 'head'), may hold values from -512 to 512
- key_rows: bfloat16 [2048, 1024], P('seq'), may hold values from -32 to 32
- value_rows: bfloat16 [2048, 1024], P('seq'), may hold values from -6 to 6
- positions: int32 [2048], P('seq'), may hold values from 0 to 511, as said below
Outputs:
- attended: bfloat16 [2048, 16384], P('seq', 'head')
- hessian: float32 [16384, 16384], P('head', 'seq')
Inputs may be any that keep to these rules, and one draw needn't show every extreme that they name: Each aligned block of 4 spans of 128 tokens is one sequence; each span holds 128 consecutive ascending positions starting at a multiple of 128, and the sequence's spans together hold every position 0 to 511 once.
All inputs are finite; a program needn't handle non-finite values.
Results may differ from a plain program's by a relative error of at most 0.0037.
Values may be sent and summed in bfloat16 or wider, within the bound.
No kernel may reach another device: no remote copies, remote signals or barrier semaphores. Data moves between devices by JAX's collectives and lax.ppermute only.
A program may use at most 64 MiB of HBM per device.

v0:
```python
import jax
import jax.numpy as jnp
from jax import lax
from jax.sharding import PartitionSpec as P

HEADS = 128
KVH = 8
HD = 128
SPANS = 4


def from_partner(value, axis, stride):
    mask = 2**stride
    pairs = [(source, source ^ mask) for source in range(lax.axis_size(axis))]
    return lax.ppermute(value, axis, pairs)


def attend_block(queries, key_block, value_block, visible, local_heads, local_tokens, score_scale):
    scores = jnp.dot(queries, key_block.T, preferred_element_type=jnp.float32) * score_scale
    scores = scores.reshape(local_heads, local_tokens, key_block.shape[0])
    masked = jnp.where(visible[None], scores, -jnp.inf)
    row_top = jnp.max(masked, axis=2, keepdims=True)
    weights = jnp.exp(masked - row_top)
    weight_sum = jnp.sum(weights, axis=2, keepdims=True)
    mixed = jnp.dot(
        weights.astype(jnp.bfloat16).reshape(local_heads * local_tokens, key_block.shape[0]),
        value_block,
        preferred_element_type=jnp.float32,
    )
    return mixed.reshape(local_heads, local_tokens, HD) / weight_sum


def on_device(query_rows, key_rows, value_rows, positions):
    local_tokens = query_rows.shape[0]
    local_heads = query_rows.shape[1] // HD
    group_size = HEADS // KVH
    score_scale = HD ** (-0.5)
    head_index = lax.axis_index("head")
    seq_devices = lax.axis_size("seq")
    head_devices = lax.axis_size("head")
    key_head = head_index * local_heads // group_size
    key_slice = lax.dynamic_slice_in_dim(key_rows, key_head * HD, HD, 1)
    value_slice = lax.dynamic_slice_in_dim(value_rows, key_head * HD, HD, 1)
    queries = jnp.transpose(query_rows.reshape(local_tokens, local_heads, HD), (1, 0, 2))
    queries = queries.reshape(local_heads * local_tokens, HD)
    key_block, value_block, place_block = (key_slice, value_slice, positions)
    for bit in range(SPANS.bit_length() - 1):
        other_keys, other_values, other_places = from_partner(
            (key_block, value_block, place_block), "seq", bit
        )
        key_block = jnp.concatenate([key_block, other_keys], axis=0)
        value_block = jnp.concatenate([value_block, other_values], axis=0)
        place_block = jnp.concatenate([place_block, other_places], axis=0)
    visible = place_block[None, :] <= positions[:, None]
    outcome = attend_block(
        queries, key_block, value_block, visible, local_heads, local_tokens, score_scale
    )
    attended = (
        jnp.transpose(outcome, (1, 0, 2))
        .reshape(local_tokens, local_heads * HD)
        .astype(jnp.bfloat16)
    )
    row_width = attended.shape[1]
    row_operand = lax.all_gather(attended, "seq", axis=0, tiled=True)
    per_slice = local_tokens // head_devices
    sectioned = attended.reshape(1, per_slice, head_devices, row_width)
    sectioned = lax.all_to_all(sectioned, "head", split_axis=2, concat_axis=3, tiled=True)
    sectioned = lax.all_to_all(sectioned, "seq", split_axis=3, concat_axis=0, tiled=True)
    row_grid = row_operand.reshape(seq_devices, per_slice, head_devices, row_width)
    hessian = lax.dot_general(
        row_grid,
        lax.all_gather(sectioned, "head", axis=2, tiled=True),
        (((0, 1, 2), (0, 1, 2)), ((), ())),
        preferred_element_type=jnp.float32,
    )
    return (attended, hessian)


def solution(mesh):
    placed = (P("seq", "head"), P("seq", None), P("seq", None), P("seq"))
    return jax.shard_map(
        on_device,
        mesh=mesh,
        in_specs=placed,
        out_specs=(P("seq", "head"), P("head", "seq")),
        check_vma=False,
    )
```

profile of v0, /device:TPU:1, one launch (start us, length us, event | category | flops | bytes accessed | tf_op | source)
XLA Modules:
  0.0 303.3 jit_solution(11701521761003018919)
XLA Ops:
  7.2 4.1 %collective-permute-start = (s32[128]{0:T(128)}, s32[128]{0:T(128)S(1)}, u32[]{:S(2)}, u32[]{:S(2)}) collective-permute-start(s32[128]{0:T(128)} %param.7), channel_id=1, source_target_pairs={{0,1},{1,0},{2,3},{3,2},{4,5},{5,4},{6,7},{7,6},{8,9},{9,8},{10,11... | collective-permute-start | bytes 1544 | tf_op jit(solution)/shard_map/ppermute | solution.py:15
  11.4 1.9 collective-permute-start.2
  14.0 4.9 %collective-permute-start.1 = (s32[256]{0:T(256)S(1)}, s32[256]{0:T(256)S(1)}, u32[]{:S(2)}, u32[]{:S(2)}) collective-permute-start(s32[256]{0:T(256)S(1)} %pad_add_fusion.1), channel_id=1, source_target_pairs={{0,2},{1,3},{2,0},{3,1},{4,6},{5,7},{6,4},{7,5},{8,10},{9,11},{10,... | collective-permute-start | bytes 3080 | tf_op jit(solution)/shard_map/ppermute | solution.py:15
  18.9 0.8 constant_dynamic-slice_fusion
  19.7 2.2 collective-permute-start.4
  22.0 1.0 copy.21
  23.8 0.8 broadcast_compare_fusion
  24.6 3.6 %collective-permute-start.3 = (bf16[256,128]{1,0:T(8,128)(2,1)S(1)}, bf16[256,128]{1,0:T(8,128)(2,1)S(1)}, u32[]{:S(2)}, u32[]{:S(2)}) collective-permute-start(bf16[256,128]{1,0:T(8,128)(2,1)S(1)} %pad_maximum_fusion), channel_id=1, source_target_pairs={{0,2},{1,3},{2,0},{3,1},{4,6},{5,7},{6,4},{7,5},{8,10},{9,11},{10,... | collective-permute-start | bytes 196616 | tf_op jit(solution)/shard_map/ppermute | solution.py:15
  28.3 3.1 %collective-permute-start.5 = (bf16[256,128]{0,1:T(8,128)(2,1)S(1)}, bf16[256,128]{0,1:T(8,128)(2,1)S(1)}, u32[]{:S(2)}, u32[]{:S(2)}) collective-permute-start(bf16[256,128]{0,1:T(8,128)(2,1)S(1)} %pad_maximum_fusion.1), channel_id=1, source_target_pairs={{0,2},{1,3},{2,0},{3,1},{4,6},{5,7},{6,4},{7,5},{8,10},{9,11},{10,... | collective-permute-start | bytes 196616 | tf_op jit(solution)/shard_map/ppermute | solution.py:15
  32.3 2.5 collective-permute-done.5
  34.8 1.0 fusion.9
  35.8 1.0 copy.25
  37.1 20.3 %all_to_all.30 = bf16[1,4,32,512]{3,1,0,2:T(4,128)(2,1)S(1)} all-to-all(bf16[1,4,32,512]{3,1,0,2:T(4,128)(2,1)S(1)} %copy.26), channel_id=1, replica_groups=mesh['head'=32,'seq'=16] {'head'}, dimensions={2} | all-to-all | bytes 262144 | tf_op jit(solution)/shard_map/all_to_all | solution.py:67
  57.3 12.9 %copy.27 = bf16[1,4,1,16384]{1,2,0,3:T(2,128)(2,1)} copy(bf16[1,4,1,16384]{3,1,2,0:T(4,128)(2,1)S(1)} %bitcast.58) | data formatting | bytes 262144 | tf_op jit(solution)/shard_map/all_to_all | solution.py:67
  70.7 90.8 %reduce.2 = bf16[16384,4]{1,0:T(8,128)(2,1)} reduce(bf16[16384,1,1,4]{3,2,1,0:T(2,128)(2,1)} %bitcast.52, bf16[]{:T(256)} %broadcast.33), dimensions={1,2}, to_apply=%bitcast.45.reduce_sub_computation | reduce | bytes 262146
  161.5 8.7 %reshape.80 = bf16[16,2,2048]{2,1,0:T(2,128)(2,1)S(1)} reshape(bf16[16384,4]{1,0:T(8,128)(2,1)} %reduce.2) | data formatting | bytes 262144
  170.2 27.8 %all_to_all.31 = bf16[16,2,2048]{2,1,0:T(2,128)(2,1)S(1)} all-to-all(bf16[16,2,2048]{2,1,0:T(2,128)(2,1)S(1)} %reshape.80), channel_id=1, replica_groups=mesh['head'=32,'seq'=16] {'seq'}, dimensions={0} | all-to-all | bytes 262144 | tf_op jit(solution)/shard_map/all_to_all | solution.py:68
  198.0 12.3 %reshape.81 = bf16[16384,1,1,4]{3,2,1,0:T(2,128)(2,1)} reshape(bf16[16,2,2048]{2,1,0:T(2,128)(2,1)S(1)} %all_to_all.31) | data formatting | bytes 262144
  210.3 15.4 %copy.28 = bf16[1,4,1,16384]{3,1,2,0:T(4,128)(2,1)S(1)} copy(bf16[1,4,1,16384]{1,2,0,3:T(2,128)(2,1)} %bitcast.53) | data formatting | bytes 262144 | tf_op jit(solution)/shard_map/all_to_all | solution.py:68
  225.7 0.7 copy.42
  226.4 0.8 copy.31
  227.2 2.9 copy.24
  230.1 57.4 %all-gather.6.cloned.1.call-done = bf16[16,1,4,32,1024]{4,0,2,1,3:T(8,128)(2,1)} async-done(((bf16[16,1,4,1,1024]{4,0,2,1,3:T(8,128)(2,1)}), bf16[16,1,4,32,1024]{4,0,2,1,3:T(8,128)(2,1)}) %all-gather.6.cloned.1.call-update) | async-done | bytes 4194320 | tf_op jit(solution)/shard_map/all_gather | solution.py:72
  287.5 9.0 %fusion.3 = f32[512,1024]{1,0:T(8,128)} fusion(bf16[16,4,32,512]{3,2,1,0:T(8,128)(2,1)S(1)} %bitcast.54, bf16[16,1,4,32,1024]{4,0,2,1,3:T(8,128)(2,1)} %all-gather.6.cloned.1.call-done), kind=kOutput, calls=%fused_computation.3 | convolution fusion | flops 2147483648 | bytes 8388608 | tf_op jit(solution)/shard_map/dot_general | solution.py:70
  (27 shorter events, 3.2 us)
Async XLA Ops:
  7.2 4.2 %copy-start = (bf16[128,1024]{1,0:T(8,128)(2,1)S(1)}, bf16[128,1024]{1,0:T(8,128)(2,1)}, u32[]{:S(2)}) copy-start(bf16[128,1024]{1,0:T(8,128)(2,1)} %param.5) | copy-start | bytes 786436
  7.2 220.0 %all-gather.4.cloned.1.call-start = ((), (), s32[]{:S(2)}) async-start(), calls=%async_computation.2 | async-start | bytes 2228224 | tf_op jit(solution)/shard_map/all_gather | solution.py:64
  7.2 6.1 %collective-permute-start = (s32[128]{0:T(128)}, s32[128]{0:T(128)S(1)}, u32[]{:S(2)}, u32[]{:S(2)}) collective-permute-start(s32[128]{0:T(128)} %param.7), channel_id=1, source_target_pairs={{0,1},{1,0},{2,3},{3,2},{4,5},{5,4},{6,7},{7,6},{8,9},{9,8},{10,11... | collective-permute-start | bytes 1544 | tf_op jit(solution)/shard_map/ppermute | solution.py:15
  11.4 13.2 %collective-permute-start.2 = (bf16[128,128]{1,0:T(8,128)(2,1)S(1)}, bf16[128,128]{1,0:T(8,128)(2,1)S(1)}, u32[]{:S(2)}, u32[]{:S(2)}) collective-permute-start(bf16[128,128]{1,0:T(8,128)(2,1)S(1)} %constant_dynamic-slice_fusion.1), channel_id=1, source_target_pairs={{0,1},{1,0},{2,3},{3,2},{4,5},{5,4},{6,7},{7,6},{8,9},{9,8},{10,11... | collective-permute-start | bytes 98312 | tf_op jit(solution)/shard_map/ppermute | solution.py:15
  14.0 9.2 %collective-permute-start.1 = (s32[256]{0:T(256)S(1)}, s32[256]{0:T(256)S(1)}, u32[]{:S(2)}, u32[]{:S(2)}) collective-permute-start(s32[256]{0:T(256)S(1)} %pad_add_fusion.1), channel_id=1, source_target_pairs={{0,2},{1,3},{2,0},{3,1},{4,6},{5,7},{6,4},{7,5},{8,10},{9,11},{10,... | collective-permute-start | bytes 3080 | tf_op jit(solution)/shard_map/ppermute | solution.py:15
  19.7 8.5 %collective-permute-start.4 = (bf16[128,128]{0,1:T(8,128)(2,1)S(1)}, bf16[128,128]{0,1:T(8,128)(2,1)S(1)}, u32[]{:S(2)}, u32[]{:S(2)}) collective-permute-start(bf16[128,128]{0,1:T(8,128)(2,1)S(1)} %copy.33), channel_id=1, source_target_pairs={{0,1},{1,0},{2,3},{3,2},{4,5},{5,4},{6,7},{7,6},{8,9},{9,8},{10,11... | collective-permute-start | bytes 98312 | tf_op jit(solution)/shard_map/ppermute | solution.py:15
  24.6 6.9 %collective-permute-start.3 = (bf16[256,128]{1,0:T(8,128)(2,1)S(1)}, bf16[256,128]{1,0:T(8,128)(2,1)S(1)}, u32[]{:S(2)}, u32[]{:S(2)}) collective-permute-start(bf16[256,128]{1,0:T(8,128)(2,1)S(1)} %pad_maximum_fusion), channel_id=1, source_target_pairs={{0,2},{1,3},{2,0},{3,1},{4,6},{5,7},{6,4},{7,5},{8,10},{9,11},{10,... | collective-permute-start | bytes 196616 | tf_op jit(solution)/shard_map/ppermute | solution.py:15
  28.3 6.5 %collective-permute-start.5 = (bf16[256,128]{0,1:T(8,128)(2,1)S(1)}, bf16[256,128]{0,1:T(8,128)(2,1)S(1)}, u32[]{:S(2)}, u32[]{:S(2)}) collective-permute-start(bf16[256,128]{0,1:T(8,128)(2,1)S(1)} %pad_maximum_fusion.1), channel_id=1, source_target_pairs={{0,2},{1,3},{2,0},{3,1},{4,6},{5,7},{6,4},{7,5},{8,10},{9,11},{10,... | collective-permute-start | bytes 196616 | tf_op jit(solution)/shard_map/ppermute | solution.py:15
  35.8 251.7 %all-gather.6.cloned.1.call-start = ((), (), s32[]{:S(2)}) async-start(), calls=%async_computation.3 | async-start | bytes 4325376 | tf_op jit(solution)/shard_map/all_gather | solution.py:72
  210.3 16.1 %copy-start.1 = (bf16[128,4,128]{0,2,1:T(8,128)(2,1)S(1)}, bf16[128,4,128]{0,2,1:T(8,128)(2,1)}, u32[]{:S(2)}) copy-start(bf16[128,4,128]{0,2,1:T(8,128)(2,1)} %fusion.9) | copy-start | bytes 393220
Sparse Core Ops, SparseCore 0:
  35.9 105.3 all-gather.3
  226.5 60.8 all-gather.5
where the time goes:
time: 304 us; the launch traced here: 303 us
  other arithmetic  93.2 us (31%)
  waiting for transfers between devices  60 us (20%)
  local copies, waits for them, and re-layouts  57.5 us (19%)
  blocking collectives  48.1 us (16%)
  starting transfers between devices  20 us (7%)
  between operations  14.3 us (5%)
  matrix products  10.4 us (3%)
    unnamed x1, other arithmetic  90.8 us
    all_gather x1, waiting for transfers between devices, on_device(): lax.all_gather(sectioned, 'head', axis=2, tiled=True)  57.4 us
    all_to_all x1, blocking collectives, on_device(): lax.all_to_all(sectioned, 'seq', split_axis=3, concat_axis=0, tiled=True)  27.8 us
    unnamed x11, local copies, waits for them, and re-layouts  24.1 us
    all_to_all x1, blocking collectives, on_device(): lax.all_to_all(sectioned, 'head', split_axis=2, concat_axis=3, tiled=True)  20.3 us
    ppermute x6, starting transfers between devices, from_partner(): return lax.ppermute(value, axis, pairs)  19.9 us
    all_to_all x1, local copies, waits for them, and re-layouts, on_device(): lax.all_to_all(sectioned, 'seq', split_axis=3, concat_axis=0, tiled=True)  15.4 us
    all_to_all x1, local copies, waits for them, and re-layouts, on_device(): lax.all_to_all(sectioned, 'head', split_axis=2, concat_axis=3, tiled=True)  12.9 us
  transfers between devices with their start and end apart: 8, of which 2 were waited for; matrix products, arithmetic and copies ran while one was open for 50% of the time, Pallas kernels for 0%

commit v1 on v0

v1 whole, which is shorter than its diff:
```python
import jax
import jax.numpy as jnp
from jax import lax
from jax.experimental import pallas as pl
from jax.experimental.pallas import tpu as pltpu
from jax.sharding import Mesh
from jax.sharding import PartitionSpec as P

HEADS = 128
KVH = 8
HD = 128
RING = 4
AXES = ("zl", "y", "core", "zh", "x")
HEAD = ("zl", "y", "core")
SEQ = ("zh", "x")
VMEM = 48 * 1024 * 1024


def pack_kernel(g_ref, k_ref, v_ref, p_ref, o_ref):
    tok = k_ref.shape[0]
    o_ref[:tok] = k_ref[...]
    o_ref[tok : 2 * tok] = v_ref[...]
    p = p_ref[...]
    high = p >> 7
    row = lax.broadcasted_iota(jnp.int32, (16, tok), 0)
    both = jnp.where(row == 0, high, p - (high << 7))
    o_ref[2 * tok :] = both.astype(jnp.float32).astype(jnp.bfloat16)


def pack(key_head, key_rows, value_rows, positions):
    tok = key_rows.shape[0]
    return pl.pallas_call(
        pack_kernel,
        out_shape=jax.ShapeDtypeStruct((2 * tok + 16, HD), jnp.bfloat16),
        grid_spec=pltpu.PrefetchScalarGridSpec(
            num_scalar_prefetch=1,
            grid=(1,),
            in_specs=[
                pl.BlockSpec((tok, HD), lambda i, g: (0, g[0])),
                pl.BlockSpec((tok, HD), lambda i, g: (0, g[0])),
                pl.BlockSpec((1, tok), lambda i, g: (0, 0)),
            ],
            out_specs=pl.BlockSpec((2 * tok + 16, HD), lambda i, g: (0, 0)),
        ),
        name="pack",
    )(key_head, key_rows, value_rows, positions.reshape(1, tok))


def attend_kernel(q_ref, kv_ref, p_ref, o_ref):
    tok, width = q_ref.shape
    spans = kv_ref.shape[0]
    keys = jnp.concatenate([kv_ref[s, :tok, :] for s in range(spans)], axis=0)
    values = jnp.concatenate([kv_ref[s, tok : 2 * tok, :] for s in range(spans)], axis=0)
    places = []
    for s in range(spans):
        both = kv_ref[s, 2 * tok :, :].astype(jnp.float32)
        places.append(both[0:1] * 128.0 + both[1:2])
    place = jnp.concatenate(places, axis=1)
    own = p_ref[...].astype(jnp.float32)
    visible = place <= own
    for h in range(width // HD):
        q = q_ref[:, h * HD : (h + 1) * HD]
        scores = lax.dot_general(
            q, keys, (((1,), (1,)), ((), ())), preferred_element_type=jnp.float32
        ) * (HD ** (-0.5))
        masked = jnp.where(visible, scores, -jnp.inf)
        top = jnp.max(masked, axis=1, keepdims=True)
        weights = jnp.exp(masked - top)
        total = jnp.sum(weights, axis=1, keepdims=True)
        mixed = jnp.dot(weights.astype(jnp.bfloat16), values, preferred_element_type=jnp.float32)
        o_ref[:, h * HD : (h + 1) * HD] = (mixed / total).astype(jnp.bfloat16)


def attend(queries, gathered, positions):
    tok, width = queries.shape
    return pl.pallas_call(
        attend_kernel,
        out_shape=jax.ShapeDtypeStruct((tok, width), jnp.bfloat16),
        compiler_params=pltpu.CompilerParams(vmem_limit_bytes=VMEM),
        name="attend",
    )(queries, gathered, positions.reshape(tok, 1))


def hessian_kernel(s_ref, r_ref, a_ref, b_ref, o_ref):
    step = pl.program_id(0)
    core = s_ref[1]
    half = a_ref.shape[2]
    contract = (((0,), (0,)), ((), ()))
    rows = r_ref[0]
    for which, ref in ((core, a_ref), (1 - core, b_ref)):
        part = lax.dot_general(rows, ref[0], contract, preferred_element_type=jnp.float32)
        cols = pl.ds(pl.multiple_of(which * half, half), half)

        @pl.when(step == 0)
        def _():
            o_ref[:, cols] = part

        @pl.when(step > 0)
        def _():
            o_ref[:, cols] += part


def hessian_of(scalars, rows, own, other):
    steps, depth, width = rows.shape
    half = own.shape[2]
    turned = lambda i, s: ((i + s[0]) & (RING - 1), 0, 0)
    return pl.pallas_call(
        hessian_kernel,
        out_shape=jax.ShapeDtypeStruct((width, 2 * half), jnp.float32),
        grid_spec=pltpu.PrefetchScalarGridSpec(
            num_scalar_prefetch=1,
            grid=(steps,),
            in_specs=[
                pl.BlockSpec((1, depth, width), lambda i, s: (i, 0, 0)),
                pl.BlockSpec((1, depth, half), turned),
                pl.BlockSpec((1, depth, half), turned),
            ],
            out_specs=pl.BlockSpec((width, 2 * half), lambda i, s: (0, 0)),
        ),
        compiler_params=pltpu.CompilerParams(vmem_limit_bytes=VMEM),
        name="hessian",
    )(scalars, rows, own, other)


def shift(value, axis, by):
    return lax.ppermute(value, axis, [(i, (i + by) % RING) for i in range(RING)])


def ring(value, axis):
    half = value.shape[0] // 2
    after = shift(value, axis, -1)
    before = shift(value, axis, 1)
    first = shift(after[:half], axis, -1)
    second = shift(before[half:], axis, 1)
    return jnp.stack([value, after, jnp.concatenate([first, second]), before])


def swap(value):
    pairs = []
    for chip in range(16):
        for core in range(2):
            for span in range(16):
                pairs.append(((chip * 2 + core) * 16 + span, (span * 2 + core) * 16 + chip))
    return lax.ppermute(value, HEAD + SEQ, pairs)


def on_device(query_rows, key_rows, value_rows, positions):
    tok = query_rows.shape[0]
    local_heads = query_rows.shape[1] // HD
    head = lax.axis_index(HEAD)
    key_head = (head * local_heads // (HEADS // KVH)).astype(jnp.int32).reshape(1)
    packed = pack(key_head, key_rows, value_rows, positions)
    gathered = lax.all_gather(packed, "x", axis=0)
    attended = attend(query_rows, gathered, positions)
    chunk = swap(attended)
    rows = lax.all_gather(attended, "zh", axis=0, tiled=True)
    cols = lax.all_gather(chunk, "zl", axis=0, tiled=True)
    own = ring(cols, "y")
    rows = ring(rows, "x")
    other = lax.ppermute(own, "core", [(0, 1), (1, 0)])
    turn = (lax.axis_index("x") - lax.axis_index("y")) & (RING - 1)
    scalars = jnp.stack([turn, lax.axis_index("core")]).astype(jnp.int32)
    return attended, hessian_of(scalars, rows, own, other)


def solution(mesh):
    fine = Mesh(mesh.devices.reshape(4, 4, 2, 4, 4), AXES)
    placed = (P(SEQ, HEAD), P(SEQ, None), P(SEQ, None), P(SEQ))
    return jax.shard_map(
        on_device,
        mesh=fine,
        in_specs=placed,
        out_specs=(P(SEQ, HEAD), P(HEAD, SEQ)),
        check_vma=False,
    )
```

time: 304 us -> 158 us (0.52)
  the two profiles are of different devices: /device:TPU:1 before, /device:TPU:46 now
where the time goes in v1:
time: 158 us; the launch traced here: 157 us
  blocking collectives  65.7 us (42%)
  starting transfers between devices  39.4 us (25%)
  waiting for transfers between devices  34.7 us (22%)
  Pallas kernels  10.6 us (7%)
  local copies, waits for them, and re-layouts  3.24 us (2%)
  other arithmetic  2.75 us (2%)
    all_gather x1, blocking collectives, on_device(): rows = lax.all_gather(attended, 'zh', axis=0, tiled=True)  31.7 us
    ppermute x8, waiting for transfers between devices, shift(): lax.ppermute(value, axis, [(i, (i + by) % RING) for i in range(RING)])  30.1 us
    ppermute x8, starting transfers between devices, shift(): lax.ppermute(value, axis, [(i, (i + by) % RING) for i in range(RING)])  27.1 us
    all_gather x1, blocking collectives, on_device(): cols = lax.all_gather(chunk, 'zl', axis=0, tiled=True)  21.5 us
    all_gather x1, blocking collectives, on_device(): gathered = lax.all_gather(packed, 'x', axis=0)  12.6 us
    ppermute x1, starting transfers between devices, swap(): return lax.ppermute(value, HEAD + SEQ, pairs)  10.4 us
    pallas_call x1, Pallas kernels, hessian_of(): pl.pallas_call(hessian_kernel, out_shape=jax.ShapeDtypeStruct((width, 2 *...  7.28 us
    ppermute x1, waiting for transfers between devices, swap(): return lax.ppermute(value, HEAD + SEQ, pairs)  4.6 us
  transfers between devices with their start and end apart: 10, of which 7 were waited for; matrix products, arithmetic and copies ran while one was open for 2% of the time, Pallas kernels for 0%

profile of v1, /device:TPU:46, one launch (start us, length us, event | category | flops | bytes accessed | tf_op | source)
XLA Modules:
  0.0 157.2 jit_solution(7232321885823687211)
XLA Ops:
  1.4 1.4 pack.1
  2.8 12.6 %all-gather = bf16[1088,128]{1,0:T(8,128)(2,1)S(1)} all-gather(bf16[272,128]{1,0:T(8,128)(2,1)} %pack.1), channel_id=2, replica_groups=mesh['zl'=4,'y'=4,'core'=2,'zh'=4,'x'=4] {'x'}, dimensions={0}, use_global_device_ids=true | all-gather | bytes 348160 | tf_op jit(solution)/shard_map/all_gather | solution.py:153
  16.3 1.8 %attend.1 = bf16[128,512]{1,0:T(8,128)(2,1)} custom-call(bf16[128,512]{1,0:T(8,128)(2,1)S(1)} %copy-done, bf16[4,272,128]{2,1,0:T(8,128)(2,1)S(1)} %bitcast.16, s32[128,1]{1,0:T(8,128)S(1)} %copy.6.p_ref), custom_call_target="tpu_custom_call" | custom-call | tf_op jit(solution)/shard_map/attend/pallas_call | solution.py:76
  18.2 10.4 %collective-permute-start.4 = (bf16[128,512]{1,0:T(8,128)(2,1)}, bf16[128,512]{1,0:T(8,128)(2,1)S(1)}, u32[]{:S(2)}, u32[]{:S(2)}) collective-permute-start(bf16[128,512]{1,0:T(8,128)(2,1)} %attend.1), channel_id=1, source_target_pairs={{0,0},{1,32},{2,64},{3,96},{4,128},{5,160},{6,192},{7,224},{8,256}... | collective-permute-start | bytes 393224 | tf_op jit(solution)/shard_map/ppermute | solution.py:144
  28.5 4.6 %collective-permute-done.4 = bf16[128,512]{1,0:T(8,128)(2,1)S(1)} collective-permute-done((bf16[128,512]{1,0:T(8,128)(2,1)}, bf16[128,512]{1,0:T(8,128)(2,1)S(1)}, u32[]{:S(2)}, u32[]{:S(2)}) %collective-permute-start.4) | collective-permute-done | bytes 131104 | tf_op jit(solution)/shard_map/ppermute | solution.py:144
  33.1 21.5 %all_gather.15 = bf16[512,512]{1,0:T(8,128)(2,1)S(1)} all-gather(bf16[128,512]{1,0:T(8,128)(2,1)S(1)} %collective-permute-done.4), channel_id=1, replica_groups=mesh['zl'=4,'y'=4,'core'=2,'zh'=4,'x'=4] {'zl'}, dimensions={0}, use_global_device_ids=true | all-gather | bytes 655360 | tf_op jit(solution)/shard_map/all_gather | solution.py:157
  54.6 1.9 %collective-permute-start.7 = (bf16[512,512]{1,0:T(8,128)(2,1)S(1)}, bf16[512,512]{1,0:T(8,128)(2,1)S(1)}, u32[]{:S(2)}, u32[]{:S(2)}) collective-permute-start(bf16[512,512]{1,0:T(8,128)(2,1)S(1)} %all_gather.15), channel_id=1, source_target_pairs={{0,32},{32,64},{64,96},{96,0},{1,33},{33,65},{65,97},{97,1},{2,34}... | collective-permute-start | bytes 1572872 | tf_op jit(solution)/shard_map/ppermute | solution.py:126
  56.5 3.9 %collective-permute-start.5 = (bf16[512,512]{1,0:T(8,128)(2,1)S(1)}, bf16[512,512]{1,0:T(8,128)(2,1)S(1)}, u32[]{:S(2)}, u32[]{:S(2)}) collective-permute-start(bf16[512,512]{1,0:T(8,128)(2,1)S(1)} %all_gather.15), channel_id=1, source_target_pairs={{0,96},{32,0},{64,32},{96,64},{1,97},{33,1},{65,33},{97,65},{2,98}... | collective-permute-start | bytes 1572872 | tf_op jit(solution)/shard_map/ppermute | solution.py:126
  60.5 8.0 %collective-permute-done.7 = bf16[512,512]{1,0:T(8,128)(2,1)S(1)} collective-permute-done((bf16[512,512]{1,0:T(8,128)(2,1)S(1)}, bf16[512,512]{1,0:T(8,128)(2,1)S(1)}, u32[]{:S(2)}, u32[]{:S(2)}) %collective-permute-start.7) | collective-permute-done | bytes 524320 | tf_op jit(solution)/shard_map/ppermute | solution.py:126
  68.5 1.9 %collective-permute-start.8 = (bf16[256,512]{1,0:T(8,128)(2,1)S(1)}, bf16[256,512]{1,0:T(8,128)(2,1)S(1)}, u32[]{:S(2)}, u32[]{:S(2)}) collective-permute-start(bf16[256,512]{1,0:T(8,128)(2,1)S(1)} %slice.19), channel_id=1, source_target_pairs={{0,32},{32,64},{64,96},{96,0},{1,33},{33,65},{65,97},{97,1},{2,34}... | collective-permute-start | bytes 786440 | tf_op jit(solution)/shard_map/ppermute | solution.py:126
  70.5 3.9 %collective-permute-start.6 = (bf16[256,512]{1,0:T(8,128)(2,1)S(1)}, bf16[256,512]{1,0:T(8,128)(2,1)S(1)}, u32[]{:S(2)}, u32[]{:S(2)}) collective-permute-start(bf16[256,512]{1,0:T(8,128)(2,1)S(1)} %slice.18), channel_id=1, source_target_pairs={{0,96},{32,0},{64,32},{96,64},{1,97},{33,1},{65,33},{97,65},{2,98}... | collective-permute-start | bytes 786440 | tf_op jit(solution)/shard_map/ppermute | solution.py:126
  74.4 2.4 %collective-permute-done.8 = bf16[256,512]{1,0:T(8,128)(2,1)S(1)} collective-permute-done((bf16[256,512]{1,0:T(8,128)(2,1)S(1)}, bf16[256,512]{1,0:T(8,128)(2,1)S(1)}, u32[]{:S(2)}, u32[]{:S(2)}) %collective-permute-start.8) | collective-permute-done | bytes 262176 | tf_op jit(solution)/shard_map/ppermute | solution.py:126
  76.8 2.0 %collective-permute-done.6 = bf16[256,512]{1,0:T(8,128)(2,1)S(1)} collective-permute-done((bf16[256,512]{1,0:T(8,128)(2,1)S(1)}, bf16[256,512]{1,0:T(8,128)(2,1)S(1)}, u32[]{:S(2)}, u32[]{:S(2)}) %collective-permute-start.6) | collective-permute-done | bytes 262176 | tf_op jit(solution)/shard_map/ppermute | solution.py:126
  79.1 1.9 %collective-permute-start.9 = (bf16[4,512,512]{2,1,0:T(8,128)(2,1)S(1)}, bf16[4,512,512]{2,1,0:T(8,128)(2,1)}, u32[]{:S(2)}, u32[]{:S(2)}) collective-permute-start(bf16[4,512,512]{2,1,0:T(8,128)(2,1)S(1)} %pad_maximum_fusion.1.a_ref), channel_id=1, source_target_pairs={{0,16},{16,0},{1,17},{17,1},{2,18},{18,2},{3,19},{19,3},{4,20},{20... | collective-permute-start | bytes 6291464 | tf_op jit(solution)/shard_map/ppermute | solution.py:160
  81.0 31.7 %all_gather.14 = bf16[512,512]{1,0:T(8,128)(2,1)S(1)} all-gather(bf16[128,512]{1,0:T(8,128)(2,1)S(1)} %copy-done.2), channel_id=1, replica_groups=mesh['zl'=4,'y'=4,'core'=2,'zh'=4,'x'=4] {'zh'}, dimensions={0}, use_global_device_ids=true | all-gather | bytes 655360 | tf_op jit(solution)/shard_map/all_gather | solution.py:156
  112.7 6.0 %collective-permute-start.2 = (bf16[512,512]{1,0:T(8,128)(2,1)S(1)}, bf16[512,512]{1,0:T(8,128)(2,1)S(1)}, u32[]{:S(2)}, u32[]{:S(2)}) collective-permute-start(bf16[512,512]{1,0:T(8,128)(2,1)S(1)} %all_gather.14), channel_id=1, source_target_pairs={{0,1},{1,2},{2,3},{3,0},{4,5},{5,6},{6,7},{7,4},{8,9},{9,10},{10,1... | collective-permute-start | bytes 1572872 | tf_op jit(solution)/shard_map/ppermute | solution.py:126
  118.7 1.9 %collective-permute-start = (bf16[512,512]{1,0:T(8,128)(2,1)S(1)}, bf16[512,512]{1,0:T(8,128)(2,1)S(1)}, u32[]{:S(2)}, u32[]{:S(2)}) collective-permute-start(bf16[512,512]{1,0:T(8,128)(2,1)S(1)} %all_gather.14), channel_id=1, source_target_pairs={{0,3},{1,0},{2,1},{3,2},{4,7},{5,4},{6,5},{7,6},{8,11},{9,8},{10,9... | collective-permute-start | bytes 1572872 | tf_op jit(solution)/shard_map/ppermute | solution.py:126
  120.6 9.3 %collective-permute-done.2 = bf16[512,512]{1,0:T(8,128)(2,1)S(1)} collective-permute-done((bf16[512,512]{1,0:T(8,128)(2,1)S(1)}, bf16[512,512]{1,0:T(8,128)(2,1)S(1)}, u32[]{:S(2)}, u32[]{:S(2)}) %collective-permute-start.2) | collective-permute-done | bytes 524320 | tf_op jit(solution)/shard_map/ppermute | solution.py:126
  130.0 5.6 %collective-permute-start.3 = (bf16[256,512]{1,0:T(8,128)(2,1)S(1)}, bf16[256,512]{1,0:T(8,128)(2,1)}, u32[]{:S(2)}, u32[]{:S(2)}) collective-permute-start(bf16[256,512]{1,0:T(8,128)(2,1)S(1)} %slice.17), channel_id=1, source_target_pairs={{0,1},{1,2},{2,3},{3,0},{4,5},{5,6},{6,7},{7,4},{8,9},{9,10},{10,1... | collective-permute-start | bytes 786440 | tf_op jit(solution)/shard_map/ppermute | solution.py:126
  137.2 1.9 %collective-permute-start.1 = (bf16[256,512]{1,0:T(8,128)(2,1)}, bf16[256,512]{1,0:T(8,128)(2,1)}, u32[]{:S(2)}, u32[]{:S(2)}) collective-permute-start(bf16[256,512]{1,0:T(8,128)(2,1)} %slice.16), channel_id=1, source_target_pairs={{0,3},{1,0},{2,1},{3,2},{4,7},{5,4},{6,5},{7,6},{8,11},{9,8},{10,9... | collective-permute-start | bytes 786440 | tf_op jit(solution)/shard_map/ppermute | solution.py:126
  139.2 1.3 collective-permute-done.3
  140.4 7.2 %collective-permute-done.1 = bf16[256,512]{1,0:T(8,128)(2,1)} collective-permute-done((bf16[256,512]{1,0:T(8,128)(2,1)}, bf16[256,512]{1,0:T(8,128)(2,1)}, u32[]{:S(2)}, u32[]{:S(2)}) %collective-permute-start.1) | collective-permute-done | bytes 262176 | tf_op jit(solution)/shard_map/ppermute | solution.py:126
  148.7 1.3 pad_maximum_fusion.r_ref
  150.0 7.3 %hessian.1 = f32[512,1024]{1,0:T(8,128)} custom-call(s32[2]{0:T(128)S(1)} %pad_add_fusion.s_ref, bf16[4,512,512]{2,1,0:T(8,128)(2,1)S(1)} %pad_maximum_fusion.r_ref, bf16[4,512,512]{2,1,0:T(8,128)(2,1)S(1)} %pad_maximum_fusion.1.a_ref, bf16[4,512,512]{2,1,0:T(8,128)(2,1)} %collective-permute-done.9.b_ref), custom_call_target="tpu_custom_call" | custom-call | tf_op jit(solution)/shard_map/hessian/pallas_call | solution.py:107
  (18 shorter events, 4.7 us)
Async XLA Ops:
  15.4 0.9 copy-start
  18.2 15.0 %collective-permute-start.4 = (bf16[128,512]{1,0:T(8,128)(2,1)}, bf16[128,512]{1,0:T(8,128)(2,1)S(1)}, u32[]{:S(2)}, u32[]{:S(2)}) collective-permute-start(bf16[128,512]{1,0:T(8,128)(2,1)} %attend.1), channel_id=1, source_target_pairs={{0,0},{1,32},{2,64},{3,96},{4,128},{5,160},{6,192},{7,224},{8,256}... | collective-permute-start | bytes 393224 | tf_op jit(solution)/shard_map/ppermute | solution.py:144
  54.6 13.9 %collective-permute-start.7 = (bf16[512,512]{1,0:T(8,128)(2,1)S(1)}, bf16[512,512]{1,0:T(8,128)(2,1)S(1)}, u32[]{:S(2)}, u32[]{:S(2)}) collective-permute-start(bf16[512,512]{1,0:T(8,128)(2,1)S(1)} %all_gather.15), channel_id=1, source_target_pairs={{0,32},{32,64},{64,96},{96,0},{1,33},{33,65},{65,97},{97,1},{2,34}... | collective-permute-start | bytes 1572872 | tf_op jit(solution)/shard_map/ppermute | solution.py:126
  56.5 13.9 %collective-permute-start.5 = (bf16[512,512]{1,0:T(8,128)(2,1)S(1)}, bf16[512,512]{1,0:T(8,128)(2,1)S(1)}, u32[]{:S(2)}, u32[]{:S(2)}) collective-permute-start(bf16[512,512]{1,0:T(8,128)(2,1)S(1)} %all_gather.15), channel_id=1, source_target_pairs={{0,96},{32,0},{64,32},{96,64},{1,97},{33,1},{65,33},{97,65},{2,98}... | collective-permute-start | bytes 1572872 | tf_op jit(solution)/shard_map/ppermute | solution.py:126
  68.5 8.3 %collective-permute-start.8 = (bf16[256,512]{1,0:T(8,128)(2,1)S(1)}, bf16[256,512]{1,0:T(8,128)(2,1)S(1)}, u32[]{:S(2)}, u32[]{:S(2)}) collective-permute-start(bf16[256,512]{1,0:T(8,128)(2,1)S(1)} %slice.19), channel_id=1, source_target_pairs={{0,32},{32,64},{64,96},{96,0},{1,33},{33,65},{65,97},{97,1},{2,34}... | collective-permute-start | bytes 786440 | tf_op jit(solution)/shard_map/ppermute | solution.py:126
  70.5 8.3 %collective-permute-start.6 = (bf16[256,512]{1,0:T(8,128)(2,1)S(1)}, bf16[256,512]{1,0:T(8,128)(2,1)S(1)}, u32[]{:S(2)}, u32[]{:S(2)}) collective-permute-start(bf16[256,512]{1,0:T(8,128)(2,1)S(1)} %slice.18), channel_id=1, source_target_pairs={{0,96},{32,0},{64,32},{96,64},{1,97},{33,1},{65,33},{97,65},{2,98}... | collective-permute-start | bytes 786440 | tf_op jit(solution)/shard_map/ppermute | solution.py:126
  78.8 2.2 %copy-start.2 = (bf16[128,512]{1,0:T(8,128)(2,1)S(1)}, bf16[128,512]{1,0:T(8,128)(2,1)}, u32[]{:S(2)}) copy-start(bf16[128,512]{1,0:T(8,128)(2,1)} %attend.1) | copy-start | bytes 393220
  79.1 70.9 %collective-permute-start.9 = (bf16[4,512,512]{2,1,0:T(8,128)(2,1)S(1)}, bf16[4,512,512]{2,1,0:T(8,128)(2,1)}, u32[]{:S(2)}, u32[]{:S(2)}) collective-permute-start(bf16[4,512,512]{2,1,0:T(8,128)(2,1)S(1)} %pad_maximum_fusion.1.a_ref), channel_id=1, source_target_pairs={{0,16},{16,0},{1,17},{17,1},{2,18},{18,2},{3,19},{19,3},{4,20},{20... | collective-permute-start | bytes 6291464 | tf_op jit(solution)/shard_map/ppermute | solution.py:160
  112.7 17.3 %collective-permute-start.2 = (bf16[512,512]{1,0:T(8,128)(2,1)S(1)}, bf16[512,512]{1,0:T(8,128)(2,1)S(1)}, u32[]{:S(2)}, u32[]{:S(2)}) collective-permute-start(bf16[512,512]{1,0:T(8,128)(2,1)S(1)} %all_gather.14), channel_id=1, source_target_pairs={{0,1},{1,2},{2,3},{3,0},{4,5},{5,6},{6,7},{7,4},{8,9},{9,10},{10,1... | collective-permute-start | bytes 1572872 | tf_op jit(solution)/shard_map/ppermute | solution.py:126
  118.7 16.9 %collective-permute-start = (bf16[512,512]{1,0:T(8,128)(2,1)S(1)}, bf16[512,512]{1,0:T(8,128)(2,1)S(1)}, u32[]{:S(2)}, u32[]{:S(2)}) collective-permute-start(bf16[512,512]{1,0:T(8,128)(2,1)S(1)} %all_gather.14), channel_id=1, source_target_pairs={{0,3},{1,0},{2,1},{3,2},{4,7},{5,4},{6,5},{7,6},{8,11},{9,8},{10,9... | collective-permute-start | bytes 1572872 | tf_op jit(solution)/shard_map/ppermute | solution.py:126
  130.0 10.4 %collective-permute-start.3 = (bf16[256,512]{1,0:T(8,128)(2,1)S(1)}, bf16[256,512]{1,0:T(8,128)(2,1)}, u32[]{:S(2)}, u32[]{:S(2)}) collective-permute-start(bf16[256,512]{1,0:T(8,128)(2,1)S(1)} %slice.17), channel_id=1, source_target_pairs={{0,1},{1,2},{2,3},{3,0},{4,5},{5,6},{6,7},{7,4},{8,9},{9,10},{10,1... | collective-permute-start | bytes 786440 | tf_op jit(solution)/shard_map/ppermute | solution.py:126
  135.6 0.8 copy-start.1
  137.2 10.4 %collective-permute-start.1 = (bf16[256,512]{1,0:T(8,128)(2,1)}, bf16[256,512]{1,0:T(8,128)(2,1)}, u32[]{:S(2)}, u32[]{:S(2)}) collective-permute-start(bf16[256,512]{1,0:T(8,128)(2,1)} %slice.16), channel_id=1, source_target_pairs={{0,3},{1,0},{2,1},{3,2},{4,7},{5,4},{6,5},{7,6},{8,11},{9,8},{10,9... | collective-permute-start | bytes 786440 | tf_op jit(solution)/shard_map/ppermute | solution.py:126

commit v2 on v1

--- a/solution.py
+++ b/solution.py
@@ -126,13 +126,20 @@
     return lax.ppermute(value, axis, [(i, (i + by) % RING) for i in range(RING)])
 
 
-def ring(value, axis):
-    half = value.shape[0] // 2
-    after = shift(value, axis, -1)
-    before = shift(value, axis, 1)
+def neighbours(value, axis):
+    return shift(value, axis, -1), shift(value, axis, 1)
+
+
+def opposite(after, before, axis):
+    half = after.shape[0] // 2
     first = shift(after[:half], axis, -1)
     second = shift(before[half:], axis, 1)
-    return jnp.stack([value, after, jnp.concatenate([first, second]), before])
+    return jnp.concatenate([first, second])
+
+
+def spread(value, axis):
+    copies = jnp.broadcast_to(value[None], (RING,) + value.shape)
+    return lax.all_to_all(copies, axis, split_axis=0, concat_axis=0, tiled=True)
 
 
 def swap(value):
@@ -150,16 +157,20 @@
     head = lax.axis_index(HEAD)
     key_head = (head * local_heads // (HEADS // KVH)).astype(jnp.int32).reshape(1)
     packed = pack(key_head, key_rows, value_rows, positions)
-    gathered = lax.all_gather(packed, "x", axis=0)
+    gathered = spread(packed, "x")
     attended = attend(query_rows, gathered, positions)
     chunk = swap(attended)
     rows = lax.all_gather(attended, "zh", axis=0, tiled=True)
-    cols = lax.all_gather(chunk, "zl", axis=0, tiled=True)
-    own = ring(cols, "y")
-    rows = ring(rows, "x")
+    chunk, rows = lax.optimization_barrier((chunk, rows))
+    cols = spread(chunk, "zl").reshape(RING * tok, -1)
+    after, before = neighbours(rows, "x")
+    cols, after, before = lax.optimization_barrier((cols, after, before))
+    across = opposite(after, before, "x")
+    own = spread(cols, "y")
+    own, across = lax.optimization_barrier((own, across))
+    rows = jnp.stack([rows, after, across, before])
     other = lax.ppermute(own, "core", [(0, 1), (1, 0)])
-    turn = (lax.axis_index("x") - lax.axis_index("y")) & (RING - 1)
-    scalars = jnp.stack([turn, lax.axis_index("core")]).astype(jnp.int32)
+    scalars = jnp.stack([lax.axis_index("x"), lax.axis_index("core")]).astype(jnp.int32)
     return attended, hessian_of(scalars, rows, own, other)
 
 

time: 158 us -> 133 us (0.84)
  the two profiles are of different devices: /device:TPU:46 before, /device:TPU:1 now
where the time goes in v2:
time: 133 us; the launch traced here: 132 us
  starting transfers between devices  51.6 us (39%)
  blocking collectives  31.4 us (24%)
  waiting for transfers between devices  29.4 us (22%)
  Pallas kernels  10.5 us (8%)
  local copies, waits for them, and re-layouts  6.61 us (5%)
  other arithmetic  1.57 us (1%)
    all_gather x1, blocking collectives, on_device(): rows = lax.all_gather(attended, 'zh', axis=0, tiled=True)  31.4 us
    all_to_all x3, starting transfers between devices, spread(): return lax.all_to_all(copies, axis, split_axis=0, concat_axis=0, tiled=True)  28.9 us
    all_to_all x3, waiting for transfers between devices, spread(): return lax.all_to_all(copies, axis, split_axis=0, concat_axis=0, tiled=True)  16.9 us
    ppermute x4, starting transfers between devices, shift(): lax.ppermute(value, axis, [(i, (i + by) % RING) for i in range(RING)])  14.8 us
    ppermute x4, waiting for transfers between devices, shift(): lax.ppermute(value, axis, [(i, (i + by) % RING) for i in range(RING)])  10.2 us
    pallas_call x1, Pallas kernels, hessian_of(): pl.pallas_call(hessian_kernel, out_shape=jax.ShapeDtypeStruct((width, 2 *...  7.26 us
    ppermute x1, starting transfers between devices, on_device(): other = lax.ppermute(own, 'core', [(0, 1), (1, 0)])  6.32 us
    broadcast_in_dim x3, local copies, waits for them, and re-layouts, spread(): copies = jnp.broadcast_to(value[None], (RING,) + value.shape)  3.95 us
  transfers between devices with their start and end apart: 9, of which 7 were waited for; matrix products, arithmetic and copies ran while one was open for 3% of the time, Pallas kernels for 0%

profile of v2, /device:TPU:1, one launch (start us, length us, event | category | flops | bytes accessed | tf_op | source)
XLA Modules:
  0.0 131.9 jit_solution(6298651132897980277)
XLA Ops:
  0.7 1.4 %pack.1 = bf16[272,128]{1,0:T(8,128)(2,1)} custom-call(s32[1]{0:T(128)} %bitcast.g_ref, bf16[128,1024]{1,0:T(8,128)(2,1)} %k_ref.1, bf16[128,1024]{1,0:T(8,128)(2,1)} %v_ref.1, s32[1,128]{1,0:T(1,128)} %bitcast.15), custom_call_target="tpu_custom_call" | custom-call | tf_op jit(solution)/shard_map/pack/pallas_call | solution.py:32
  2.1 1.6 %broadcast_in_dim.6 = bf16[4,272,128]{2,1,0:T(8,128)(2,1)} broadcast(bf16[272,128]{1,0:T(8,128)(2,1)} %pack.1), dimensions={1,2} | broadcast | bytes 348160 | tf_op jit(solution)/shard_map/broadcast_in_dim | solution.py:141
  3.7 4.8 %all-to-all-start = ((bf16[4,272,128]{2,1,0:T(8,128)(2,1)}), bf16[4,272,128]{2,1,0:T(8,128)(2,1)S(1)}, u32[]{:S(2)}, u32[]{:S(2)}) async-start(bf16[4,272,128]{2,1,0:T(8,128)(2,1)} %broadcast_in_dim.6), calls=%async_computation | async-start | bytes 557056 | tf_op jit(solution)/shard_map/all_to_all | solution.py:142
  9.3 4.9 %all-to-all-done.kv_ref = bf16[4,272,128]{2,1,0:T(8,128)(2,1)S(1)} async-done(((bf16[4,272,128]{2,1,0:T(8,128)(2,1)}), bf16[4,272,128]{2,1,0:T(8,128)(2,1)S(1)}, u32[]{:S(2)}, u32[]{:S(2)}) %all-to-all-start) | async-done | bytes 278560 | tf_op jit(solution)/shard_map/all_to_all | solution.py:142
  15.1 1.8 %attend.1 = bf16[128,512]{1,0:T(8,128)(2,1)} custom-call(bf16[128,512]{1,0:T(8,128)(2,1)S(1)} %copy-done, bf16[4,272,128]{2,1,0:T(8,128)(2,1)S(1)} %all-to-all-done.kv_ref, s32[128,1]{1,0:T(8,128)S(1)} %copy.6.p_ref), custom_call_target="tpu_custom_call" | custom-call | tf_op jit(solution)/shard_map/attend/pallas_call | solution.py:76
  16.9 1.6 %collective-permute-start = (bf16[128,512]{1,0:T(8,128)(2,1)}, bf16[128,512]{1,0:T(8,128)(2,1)S(1)}, u32[]{:S(2)}, u32[]{:S(2)}) collective-permute-start(bf16[128,512]{1,0:T(8,128)(2,1)} %attend.1), channel_id=1, source_target_pairs={{0,0},{1,32},{2,64},{3,96},{4,128},{5,160},{6,192},{7,224},{8,256}... | collective-permute-start | bytes 393224 | tf_op jit(solution)/shard_map/ppermute | solution.py:151
  18.5 31.4 %all_gather.3 = bf16[512,512]{1,0:T(8,128)(2,1)S(1)} all-gather(bf16[128,512]{1,0:T(8,128)(2,1)} %attend.1), channel_id=1, replica_groups=mesh['zl'=4,'y'=4,'core'=2,'zh'=4,'x'=4] {'zh'}, dimensions={0}, use_global_device_ids=true | all-gather | bytes 655360 | tf_op jit(solution)/shard_map/all_gather | solution.py:163
  50.7 15.7 %all-to-all-start.1 = ((bf16[4,128,512]{2,1,0:T(8,128)(2,1)}), bf16[4,128,512]{2,1,0:T(8,128)(2,1)S(1)}, u32[]{:S(2)}, u32[]{:S(2)}) async-start(bf16[4,128,512]{2,1,0:T(8,128)(2,1)} %broadcast_in_dim.7), calls=%async_computation.1 | async-start | bytes 1048576 | tf_op jit(solution)/shard_map/all_to_all | solution.py:142
  66.4 4.7 %collective-permute-start.2 = (bf16[512,512]{1,0:T(8,128)(2,1)S(1)}, bf16[512,512]{1,0:T(8,128)(2,1)S(1)}, u32[]{:S(2)}, u32[]{:S(2)}) collective-permute-start(bf16[512,512]{1,0:T(8,128)(2,1)S(1)} %all_gather.3), channel_id=1, source_target_pairs={{0,1},{1,2},{2,3},{3,0},{4,5},{5,6},{6,7},{7,4},{8,9},{9,10},{10,1... | collective-permute-start | bytes 1572872 | tf_op jit(solution)/shard_map/ppermute | solution.py:126
  71.1 3.6 %collective-permute-start.1 = (bf16[512,512]{1,0:T(8,128)(2,1)S(1)}, bf16[512,512]{1,0:T(8,128)(2,1)S(1)}, u32[]{:S(2)}, u32[]{:S(2)}) collective-permute-start(bf16[512,512]{1,0:T(8,128)(2,1)S(1)} %all_gather.3), channel_id=1, source_target_pairs={{0,3},{1,0},{2,1},{3,2},{4,7},{5,4},{6,5},{7,6},{8,11},{9,8},{10,9... | collective-permute-start | bytes 1572872 | tf_op jit(solution)/shard_map/ppermute | solution.py:126
  74.7 5.0 %collective-permute-done.2 = bf16[512,512]{1,0:T(8,128)(2,1)S(1)} collective-permute-done((bf16[512,512]{1,0:T(8,128)(2,1)S(1)}, bf16[512,512]{1,0:T(8,128)(2,1)S(1)}, u32[]{:S(2)}, u32[]{:S(2)}) %collective-permute-start.2) | collective-permute-done | bytes 524320 | tf_op jit(solution)/shard_map/ppermute | solution.py:126
  79.8 1.9 %collective-permute-done.1 = bf16[512,512]{1,0:T(8,128)(2,1)S(1)} collective-permute-done((bf16[512,512]{1,0:T(8,128)(2,1)S(1)}, bf16[512,512]{1,0:T(8,128)(2,1)S(1)}, u32[]{:S(2)}, u32[]{:S(2)}) %collective-permute-start.1) | collective-permute-done | bytes 524320 | tf_op jit(solution)/shard_map/ppermute | solution.py:126
  81.6 1.5 %broadcast_in_dim.8 = bf16[4,512,512]{2,1,0:T(8,128)(2,1)} broadcast(bf16[512,512]{1,0:T(8,128)(2,1)S(1)} %bitcast.10), dimensions={1,2} | broadcast | bytes 2621440 | tf_op jit(solution)/shard_map/broadcast_in_dim | solution.py:141
  83.1 8.4 %all-to-all-start.2 = ((bf16[4,512,512]{2,1,0:T(8,128)(2,1)}), bf16[4,512,512]{2,1,0:T(8,128)(2,1)S(1)}, u32[]{:S(2)}, u32[]{:S(2)}) async-start(bf16[4,512,512]{2,1,0:T(8,128)(2,1)} %broadcast_in_dim.8), calls=%async_computation.2 | async-start | bytes 4194304 | tf_op jit(solution)/shard_map/all_to_all | solution.py:142
  91.5 1.0 slice.6
  92.5 2.2 %collective-permute-start.4 = (bf16[256,512]{1,0:T(8,128)(2,1)S(1)}, bf16[256,512]{1,0:T(8,128)(2,1)S(1)}, u32[]{:S(2)}, u32[]{:S(2)}) collective-permute-start(bf16[256,512]{1,0:T(8,128)(2,1)S(1)} %slice.7), channel_id=1, source_target_pairs={{0,1},{1,2},{2,3},{3,0},{4,5},{5,6},{6,7},{7,4},{8,9},{9,10},{10,1... | collective-permute-start | bytes 786440 | tf_op jit(solution)/shard_map/ppermute | solution.py:126
  94.7 4.3 %collective-permute-start.3 = (bf16[256,512]{1,0:T(8,128)(2,1)S(1)}, bf16[256,512]{1,0:T(8,128)(2,1)S(1)}, u32[]{:S(2)}, u32[]{:S(2)}) collective-permute-start(bf16[256,512]{1,0:T(8,128)(2,1)S(1)} %slice.6), channel_id=1, source_target_pairs={{0,3},{1,0},{2,1},{3,2},{4,7},{5,4},{6,5},{7,6},{8,11},{9,8},{10,9... | collective-permute-start | bytes 786440 | tf_op jit(solution)/shard_map/ppermute | solution.py:126
  99.0 2.1 %collective-permute-done.4 = bf16[256,512]{1,0:T(8,128)(2,1)S(1)} collective-permute-done((bf16[256,512]{1,0:T(8,128)(2,1)S(1)}, bf16[256,512]{1,0:T(8,128)(2,1)S(1)}, u32[]{:S(2)}, u32[]{:S(2)}) %collective-permute-start.4) | collective-permute-done | bytes 262176 | tf_op jit(solution)/shard_map/ppermute | solution.py:126
  101.2 1.2 collective-permute-done.3
  102.4 12.0 %all-to-all-done.2.a_ref = bf16[4,512,512]{2,1,0:T(8,128)(2,1)S(1)} async-done(((bf16[4,512,512]{2,1,0:T(8,128)(2,1)}), bf16[4,512,512]{2,1,0:T(8,128)(2,1)S(1)}, u32[]{:S(2)}, u32[]{:S(2)}) %all-to-all-start.2) | async-done | bytes 2097184 | tf_op jit(solution)/shard_map/all_to_all | solution.py:142
  114.4 6.3 %collective-permute-start.5 = (bf16[4,512,512]{2,1,0:T(8,128)(2,1)S(1)}, bf16[4,512,512]{2,1,0:T(8,128)(2,1)}, u32[]{:S(2)}, u32[]{:S(2)}) collective-permute-start(bf16[4,512,512]{2,1,0:T(8,128)(2,1)S(1)} %all-to-all-done.2.a_ref), channel_id=1, source_target_pairs={{0,16},{16,0},{1,17},{17,1},{2,18},{18,2},{3,19},{19,3},{4,20},{20... | collective-permute-start | bytes 6291464 | tf_op jit(solution)/shard_map/ppermute | solution.py:172
  120.8 1.5 %pad_maximum_fusion.r_ref = bf16[4,512,512]{2,1,0:T(8,128)(2,1)S(1)} fusion(bf16[1,512,512]{2,1,0:T(8,128)(2,1)} %bitcast.13, bf16[1,512,512]{2,1,0:T(8,128)(2,1)S(1)} %bitcast.12, bf16[1,512,512]{2,1,0:T(8,128)(2,1)} %bitcast.14, bf16[1,512,512]{2,1,0:T(8,128)(2,1)S(1)} %bitcast.11), kind=kLoop, calls=%fused_computation | loop fusion | flops 3145728 | bytes 4194304 | tf_op jit(solution)/shard_map/stack | solution.py:171
  122.3 2.4 %collective-permute-done.5.b_ref = bf16[4,512,512]{2,1,0:T(8,128)(2,1)} collective-permute-done((bf16[4,512,512]{2,1,0:T(8,128)(2,1)S(1)}, bf16[4,512,512]{2,1,0:T(8,128)(2,1)}, u32[]{:S(2)}, u32[]{:S(2)}) %collective-permute-start.5) | collective-permute-done | bytes 2097184 | tf_op jit(solution)/shard_map/ppermute | solution.py:172
  124.6 7.3 %hessian.1 = f32[512,1024]{1,0:T(8,128)} custom-call(s32[2]{0:T(128)S(1)} %pad_add_fusion.s_ref, bf16[4,512,512]{2,1,0:T(8,128)(2,1)S(1)} %pad_maximum_fusion.r_ref, bf16[4,512,512]{2,1,0:T(8,128)(2,1)S(1)} %all-to-all-done.2.a_ref, bf16[4,512,512]{2,1,0:T(8,128)(2,1)} %collective-permute-done.5.b_ref), custom_call_target="tpu_custom_call" | custom-call | tf_op jit(solution)/shard_map/hessian/pallas_call | solution.py:107
  (13 shorter events, 2.6 us)
Async XLA Ops:
  3.7 10.5 %all-to-all-start = ((bf16[4,272,128]{2,1,0:T(8,128)(2,1)}), bf16[4,272,128]{2,1,0:T(8,128)(2,1)S(1)}, u32[]{:S(2)}, u32[]{:S(2)}) async-start(bf16[4,272,128]{2,1,0:T(8,128)(2,1)} %broadcast_in_dim.6), calls=%async_computation | async-start | bytes 557056 | tf_op jit(solution)/shard_map/all_to_all | solution.py:142
  14.2 0.9 copy-start
  16.9 33.0 %collective-permute-start = (bf16[128,512]{1,0:T(8,128)(2,1)}, bf16[128,512]{1,0:T(8,128)(2,1)S(1)}, u32[]{:S(2)}, u32[]{:S(2)}) collective-permute-start(bf16[128,512]{1,0:T(8,128)(2,1)} %attend.1), channel_id=1, source_target_pairs={{0,0},{1,32},{2,64},{3,96},{4,128},{5,160},{6,192},{7,224},{8,256}... | collective-permute-start | bytes 393224 | tf_op jit(solution)/shard_map/ppermute | solution.py:151
  50.7 30.9 %all-to-all-start.1 = ((bf16[4,128,512]{2,1,0:T(8,128)(2,1)}), bf16[4,128,512]{2,1,0:T(8,128)(2,1)S(1)}, u32[]{:S(2)}, u32[]{:S(2)}) async-start(bf16[4,128,512]{2,1,0:T(8,128)(2,1)} %broadcast_in_dim.7), calls=%async_computation.1 | async-start | bytes 1048576 | tf_op jit(solution)/shard_map/all_to_all | solution.py:142
  66.4 13.4 %collective-permute-start.2 = (bf16[512,512]{1,0:T(8,128)(2,1)S(1)}, bf16[512,512]{1,0:T(8,128)(2,1)S(1)}, u32[]{:S(2)}, u32[]{:S(2)}) collective-permute-start(bf16[512,512]{1,0:T(8,128)(2,1)S(1)} %all_gather.3), channel_id=1, source_target_pairs={{0,1},{1,2},{2,3},{3,0},{4,5},{5,6},{6,7},{7,4},{8,9},{9,10},{10,1... | collective-permute-start | bytes 1572872 | tf_op jit(solution)/shard_map/ppermute | solution.py:126
  71.1 10.5 %collective-permute-start.1 = (bf16[512,512]{1,0:T(8,128)(2,1)S(1)}, bf16[512,512]{1,0:T(8,128)(2,1)S(1)}, u32[]{:S(2)}, u32[]{:S(2)}) collective-permute-start(bf16[512,512]{1,0:T(8,128)(2,1)S(1)} %all_gather.3), channel_id=1, source_target_pairs={{0,3},{1,0},{2,1},{3,2},{4,7},{5,4},{6,5},{7,6},{8,11},{9,8},{10,9... | collective-permute-start | bytes 1572872 | tf_op jit(solution)/shard_map/ppermute | solution.py:126
  79.8 12.7 %copy-start.1 = (bf16[512,512]{1,0:T(8,128)(2,1)}, bf16[512,512]{1,0:T(8,128)(2,1)S(1)}, u32[]{:S(2)}) copy-start(bf16[512,512]{1,0:T(8,128)(2,1)S(1)} %collective-permute-done.2) | copy-start | bytes 1572868
  81.6 1.5 %copy-start.2 = (bf16[512,512]{1,0:T(8,128)(2,1)}, bf16[512,512]{1,0:T(8,128)(2,1)S(1)}, u32[]{:S(2)}) copy-start(bf16[512,512]{1,0:T(8,128)(2,1)S(1)} %collective-permute-done.1) | copy-start | bytes 1572868
  83.1 31.3 %all-to-all-start.2 = ((bf16[4,512,512]{2,1,0:T(8,128)(2,1)}), bf16[4,512,512]{2,1,0:T(8,128)(2,1)S(1)}, u32[]{:S(2)}, u32[]{:S(2)}) async-start(bf16[4,512,512]{2,1,0:T(8,128)(2,1)} %broadcast_in_dim.8), calls=%async_computation.2 | async-start | bytes 4194304 | tf_op jit(solution)/shard_map/all_to_all | solution.py:142
  92.5 8.6 %collective-permute-start.4 = (bf16[256,512]{1,0:T(8,128)(2,1)S(1)}, bf16[256,512]{1,0:T(8,128)(2,1)S(1)}, u32[]{:S(2)}, u32[]{:S(2)}) collective-permute-start(bf16[256,512]{1,0:T(8,128)(2,1)S(1)} %slice.7), channel_id=1, source_target_pairs={{0,1},{1,2},{2,3},{3,0},{4,5},{5,6},{6,7},{7,4},{8,9},{9,10},{10,1... | collective-permute-start | bytes 786440 | tf_op jit(solution)/shard_map/ppermute | solution.py:126
  94.7 7.6 %collective-permute-start.3 = (bf16[256,512]{1,0:T(8,128)(2,1)S(1)}, bf16[256,512]{1,0:T(8,128)(2,1)S(1)}, u32[]{:S(2)}, u32[]{:S(2)}) collective-permute-start(bf16[256,512]{1,0:T(8,128)(2,1)S(1)} %slice.6), channel_id=1, source_target_pairs={{0,3},{1,0},{2,1},{3,2},{4,7},{5,4},{6,5},{7,6},{8,11},{9,8},{10,9... | collective-permute-start | bytes 786440 | tf_op jit(solution)/shard_map/ppermute | solution.py:126
  114.4 10.2 %collective-permute-start.5 = (bf16[4,512,512]{2,1,0:T(8,128)(2,1)S(1)}, bf16[4,512,512]{2,1,0:T(8,128)(2,1)}, u32[]{:S(2)}, u32[]{:S(2)}) collective-permute-start(bf16[4,512,512]{2,1,0:T(8,128)(2,1)S(1)} %all-to-all-done.2.a_ref), channel_id=1, source_target_pairs={{0,16},{16,0},{1,17},{17,1},{2,18},{18,2},{3,19},{19,3},{4,20},{20... | collective-permute-start | bytes 6291464 | tf_op jit(solution)/shard_map/ppermute | solution.py:172

commit v3 on v1

v3 whole, which is shorter than its diff:
```python
import functools

import jax
import jax.numpy as jnp
from jax import lax
from jax.experimental import pallas as pl
from jax.experimental.pallas import tpu as pltpu
from jax.sharding import Mesh
from jax.sharding import PartitionSpec as P

HEADS = 128
KVH = 8
HD = 128
RING = 4
AXES = ("zl", "y", "core", "zh", "x")
HEAD = ("zl", "y", "core")
SEQ = ("zh", "x")
VMEM = 24 * 1024 * 1024


def pack_kernel(g_ref, k_ref, v_ref, p_ref, o_ref):
    tok = k_ref.shape[0]
    p = p_ref[...]
    high = p >> 7
    row = lax.broadcasted_iota(jnp.int32, (16, tok), 0)
    both = jnp.where(row == 0, high, p - (high << 7))
    both = both.astype(jnp.float32).astype(jnp.bfloat16)
    for copy in range(o_ref.shape[0]):
        o_ref[copy, :tok] = k_ref[...]
        o_ref[copy, tok : 2 * tok] = v_ref[...]
        o_ref[copy, 2 * tok :] = both


def pack(key_head, key_rows, value_rows, positions):
    tok = key_rows.shape[0]
    return pl.pallas_call(
        pack_kernel,
        out_shape=jax.ShapeDtypeStruct((RING, 2 * tok + 16, HD), jnp.bfloat16),
        grid_spec=pltpu.PrefetchScalarGridSpec(
            num_scalar_prefetch=1,
            grid=(1,),
            in_specs=[
                pl.BlockSpec((tok, HD), lambda i, g: (0, g[0])),
                pl.BlockSpec((tok, HD), lambda i, g: (0, g[0])),
                pl.BlockSpec((1, tok), lambda i, g: (0, 0)),
            ],
            out_specs=pl.BlockSpec((RING, 2 * tok + 16, HD), lambda i, g: (0, 0, 0)),
        ),
        name="pack",
    )(key_head, key_rows, value_rows, positions.reshape(1, tok))


def attend_kernel(q_ref, kv_ref, p_ref, o_ref):
    heads, tok, _ = q_ref.shape
    spans = kv_ref.shape[0]
    keys = jnp.concatenate([kv_ref[s, :tok, :] for s in range(spans)], axis=0)
    values = jnp.concatenate([kv_ref[s, tok : 2 * tok, :] for s in range(spans)], axis=0)
    places = []
    for s in range(spans):
        both = kv_ref[s, 2 * tok :, :].astype(jnp.float32)
        places.append(both[0:1] * 128.0 + both[1:2])
    place = jnp.concatenate(places, axis=1)
    own = p_ref[...].astype(jnp.float32)
    visible = place <= own
    for h in range(heads):
        q = q_ref[h]
        scores = lax.dot_general(
            q, keys, (((1,), (1,)), ((), ())), preferred_element_type=jnp.float32
        ) * (HD ** (-0.5))
        masked = jnp.where(visible, scores, -jnp.inf)
        top = jnp.max(masked, axis=1, keepdims=True)
        weights = jnp.exp(masked - top)
        total = jnp.sum(weights, axis=1, keepdims=True)
        mixed = jnp.dot(weights.astype(jnp.bfloat16), values, preferred_element_type=jnp.float32)
        o_ref[:, h * HD : (h + 1) * HD] = (mixed / total).astype(jnp.bfloat16)


def attend(queries, gathered, positions):
    heads, tok, _ = queries.shape
    return pl.pallas_call(
        attend_kernel,
        out_shape=jax.ShapeDtypeStruct((tok, heads * HD), jnp.bfloat16),
        compiler_params=pltpu.CompilerParams(vmem_limit_bytes=VMEM),
        name="attend",
    )(queries, gathered, positions.reshape(tok, 1))


CONTRACT = (((0,), (0,)), ((), ()))


def product_kernel(final, s_ref, one_ref, two_ref, *rest):
    o_ref = rest[-1]
    core = s_ref[0]

    def product(left, right):
        depth = left.shape[0] * left.shape[1]
        o_ref[...] = lax.dot_general(
            left[...].reshape(depth, left.shape[2]),
            right[...].reshape(depth, right.shape[2]),
            CONTRACT,
            preferred_element_type=jnp.float32,
        )

    @pl.when(core == 0)
    def _():
        product(one_ref, rest[0] if final else two_ref)

    @pl.when(core == 1)
    def _():
        product(two_ref, rest[1] if final else one_ref)


def hessian_half(core, operands, filled=None):
    width = operands[0].shape[2]
    final = filled is not None
    whole = [pl.BlockSpec(v.shape, lambda i, s: (0, 0, 0)) for v in operands]
    args = [core, *operands]
    aliases = {}
    if final:
        aliases = {len(args): 0}
        whole.append(pl.BlockSpec(memory_space=pl.ANY))
        args.append(filled)
    return pl.pallas_call(
        functools.partial(product_kernel, final),
        out_shape=jax.ShapeDtypeStruct((width, 2 * width), jnp.float32),
        grid_spec=pltpu.PrefetchScalarGridSpec(
            num_scalar_prefetch=1,
            grid=(1,),
            in_specs=whole,
            out_specs=pl.BlockSpec(
                (width, width), lambda i, s: (0, 1 - s[0] if final else s[0])
            ),
        ),
        input_output_aliases=aliases,
        compiler_params=pltpu.CompilerParams(vmem_limit_bytes=VMEM),
        name="hessian_half",
    )(*args)


PLANE = ("y", "core", "x")


def mixed_groups(along_x):
    place = lambda y, core, x: (y * 2 + core) * RING + x
    groups = [[place(y, along_x, x) for x in range(RING)] for y in range(RING)]
    return groups + [[place(y, 1 - along_x, x) for y in range(RING)] for x in range(RING)]


def exchange_plane(value, along_x):
    return lax.all_to_all(value, PLANE, 0, 0, axis_index_groups=mixed_groups(along_x), tiled=True)


def swap_cores(value):
    return lax.ppermute(value, "core", [(0, 1), (1, 0)])


def copies(value):
    return jnp.broadcast_to(value[None], (RING,) + value.shape)


def exchange(value, axis):
    return lax.all_to_all(value, axis, split_axis=0, concat_axis=0, tiled=True)


def swap(value):
    pairs = []
    for chip in range(16):
        for core in range(2):
            for span in range(16):
                pairs.append(((chip * 2 + core) * 16 + span, (span * 2 + core) * 16 + chip))
    return lax.ppermute(value, HEAD + SEQ, pairs)


def on_device(query_rows, key_rows, value_rows, positions):
    tok = query_rows.shape[0]
    local_heads = query_rows.shape[1] // HD
    head = lax.axis_index(HEAD)
    key_head = (head * local_heads // (HEADS // KVH)).astype(jnp.int32).reshape(1)
    packed = pack(key_head, key_rows, value_rows, positions)
    gathered = exchange(packed, "x")
    queries = jnp.transpose(query_rows.reshape(tok, local_heads, HD), (1, 0, 2))
    attended = attend(queries, gathered, positions)
    chunk = swap(attended)
    chunk, mine = lax.optimization_barrier((chunk, attended))
    cols = exchange(copies(chunk), "zl").reshape(RING * tok, -1)
    rows = lax.all_gather(mine, "zh", axis=0, tiled=True)
    cols, rows = lax.optimization_barrier((cols, rows))
    core = lax.axis_index("core")
    one = exchange_plane(copies(jnp.where(core == 0, rows, cols)), 0)
    later = copies(jnp.where(core == 0, cols, rows))
    one, later = lax.optimization_barrier((one, later))
    one_across = swap_cores(one)
    two = exchange_plane(later, 1)
    two, one_across = lax.optimization_barrier((two, one_across))
    two_across = swap_cores(two)
    core = core.astype(jnp.int32).reshape(1)
    hessian = hessian_half(core, (one, two))
    hessian = hessian_half(core, (one, two, one_across, two_across), hessian)
    return attended, hessian


def solution(mesh):
    fine = Mesh(mesh.devices.reshape(4, 4, 2, 4, 4), AXES)
    placed = (P(SEQ, HEAD), P(SEQ, None), P(SEQ, None), P(SEQ))
    return jax.shard_map(
        on_device,
        mesh=fine,
        in_specs=placed,
        out_specs=(P(SEQ, HEAD), P(HEAD, SEQ)),
        check_vma=False,
    )
```

time: 158 us -> 135 us (0.85)
  the two profiles are of different devices: /device:TPU:46 before, /device:TPU:33 now
where the time goes in v3:
time: 135 us; the launch traced here: 134 us
  blocking collectives  78.7 us (58%)
  starting transfers between devices  35.9 us (27%)
  Pallas kernels  7.87 us (6%)
  waiting for transfers between devices  7.79 us (6%)
  local copies, waits for them, and re-layouts  3.07 us (2%)
    all_to_all x2, blocking collectives, exchange_plane(): lax.all_to_all(value, PLANE, 0, 0, axis_index_groups=mixed_groups(along_x...  43.8 us
    all_gather x1, blocking collectives, on_device(): rows = lax.all_gather(mine, 'zh', axis=0, tiled=True)  34.8 us
    all_to_all x2, starting transfers between devices, exchange(): return lax.all_to_all(value, axis, split_axis=0, concat_axis=0, tiled=True)  16.9 us
    ppermute x2, starting transfers between devices, swap_cores(): return lax.ppermute(value, 'core', [(0, 1), (1, 0)])  11.6 us
    ppermute x1, starting transfers between devices, swap(): return lax.ppermute(value, HEAD + SEQ, pairs)  7.45 us
    pallas_call x2, Pallas kernels, hessian_half(): pl.pallas_call(functools.partial(product_kernel, final), out_shape=jax.Sh...  4.5 us
    all_to_all x2, waiting for transfers between devices, exchange(): return lax.all_to_all(value, axis, split_axis=0, concat_axis=0, tiled=True)  3.73 us
  transfers between devices with their start and end apart: 5, of which 3 were waited for; matrix products, arithmetic and copies ran while one was open for 1% of the time, Pallas kernels for 2%

profile of v3, /device:TPU:33, one launch (start us, length us, event | category | flops | bytes accessed | tf_op | source)
XLA Modules:
  0.0 134.1 jit_solution(7693593877345698005)
XLA Ops:
  0.7 1.5 %pack.1 = bf16[4,272,128]{2,1,0:T(8,128)(2,1)} custom-call(s32[1]{0:T(128)} %bitcast.2.g_ref, bf16[128,1024]{1,0:T(8,128)(2,1)} %k_ref.1, bf16[128,1024]{1,0:T(8,128)(2,1)} %v_ref.1, s32[1,128]{1,0:T(1,128)} %bitcast.10), custom_call_target="tpu_custom_call" | custom-call | tf_op jit(solution)/shard_map/pack/pallas_call | solution.py:36
  2.2 4.0 %all-to-all-start = ((bf16[4,272,128]{2,1,0:T(8,128)(2,1)}), bf16[4,272,128]{2,1,0:T(8,128)(2,1)S(1)}, u32[]{:S(2)}, u32[]{:S(2)}) async-start(bf16[4,272,128]{2,1,0:T(8,128)(2,1)} %pack.1), calls=%async_computation | async-start | bytes 557056 | tf_op jit(solution)/shard_map/all_to_all | solution.py:162
  6.2 0.8 copy.10.p_ref
  6.9 1.0 copy.8
  8.0 0.1 copy.9
  8.1 3.7 %all-to-all-done.kv_ref = bf16[4,272,128]{2,1,0:T(8,128)(2,1)S(1)} async-done(((bf16[4,272,128]{2,1,0:T(8,128)(2,1)}), bf16[4,272,128]{2,1,0:T(8,128)(2,1)S(1)}, u32[]{:S(2)}, u32[]{:S(2)}) %all-to-all-start) | async-done | bytes 278560 | tf_op jit(solution)/shard_map/all_to_all | solution.py:162
  11.8 1.9 %attend.1 = bf16[128,512]{1,0:T(8,128)(2,1)} custom-call(bf16[4,128,128]{2,1,0:T(8,128)(2,1)S(1)} %bitcast.7, bf16[4,272,128]{2,1,0:T(8,128)(2,1)S(1)} %all-to-all-done.kv_ref, s32[128,1]{1,0:T(8,128)S(1)} %copy.10.p_ref), custom_call_target="tpu_custom_call" | custom-call | tf_op jit(solution)/shard_map/attend/pallas_call | solution.py:80
  13.7 7.5 %collective-permute-start = (bf16[128,512]{1,0:T(8,128)(2,1)}, bf16[128,512]{1,0:T(8,128)(2,1)S(1)}, u32[]{:S(2)}, u32[]{:S(2)}) collective-permute-start(bf16[128,512]{1,0:T(8,128)(2,1)} %attend.1), channel_id=1, source_target_pairs={{0,0},{1,32},{2,64},{3,96},{4,128},{5,160},{6,192},{7,224},{8,256}... | collective-permute-start | bytes 393224 | tf_op jit(solution)/shard_map/ppermute | solution.py:171
  21.2 2.6 %collective-permute-done = bf16[128,512]{1,0:T(8,128)(2,1)S(1)} collective-permute-done((bf16[128,512]{1,0:T(8,128)(2,1)}, bf16[128,512]{1,0:T(8,128)(2,1)S(1)}, u32[]{:S(2)}, u32[]{:S(2)}) %collective-permute-start) | collective-permute-done | bytes 131104 | tf_op jit(solution)/shard_map/ppermute | solution.py:171
  23.7 0.8 broadcast_in_dim.6
  24.5 12.9 %all-to-all-start.1 = ((bf16[4,128,512]{2,1,0:T(8,128)(2,1)}), bf16[4,128,512]{2,1,0:T(8,128)(2,1)S(1)}, u32[]{:S(2)}, u32[]{:S(2)}) async-start(bf16[4,128,512]{2,1,0:T(8,128)(2,1)} %broadcast_in_dim.6), calls=%async_computation.1 | async-start | bytes 1048576 | tf_op jit(solution)/shard_map/all_to_all | solution.py:162
  37.4 34.8 %all_gather.3 = bf16[512,512]{1,0:T(8,128)(2,1)S(1)} all-gather(bf16[128,512]{1,0:T(8,128)(2,1)} %attend.1), channel_id=1, replica_groups=mesh['zl'=4,'y'=4,'core'=2,'zh'=4,'x'=4] {'zh'}, dimensions={0}, use_global_device_ids=true | all-gather | bytes 655360 | tf_op jit(solution)/shard_map/all_gather | solution.py:186
  72.3 0.0 all-to-all-done.1
  72.3 0.1 broadcast_select_fusion
  72.3 0.2 broadcast_in_dim.7
  72.5 25.9 %all_to_all.20.one_ref = bf16[4,512,512]{2,1,0:T(8,128)(2,1)S(1)} all-to-all(bf16[4,512,512]{2,1,0:T(8,128)(2,1)S(1)} %broadcast_in_dim.7), channel_id=1, replica_groups={{0,1,2,3},{32,33,34,35},{64,65,66,67},{96,97,98,99},{16,48,80,112},{17,..., dimensions={0} | all-to-all | bytes 4194304 | tf_op jit(solution)/shard_map/all_to_all | solution.py:150
  98.4 0.2 broadcast_in_dim.8
  98.5 5.8 %collective-permute-start.1 = (bf16[4,512,512]{2,1,0:T(8,128)(2,1)S(1)}, bf16[4,512,512]{2,1,0:T(8,128)(2,1)S(1)}, u32[]{:S(2)}, u32[]{:S(2)}) collective-permute-start(bf16[4,512,512]{2,1,0:T(8,128)(2,1)S(1)} %all_to_all.20.one_ref), channel_id=1, source_target_pairs={{0,16},{16,0},{1,17},{17,1},{2,18},{18,2},{3,19},{19,3},{4,20},{20... | collective-permute-start | bytes 6291464 | tf_op jit(solution)/shard_map/ppermute | solution.py:154
  104.4 18.0 %all_to_all.21.two_ref = bf16[4,512,512]{2,1,0:T(8,128)(2,1)S(1)} all-to-all(bf16[4,512,512]{2,1,0:T(8,128)(2,1)S(1)} %broadcast_in_dim.8), channel_id=1, replica_groups={{16,17,18,19},{48,49,50,51},{80,81,82,83},{112,113,114,115},{0,32,64,96..., dimensions={0} | all-to-all | bytes 4194304 | tf_op jit(solution)/shard_map/all_to_all | solution.py:150
  122.3 0.0 collective-permute-done.1.rest_0_
  122.3 5.8 %collective-permute-start.2 = (bf16[4,512,512]{2,1,0:T(8,128)(2,1)S(1)}, bf16[4,512,512]{2,1,0:T(8,128)(2,1)S(1)}, u32[]{:S(2)}, u32[]{:S(2)}) collective-permute-start(bf16[4,512,512]{2,1,0:T(8,128)(2,1)S(1)} %all_to_all.21.two_ref), channel_id=1, source_target_pairs={{0,16},{16,0},{1,17},{17,1},{2,18},{18,2},{3,19},{19,3},{4,20},{20... | collective-permute-start | bytes 6291464 | tf_op jit(solution)/shard_map/ppermute | solution.py:154
  128.1 2.3 %hessian_half.2.rest_2_ = f32[512,1024]{1,0:T(8,128)} custom-call(s32[1]{0:T(128)} %bitcast.5.s_ref, bf16[4,512,512]{2,1,0:T(8,128)(2,1)S(1)} %all_to_all.20.one_ref, bf16[4,512,512]{2,1,0:T(8,128)(2,1)S(1)} %all_to_all.21.two_ref), custom_call_target="tpu_custom_call" | custom-call | tf_op jit(solution)/shard_map/hessian_half/pallas_call | solution.py:123
  130.4 1.5 %collective-permute-done.2.rest_1_ = bf16[4,512,512]{2,1,0:T(8,128)(2,1)S(1)} collective-permute-done((bf16[4,512,512]{2,1,0:T(8,128)(2,1)S(1)}, bf16[4,512,512]{2,1,0:T(8,128)(2,1)S(1)}, u32[]{:S(2)}, u32[]{:S(2)}) %collective-permute-start.2) | collective-permute-done | bytes 2097184 | tf_op jit(solution)/shard_map/ppermute | solution.py:154
  131.9 2.2 %hessian_half.3 = f32[512,1024]{1,0:T(8,128)} custom-call(s32[1]{0:T(128)} %bitcast.5.s_ref, bf16[4,512,512]{2,1,0:T(8,128)(2,1)S(1)} %all_to_all.20.one_ref, bf16[4,512,512]{2,1,0:T(8,128)(2,1)S(1)} %all_to_all.21.two_ref, bf16[4,512,512]{2,1,0:T(8,128)(2,1)S(1)} %collective-permute-done.1.rest_0_, ...), custom_call_target="tpu_custom_call", output_to_operand_aliasing={{}: (5, {})} | custom-call | tf_op jit(solution)/shard_map/hessian_half/pallas_call | solution.py:123
Async XLA Ops:
  2.2 9.7 %all-to-all-start = ((bf16[4,272,128]{2,1,0:T(8,128)(2,1)}), bf16[4,272,128]{2,1,0:T(8,128)(2,1)S(1)}, u32[]{:S(2)}, u32[]{:S(2)}) async-start(bf16[4,272,128]{2,1,0:T(8,128)(2,1)} %pack.1), calls=%async_computation | async-start | bytes 557056 | tf_op jit(solution)/shard_map/all_to_all | solution.py:162
  13.7 10.0 %collective-permute-start = (bf16[128,512]{1,0:T(8,128)(2,1)}, bf16[128,512]{1,0:T(8,128)(2,1)S(1)}, u32[]{:S(2)}, u32[]{:S(2)}) collective-permute-start(bf16[128,512]{1,0:T(8,128)(2,1)} %attend.1), channel_id=1, source_target_pairs={{0,0},{1,32},{2,64},{3,96},{4,128},{5,160},{6,192},{7,224},{8,256}... | collective-permute-start | bytes 393224 | tf_op jit(solution)/shard_map/ppermute | solution.py:171
  24.5 47.7 %all-to-all-start.1 = ((bf16[4,128,512]{2,1,0:T(8,128)(2,1)}), bf16[4,128,512]{2,1,0:T(8,128)(2,1)S(1)}, u32[]{:S(2)}, u32[]{:S(2)}) async-start(bf16[4,128,512]{2,1,0:T(8,128)(2,1)} %broadcast_in_dim.6), calls=%async_computation.1 | async-start | bytes 1048576 | tf_op jit(solution)/shard_map/all_to_all | solution.py:162
  98.5 23.8 %collective-permute-start.1 = (bf16[4,512,512]{2,1,0:T(8,128)(2,1)S(1)}, bf16[4,512,512]{2,1,0:T(8,128)(2,1)S(1)}, u32[]{:S(2)}, u32[]{:S(2)}) collective-permute-start(bf16[4,512,512]{2,1,0:T(8,128)(2,1)S(1)} %all_to_all.20.one_ref), channel_id=1, source_target_pairs={{0,16},{16,0},{1,17},{17,1},{2,18},{18,2},{3,19},{19,3},{4,20},{20... | collective-permute-start | bytes 6291464 | tf_op jit(solution)/shard_map/ppermute | solution.py:154
  122.3 9.6 %collective-permute-start.2 = (bf16[4,512,512]{2,1,0:T(8,128)(2,1)S(1)}, bf16[4,512,512]{2,1,0:T(8,128)(2,1)S(1)}, u32[]{:S(2)}, u32[]{:S(2)}) collective-permute-start(bf16[4,512,512]{2,1,0:T(8,128)(2,1)S(1)} %all_to_all.21.two_ref), channel_id=1, source_target_pairs={{0,16},{16,0},{1,17},{17,1},{2,18},{18,2},{3,19},{19,3},{4,20},{20... | collective-permute-start | bytes 6291464 | tf_op jit(solution)/shard_map/ppermute | solution.py:154

commit v4 on v3

--- a/solution.py
+++ b/solution.py
@@ -1,5 +1,3 @@
-import functools
-
 import jax
 import jax.numpy as jnp
 from jax import lax
@@ -88,48 +86,34 @@
 CONTRACT = (((0,), (0,)), ((), ()))
 
 
-def product_kernel(final, s_ref, one_ref, two_ref, *rest):
+def half_kernel(s_ref, rows_ref, own_ref, after_ref, first_ref, second_ref, before_ref, *rest):
     o_ref = rest[-1]
-    core = s_ref[0]
-
-    def product(left, right):
-        depth = left.shape[0] * left.shape[1]
-        o_ref[...] = lax.dot_general(
-            left[...].reshape(depth, left.shape[2]),
-            right[...].reshape(depth, right.shape[2]),
-            CONTRACT,
-            preferred_element_type=jnp.float32,
-        )
-
-    @pl.when(core == 0)
-    def _():
-        product(one_ref, rest[0] if final else two_ref)
-
-    @pl.when(core == 1)
-    def _():
-        product(two_ref, rest[1] if final else one_ref)
+    me = s_ref[0]
+    rows = jnp.concatenate([rows_ref[(me + d) & (RING - 1)] for d in range(RING)], axis=0)
+    pieces = (own_ref, after_ref, first_ref, second_ref, before_ref)
+    cols = jnp.concatenate([ref[...] for ref in pieces], axis=0)
+    o_ref[...] = lax.dot_general(rows, cols, CONTRACT, preferred_element_type=jnp.float32)
 
 
-def hessian_half(core, operands, filled=None):
-    width = operands[0].shape[2]
-    final = filled is not None
-    whole = [pl.BlockSpec(v.shape, lambda i, s: (0, 0, 0)) for v in operands]
-    args = [core, *operands]
+def hessian_half(scalars, rows, pieces, filled=None):
+    width = rows.shape[2]
+    half = pieces[0].shape[1]
+    whole = [pl.BlockSpec(rows.shape, lambda i, s: (0, 0, 0))]
+    whole += [pl.BlockSpec(v.shape, lambda i, s: (0, 0)) for v in pieces]
+    args = [scalars, rows, *pieces]
     aliases = {}
-    if final:
+    if filled is not None:
         aliases = {len(args): 0}
         whole.append(pl.BlockSpec(memory_space=pl.ANY))
         args.append(filled)
     return pl.pallas_call(
-        functools.partial(product_kernel, final),
-        out_shape=jax.ShapeDtypeStruct((width, 2 * width), jnp.float32),
+        half_kernel,
+        out_shape=jax.ShapeDtypeStruct((width, 2 * half), jnp.float32),
         grid_spec=pltpu.PrefetchScalarGridSpec(
             num_scalar_prefetch=1,
             grid=(1,),
             in_specs=whole,
-            out_specs=pl.BlockSpec(
-                (width, width), lambda i, s: (0, 1 - s[0] if final else s[0])
-            ),
+            out_specs=pl.BlockSpec((width, half), lambda i, s: (0, s[1])),
         ),
         input_output_aliases=aliases,
         compiler_params=pltpu.CompilerParams(vmem_limit_bytes=VMEM),
@@ -137,17 +121,8 @@
     )(*args)
 
 
-PLANE = ("y", "core", "x")
-
-
-def mixed_groups(along_x):
-    place = lambda y, core, x: (y * 2 + core) * RING + x
-    groups = [[place(y, along_x, x) for x in range(RING)] for y in range(RING)]
-    return groups + [[place(y, 1 - along_x, x) for y in range(RING)] for x in range(RING)]
-
-
-def exchange_plane(value, along_x):
-    return lax.all_to_all(value, PLANE, 0, 0, axis_index_groups=mixed_groups(along_x), tiled=True)
+def shift(value, axis, by):
+    return lax.ppermute(value, axis, [(i, (i + by) % RING) for i in range(RING)])
 
 
 def swap_cores(value):
@@ -181,21 +156,29 @@
     queries = jnp.transpose(query_rows.reshape(tok, local_heads, HD), (1, 0, 2))
     attended = attend(queries, gathered, positions)
     chunk = swap(attended)
-    chunk, mine = lax.optimization_barrier((chunk, attended))
-    cols = exchange(copies(chunk), "zl").reshape(RING * tok, -1)
-    rows = lax.all_gather(mine, "zh", axis=0, tiled=True)
-    cols, rows = lax.optimization_barrier((cols, rows))
-    core = lax.axis_index("core")
-    one = exchange_plane(copies(jnp.where(core == 0, rows, cols)), 0)
-    later = copies(jnp.where(core == 0, cols, rows))
-    one, later = lax.optimization_barrier((one, later))
-    one_across = swap_cores(one)
-    two = exchange_plane(later, 1)
-    two, one_across = lax.optimization_barrier((two, one_across))
-    two_across = swap_cores(two)
-    core = core.astype(jnp.int32).reshape(1)
-    hessian = hessian_half(core, (one, two))
-    hessian = hessian_half(core, (one, two, one_across, two_across), hessian)
+    rows = lax.all_gather(attended, "zh", axis=0, tiled=True)
+    chunk, rows = lax.optimization_barrier((chunk, rows))
+    rows = exchange(copies(rows), "x")
+    own = lax.all_gather(chunk, "zl", axis=0, tiled=True)
+    after, before = shift(own, "y", -1), shift(own, "y", 1)
+    far_own = swap_cores(own)
+    after, before, far_own = lax.optimization_barrier((after, before, far_own))
+    cut = after.shape[0] // 2
+    first, second, after, before = lax.optimization_barrier(
+        (after[:cut], before[cut:], after, before)
+    )
+    first, second = shift(first, "y", -1), shift(second, "y", 1)
+    far_after, far_before = swap_cores(after), swap_cores(before)
+    first, second, far_after, far_before, rows = lax.optimization_barrier(
+        (first, second, far_after, far_before, rows)
+    )
+    far_first, far_second = swap_cores(first), swap_cores(second)
+    y, core = lax.axis_index("y"), lax.axis_index("core")
+    near = jnp.stack([y, core]).astype(jnp.int32)
+    far = jnp.stack([y, 1 - core]).astype(jnp.int32)
+    hessian = hessian_half(near, rows, (own, after, first, second, before))
+    far_pieces = (far_own, far_after, far_first, far_second, far_before)
+    hessian = hessian_half(far, rows, far_pieces, hessian)
     return attended, hessian
 
 

time: 135 us -> 135 us (level)
  the two profiles are of different devices: /device:TPU:33 before, /device:TPU:1 now
where the time goes in v4:
time: 135 us; the launch traced here: 134 us
  blocking collectives  58.5 us (43%)
  starting transfers between devices  44.1 us (33%)
  waiting for transfers between devices  12.3 us (9%)
  Pallas kernels  10 us (7%)
  local copies, waits for them, and re-layouts  8.55 us (6%)
    all_gather x1, blocking collectives, on_device(): rows = lax.all_gather(attended, 'zh', axis=0, tiled=True)  31.4 us
    all_gather x1, blocking collectives, on_device(): own = lax.all_gather(chunk, 'zl', axis=0, tiled=True)  27.1 us
    ppermute x5, starting transfers between devices, swap_cores(): return lax.ppermute(value, 'core', [(0, 1), (1, 0)])  22.8 us
    ppermute x4, starting transfers between devices, shift(): lax.ppermute(value, axis, [(i, (i + by) % RING) for i in range(RING)])  11.3 us
    all_to_all x2, starting transfers between devices, exchange(): return lax.all_to_all(value, axis, split_axis=0, concat_axis=0, tiled=True)  8.45 us
    ppermute x4, waiting for transfers between devices, shift(): lax.ppermute(value, axis, [(i, (i + by) % RING) for i in range(RING)])  7.21 us
    pallas_call x2, Pallas kernels, hessian_half(): pl.pallas_call(half_kernel, out_shape=jax.ShapeDtypeStruct((width, 2 * ha...  6.63 us
    unnamed x21, local copies, waits for them, and re-layouts  6.13 us
  transfers between devices with their start and end apart: 12, of which 5 were waited for; matrix products, arithmetic and copies ran while one was open for 2% of the time, Pallas kernels for 2%

profile of v4, /device:TPU:1, one launch (start us, length us, event | category | flops | bytes accessed | tf_op | source)
XLA Modules:
  0.0 134.4 jit_solution(7102437295080944659)
XLA Ops:
  0.7 1.5 %pack.1 = bf16[4,272,128]{2,1,0:T(8,128)(2,1)} custom-call(s32[1]{0:T(128)} %bitcast.2.g_ref, bf16[128,1024]{1,0:T(8,128)(2,1)} %k_ref.1, bf16[128,1024]{1,0:T(8,128)(2,1)} %v_ref.1, s32[1,128]{1,0:T(1,128)} %bitcast.10), custom_call_target="tpu_custom_call" | custom-call | tf_op jit(solution)/shard_map/pack/pallas_call | solution.py:34
  2.2 4.8 %all-to-all-start = ((bf16[4,272,128]{2,1,0:T(8,128)(2,1)}), bf16[4,272,128]{2,1,0:T(8,128)(2,1)S(1)}, u32[]{:S(2)}, u32[]{:S(2)}) async-start(bf16[4,272,128]{2,1,0:T(8,128)(2,1)} %pack.1), calls=%async_computation | async-start | bytes 557056 | tf_op jit(solution)/shard_map/all_to_all | solution.py:137
  9.0 3.7 %all-to-all-done.kv_ref = bf16[4,272,128]{2,1,0:T(8,128)(2,1)S(1)} async-done(((bf16[4,272,128]{2,1,0:T(8,128)(2,1)}), bf16[4,272,128]{2,1,0:T(8,128)(2,1)S(1)}, u32[]{:S(2)}, u32[]{:S(2)}) %all-to-all-start) | async-done | bytes 278560 | tf_op jit(solution)/shard_map/all_to_all | solution.py:137
  12.6 1.8 %attend.1 = bf16[128,512]{1,0:T(8,128)(2,1)} custom-call(bf16[4,128,128]{2,1,0:T(8,128)(2,1)S(1)} %bitcast.8, bf16[4,272,128]{2,1,0:T(8,128)(2,1)S(1)} %all-to-all-done.kv_ref, s32[128,1]{1,0:T(8,128)S(1)} %copy.10.p_ref), custom_call_target="tpu_custom_call" | custom-call | tf_op jit(solution)/shard_map/attend/pallas_call | solution.py:78
  14.5 1.6 %collective-permute-start = (bf16[128,512]{1,0:T(8,128)(2,1)}, bf16[128,512]{1,0:T(8,128)(2,1)S(1)}, u32[]{:S(2)}, u32[]{:S(2)}) collective-permute-start(bf16[128,512]{1,0:T(8,128)(2,1)} %attend.1), channel_id=1, source_target_pairs={{0,0},{1,32},{2,64},{3,96},{4,128},{5,160},{6,192},{7,224},{8,256}... | collective-permute-start | bytes 393224 | tf_op jit(solution)/shard_map/ppermute | solution.py:146
  16.0 31.4 %all_gather.6 = bf16[512,512]{1,0:T(8,128)(2,1)S(1)} all-gather(bf16[128,512]{1,0:T(8,128)(2,1)} %attend.1), channel_id=1, replica_groups=mesh['zl'=4,'y'=4,'core'=2,'zh'=4,'x'=4] {'zh'}, dimensions={0}, use_global_device_ids=true | all-gather | bytes 655360 | tf_op jit(solution)/shard_map/all_gather | solution.py:159
  47.5 1.5 %broadcast_in_dim.2 = bf16[4,512,512]{2,1,0:T(8,128)(2,1)} broadcast(bf16[512,512]{1,0:T(8,128)(2,1)S(1)} %all_gather.6), dimensions={1,2} | broadcast | bytes 2621440 | tf_op jit(solution)/shard_map/broadcast_in_dim | solution.py:133
  49.0 3.6 %all-to-all-start.1 = ((bf16[4,512,512]{2,1,0:T(8,128)(2,1)}), bf16[4,512,512]{2,1,0:T(8,128)(2,1)S(1)}, u32[]{:S(2)}, u32[]{:S(2)}) async-start(bf16[4,512,512]{2,1,0:T(8,128)(2,1)} %broadcast_in_dim.2), calls=%async_computation.1 | async-start | bytes 4194304 | tf_op jit(solution)/shard_map/all_to_all | solution.py:137
  52.6 27.1 %all_gather.7.own_ref = bf16[512,512]{1,0:T(8,128)(2,1)S(1)} all-gather(bf16[128,512]{1,0:T(8,128)(2,1)S(1)} %collective-permute-done), channel_id=1, replica_groups=mesh['zl'=4,'y'=4,'core'=2,'zh'=4,'x'=4] {'zl'}, dimensions={0}, use_global_device_ids=true | all-gather | bytes 655360 | tf_op jit(solution)/shard_map/all_gather | solution.py:162
  79.6 3.8 %collective-permute-start.1 = (bf16[512,512]{1,0:T(8,128)(2,1)S(1)}, bf16[512,512]{1,0:T(8,128)(2,1)S(1)}, u32[]{:S(2)}, u32[]{:S(2)}) collective-permute-start(bf16[512,512]{1,0:T(8,128)(2,1)S(1)} %all_gather.7.own_ref), channel_id=1, source_target_pairs={{0,96},{32,0},{64,32},{96,64},{1,97},{33,1},{65,33},{97,65},{2,98}... | collective-permute-start | bytes 1572872 | tf_op jit(solution)/shard_map/ppermute | solution.py:125
  83.5 2.2 %collective-permute-start.2 = (bf16[512,512]{1,0:T(8,128)(2,1)S(1)}, bf16[512,512]{1,0:T(8,128)(2,1)S(1)}, u32[]{:S(2)}, u32[]{:S(2)}) collective-permute-start(bf16[512,512]{1,0:T(8,128)(2,1)S(1)} %all_gather.7.own_ref), channel_id=1, source_target_pairs={{0,32},{32,64},{64,96},{96,0},{1,33},{33,65},{65,97},{97,1},{2,34}... | collective-permute-start | bytes 1572872 | tf_op jit(solution)/shard_map/ppermute | solution.py:125
  85.7 8.8 %collective-permute-start.3 = (bf16[512,512]{1,0:T(8,128)(2,1)S(1)}, bf16[512,512]{1,0:T(8,128)(2,1)S(1)}, u32[]{:S(2)}, u32[]{:S(2)}) collective-permute-start(bf16[512,512]{1,0:T(8,128)(2,1)S(1)} %all_gather.7.own_ref), channel_id=1, source_target_pairs={{0,16},{16,0},{1,17},{17,1},{2,18},{18,2},{3,19},{19,3},{4,20},{20... | collective-permute-start | bytes 1572872 | tf_op jit(solution)/shard_map/ppermute | solution.py:129
  94.6 1.4 %collective-permute-done.3.own_ref = bf16[512,512]{1,0:T(8,128)(2,1)S(1)} collective-permute-done((bf16[512,512]{1,0:T(8,128)(2,1)S(1)}, bf16[512,512]{1,0:T(8,128)(2,1)S(1)}, u32[]{:S(2)}, u32[]{:S(2)}) %collective-permute-start.3) | collective-permute-done | bytes 524320 | tf_op jit(solution)/shard_map/ppermute | solution.py:129
  96.8 6.9 %collective-permute-start.6 = (bf16[512,512]{1,0:T(8,128)(2,1)S(1)}, bf16[512,512]{1,0:T(8,128)(2,1)S(1)}, u32[]{:S(2)}, u32[]{:S(2)}) collective-permute-start(bf16[512,512]{1,0:T(8,128)(2,1)S(1)} %collective-permute-done.1.after_ref), channel_id=1, source_target_pairs={{0,16},{16,0},{1,17},{17,1},{2,18},{18,2},{3,19},{19,3},{4,20},{20... | collective-permute-start | bytes 1572872 | tf_op jit(solution)/shard_map/ppermute | solution.py:129
  103.7 1.9 %collective-permute-start.7 = (bf16[512,512]{1,0:T(8,128)(2,1)S(1)}, bf16[512,512]{1,0:T(8,128)(2,1)S(1)}, u32[]{:S(2)}, u32[]{:S(2)}) collective-permute-start(bf16[512,512]{1,0:T(8,128)(2,1)S(1)} %collective-permute-done.2.before_ref), channel_id=1, source_target_pairs={{0,16},{16,0},{1,17},{17,1},{2,18},{18,2},{3,19},{19,3},{4,20},{20... | collective-permute-start | bytes 1572872 | tf_op jit(solution)/shard_map/ppermute | solution.py:129
  105.6 1.9 %collective-permute-start.4 = (bf16[256,512]{1,0:T(8,128)(2,1)S(1)}, bf16[256,512]{1,0:T(8,128)(2,1)S(1)}, u32[]{:S(2)}, u32[]{:S(2)}) collective-permute-start(bf16[256,512]{1,0:T(8,128)(2,1)S(1)} %slice.6), channel_id=1, source_target_pairs={{0,96},{32,0},{64,32},{96,64},{1,97},{33,1},{65,33},{97,65},{2,98}... | collective-permute-start | bytes 786440 | tf_op jit(solution)/shard_map/ppermute | solution.py:125
  107.6 3.4 %collective-permute-start.5 = (bf16[256,512]{1,0:T(8,128)(2,1)S(1)}, bf16[256,512]{1,0:T(8,128)(2,1)S(1)}, u32[]{:S(2)}, u32[]{:S(2)}) collective-permute-start(bf16[256,512]{1,0:T(8,128)(2,1)S(1)} %slice.7), channel_id=1, source_target_pairs={{0,32},{32,64},{64,96},{96,0},{1,33},{33,65},{65,97},{97,1},{2,34}... | collective-permute-start | bytes 786440 | tf_op jit(solution)/shard_map/ppermute | solution.py:125
  110.9 4.0 %collective-permute-done.4.first_ref = bf16[256,512]{1,0:T(8,128)(2,1)S(1)} collective-permute-done((bf16[256,512]{1,0:T(8,128)(2,1)S(1)}, bf16[256,512]{1,0:T(8,128)(2,1)S(1)}, u32[]{:S(2)}, u32[]{:S(2)}) %collective-permute-start.4) | collective-permute-done | bytes 262176 | tf_op jit(solution)/shard_map/ppermute | solution.py:125
  114.9 3.1 %collective-permute-done.5.second_ref = bf16[256,512]{1,0:T(8,128)(2,1)S(1)} collective-permute-done((bf16[256,512]{1,0:T(8,128)(2,1)S(1)}, bf16[256,512]{1,0:T(8,128)(2,1)S(1)}, u32[]{:S(2)}, u32[]{:S(2)}) %collective-permute-start.5) | collective-permute-done | bytes 262176 | tf_op jit(solution)/shard_map/ppermute | solution.py:125
  120.4 3.2 %collective-permute-start.8 = (bf16[256,512]{1,0:T(8,128)(2,1)S(1)}, bf16[256,512]{1,0:T(8,128)(2,1)}, u32[]{:S(2)}, u32[]{:S(2)}) collective-permute-start(bf16[256,512]{1,0:T(8,128)(2,1)S(1)} %collective-permute-done.4.first_ref), channel_id=1, source_target_pairs={{0,16},{16,0},{1,17},{17,1},{2,18},{18,2},{3,19},{19,3},{4,20},{20... | collective-permute-start | bytes 786440 | tf_op jit(solution)/shard_map/ppermute | solution.py:129
  123.6 1.9 %collective-permute-start.9 = (bf16[256,512]{1,0:T(8,128)(2,1)}, bf16[256,512]{1,0:T(8,128)(2,1)}, u32[]{:S(2)}, u32[]{:S(2)}) collective-permute-start(bf16[256,512]{1,0:T(8,128)(2,1)} %copy-done.8), channel_id=1, source_target_pairs={{0,16},{16,0},{1,17},{17,1},{2,18},{18,2},{3,19},{19,3},{4,20},{20... | collective-permute-start | bytes 786440 | tf_op jit(solution)/shard_map/ppermute | solution.py:129
  125.7 1.0 copy-done.1
  127.7 2.8 %hessian_half.2.rest_0_ = f32[512,1024]{1,0:T(8,128)} custom-call(s32[2]{0:T(128)S(1)} %pad_add_fusion.1.s_ref, bf16[4,512,512]{2,1,0:T(8,128)(2,1)S(1)} %all-to-all-done.1.rows_ref, bf16[512,512]{1,0:T(8,128)(2,1)S(1)} %all_gather.7.own_ref, bf16[512,512]{1,0:T(8,128)(2,1)S(1)} %collective-permute-done.1.after_ref, ...), custom_call_target="tpu_custom_call" | custom-call | tf_op jit(solution)/shard_map/hessian_half/pallas_call | solution.py:109
  130.5 3.8 %hessian_half.3 = f32[512,1024]{1,0:T(8,128)} custom-call(s32[2]{0:T(128)S(1)} %pad_add_fusion.s_ref, bf16[4,512,512]{2,1,0:T(8,128)(2,1)S(1)} %all-to-all-done.1.rows_ref, bf16[512,512]{1,0:T(8,128)(2,1)S(1)} %copy-done.3, bf16[512,512]{1,0:T(8,128)(2,1)S(1)} %copy-done.5, ...), custom_call_target="tpu_custom_call", output_to_operand_aliasing={{}: (7, {})} | custom-call | tf_op jit(solution)/shard_map/hessian_half/pallas_call | solution.py:109
  (34 shorter events, 6.3 us)
Async XLA Ops:
  2.2 10.5 %all-to-all-start = ((bf16[4,272,128]{2,1,0:T(8,128)(2,1)}), bf16[4,272,128]{2,1,0:T(8,128)(2,1)S(1)}, u32[]{:S(2)}, u32[]{:S(2)}) async-start(bf16[4,272,128]{2,1,0:T(8,128)(2,1)} %pack.1), calls=%async_computation | async-start | bytes 557056 | tf_op jit(solution)/shard_map/all_to_all | solution.py:137
  14.5 33.0 %collective-permute-start = (bf16[128,512]{1,0:T(8,128)(2,1)}, bf16[128,512]{1,0:T(8,128)(2,1)S(1)}, u32[]{:S(2)}, u32[]{:S(2)}) collective-permute-start(bf16[128,512]{1,0:T(8,128)(2,1)} %attend.1), channel_id=1, source_target_pairs={{0,0},{1,32},{2,64},{3,96},{4,128},{5,160},{6,192},{7,224},{8,256}... | collective-permute-start | bytes 393224 | tf_op jit(solution)/shard_map/ppermute | solution.py:146
  49.0 71.4 %all-to-all-start.1 = ((bf16[4,512,512]{2,1,0:T(8,128)(2,1)}), bf16[4,512,512]{2,1,0:T(8,128)(2,1)S(1)}, u32[]{:S(2)}, u32[]{:S(2)}) async-start(bf16[4,512,512]{2,1,0:T(8,128)(2,1)} %broadcast_in_dim.2), calls=%async_computation.1 | async-start | bytes 4194304 | tf_op jit(solution)/shard_map/all_to_all | solution.py:137
  79.6 14.9 %collective-permute-start.1 = (bf16[512,512]{1,0:T(8,128)(2,1)S(1)}, bf16[512,512]{1,0:T(8,128)(2,1)S(1)}, u32[]{:S(2)}, u32[]{:S(2)}) collective-permute-start(bf16[512,512]{1,0:T(8,128)(2,1)S(1)} %all_gather.7.own_ref), channel_id=1, source_target_pairs={{0,96},{32,0},{64,32},{96,64},{1,97},{33,1},{65,33},{97,65},{2,98}... | collective-permute-start | bytes 1572872 | tf_op jit(solution)/shard_map/ppermute | solution.py:125
  83.5 11.1 %collective-permute-start.2 = (bf16[512,512]{1,0:T(8,128)(2,1)S(1)}, bf16[512,512]{1,0:T(8,128)(2,1)S(1)}, u32[]{:S(2)}, u32[]{:S(2)}) collective-permute-start(bf16[512,512]{1,0:T(8,128)(2,1)S(1)} %all_gather.7.own_ref), channel_id=1, source_target_pairs={{0,32},{32,64},{64,96},{96,0},{1,33},{33,65},{65,97},{97,1},{2,34}... | collective-permute-start | bytes 1572872 | tf_op jit(solution)/shard_map/ppermute | solution.py:125
  85.7 10.3 %collective-permute-start.3 = (bf16[512,512]{1,0:T(8,128)(2,1)S(1)}, bf16[512,512]{1,0:T(8,128)(2,1)S(1)}, u32[]{:S(2)}, u32[]{:S(2)}) collective-permute-start(bf16[512,512]{1,0:T(8,128)(2,1)S(1)} %all_gather.7.own_ref), channel_id=1, source_target_pairs={{0,16},{16,0},{1,17},{17,1},{2,18},{18,2},{3,19},{19,3},{4,20},{20... | collective-permute-start | bytes 1572872 | tf_op jit(solution)/shard_map/ppermute | solution.py:129
  94.6 23.5 %copy-start = (bf16[512,512]{1,0:T(8,128)(2,1)}, bf16[512,512]{1,0:T(8,128)(2,1)S(1)}, u32[]{:S(2)}) copy-start(bf16[512,512]{1,0:T(8,128)(2,1)S(1)} %collective-permute-done.2.before_ref) | copy-start | bytes 1572868
  96.0 0.8 copy-start.2
  96.8 21.2 %collective-permute-start.6 = (bf16[512,512]{1,0:T(8,128)(2,1)S(1)}, bf16[512,512]{1,0:T(8,128)(2,1)S(1)}, u32[]{:S(2)}, u32[]{:S(2)}) collective-permute-start(bf16[512,512]{1,0:T(8,128)(2,1)S(1)} %collective-permute-done.1.after_ref), channel_id=1, source_target_pairs={{0,16},{16,0},{1,17},{17,1},{2,18},{18,2},{3,19},{19,3},{4,20},{20... | collective-permute-start | bytes 1572872 | tf_op jit(solution)/shard_map/ppermute | solution.py:129
  103.7 15.8 %collective-permute-start.7 = (bf16[512,512]{1,0:T(8,128)(2,1)S(1)}, bf16[512,512]{1,0:T(8,128)(2,1)S(1)}, u32[]{:S(2)}, u32[]{:S(2)}) collective-permute-start(bf16[512,512]{1,0:T(8,128)(2,1)S(1)} %collective-permute-done.2.before_ref), channel_id=1, source_target_pairs={{0,16},{16,0},{1,17},{17,1},{2,18},{18,2},{3,19},{19,3},{4,20},{20... | collective-permute-start | bytes 1572872 | tf_op jit(solution)/shard_map/ppermute | solution.py:129
  105.6 9.3 %collective-permute-start.4 = (bf16[256,512]{1,0:T(8,128)(2,1)S(1)}, bf16[256,512]{1,0:T(8,128)(2,1)S(1)}, u32[]{:S(2)}, u32[]{:S(2)}) collective-permute-start(bf16[256,512]{1,0:T(8,128)(2,1)S(1)} %slice.6), channel_id=1, source_target_pairs={{0,96},{32,0},{64,32},{96,64},{1,97},{33,1},{65,33},{97,65},{2,98}... | collective-permute-start | bytes 786440 | tf_op jit(solution)/shard_map/ppermute | solution.py:125
  107.6 10.5 %collective-permute-start.5 = (bf16[256,512]{1,0:T(8,128)(2,1)S(1)}, bf16[256,512]{1,0:T(8,128)(2,1)S(1)}, u32[]{:S(2)}, u32[]{:S(2)}) collective-permute-start(bf16[256,512]{1,0:T(8,128)(2,1)S(1)} %slice.7), channel_id=1, source_target_pairs={{0,32},{32,64},{64,96},{96,0},{1,33},{33,65},{65,97},{97,1},{2,34}... | collective-permute-start | bytes 786440 | tf_op jit(solution)/shard_map/ppermute | solution.py:125
  118.1 0.7 copy-start.8
  118.8 0.8 copy-start.4
  119.6 0.8 copy-start.6
  120.4 10.1 %collective-permute-start.8 = (bf16[256,512]{1,0:T(8,128)(2,1)S(1)}, bf16[256,512]{1,0:T(8,128)(2,1)}, u32[]{:S(2)}, u32[]{:S(2)}) collective-permute-start(bf16[256,512]{1,0:T(8,128)(2,1)S(1)} %collective-permute-done.4.first_ref), channel_id=1, source_target_pairs={{0,16},{16,0},{1,17},{17,1},{2,18},{18,2},{3,19},{19,3},{4,20},{20... | collective-permute-start | bytes 786440 | tf_op jit(solution)/shard_map/ppermute | solution.py:129
  123.6 6.9 %collective-permute-start.9 = (bf16[256,512]{1,0:T(8,128)(2,1)}, bf16[256,512]{1,0:T(8,128)(2,1)}, u32[]{:S(2)}, u32[]{:S(2)}) collective-permute-start(bf16[256,512]{1,0:T(8,128)(2,1)} %copy-done.8), channel_id=1, source_target_pairs={{0,16},{16,0},{1,17},{17,1},{2,18},{18,2},{3,19},{19,3},{4,20},{20... | collective-permute-start | bytes 786440 | tf_op jit(solution)/shard_map/ppermute | solution.py:129
  125.7 1.0 copy-start.1
  126.8 0.9 copy-start.9
  127.7 2.8 %copy-start.3 = (bf16[512,512]{1,0:T(8,128)(2,1)S(1)}, bf16[512,512]{1,0:T(8,128)(2,1)}, u32[]{:S(2)}) copy-start(bf16[512,512]{1,0:T(8,128)(2,1)} %copy-done.2) | copy-start | bytes 1572868
  127.7 2.8 %copy-start.5 = (bf16[512,512]{1,0:T(8,128)(2,1)S(1)}, bf16[512,512]{1,0:T(8,128)(2,1)}, u32[]{:S(2)}) copy-start(bf16[512,512]{1,0:T(8,128)(2,1)} %copy-done.4) | copy-start | bytes 1572868
  127.7 2.8 %copy-start.7 = (bf16[512,512]{1,0:T(8,128)(2,1)S(1)}, bf16[512,512]{1,0:T(8,128)(2,1)}, u32[]{:S(2)}) copy-start(bf16[512,512]{1,0:T(8,128)(2,1)} %copy-done.6) | copy-start | bytes 1572868

commit v5 on v4

--- a/solution.py
+++ b/solution.py
@@ -1,3 +1,5 @@
+import itertools
+
 import jax
 import jax.numpy as jnp
 from jax import lax
@@ -83,24 +85,34 @@
     )(queries, gathered, positions.reshape(tok, 1))
 
 
+LANDING = ((0, 2, 3, 1), (2, 1, 3, 0), (3, 0, 2, 1), (2, 0, 1, 3))
 CONTRACT = (((0,), (0,)), ((), ()))
 
 
-def half_kernel(s_ref, rows_ref, own_ref, after_ref, first_ref, second_ref, before_ref, *rest):
+def half_kernel(s_ref, rows_ref, cols_ref, *rest):
     o_ref = rest[-1]
-    me = s_ref[0]
-    rows = jnp.concatenate([rows_ref[(me + d) & (RING - 1)] for d in range(RING)], axis=0)
-    pieces = (own_ref, after_ref, first_ref, second_ref, before_ref)
-    cols = jnp.concatenate([ref[...] for ref in pieces], axis=0)
-    o_ref[...] = lax.dot_general(rows, cols, CONTRACT, preferred_element_type=jnp.float32)
+    x, zh = s_ref[0], s_ref[2]
+    tok = cols_ref.shape[1] // RING
+    blocks = []
+    for d in range(RING):
+        for span in range(RING):
+            place = jnp.int32(LANDING[0][span])
+            for group in range(1, RING):
+                place = jnp.where(zh == group, LANDING[group][span], place)
+            part = pl.ds(pl.multiple_of(place * tok, tok), tok)
+            blocks.append(cols_ref[(x + d) & (RING - 1), part])
+    cols = jnp.concatenate(blocks, axis=0)
+    o_ref[...] = lax.dot_general(rows_ref[...], cols, CONTRACT, preferred_element_type=jnp.float32)
 
 
-def hessian_half(scalars, rows, pieces, filled=None):
-    width = rows.shape[2]
-    half = pieces[0].shape[1]
-    whole = [pl.BlockSpec(rows.shape, lambda i, s: (0, 0, 0))]
-    whole += [pl.BlockSpec(v.shape, lambda i, s: (0, 0)) for v in pieces]
-    args = [scalars, rows, *pieces]
+def hessian_half(scalars, rows, cols, filled=None):
+    width = rows.shape[1]
+    half = cols.shape[2]
+    whole = [
+        pl.BlockSpec(rows.shape, lambda i, s: (0, 0)),
+        pl.BlockSpec(cols.shape, lambda i, s: (0, 0, 0)),
+    ]
+    args = [scalars, rows, cols]
     aliases = {}
     if filled is not None:
         aliases = {len(args): 0}
@@ -138,11 +150,10 @@
 
 
 def swap(value):
+    at = lambda zl, y, core, zh, x: (((zl * RING + y) * 2 + core) * RING + zh) * RING + x
     pairs = []
-    for chip in range(16):
-        for core in range(2):
-            for span in range(16):
-                pairs.append(((chip * 2 + core) * 16 + span, (span * 2 + core) * 16 + chip))
+    for zl, y, core, zh, x in itertools.product(*(range(n) for n in (RING, RING, 2, RING, RING))):
+        pairs.append((at(zl, y, core, zh, x), at(LANDING[zl][zh], x, core, zl, y)))
     return lax.ppermute(value, HEAD + SEQ, pairs)
 
 
@@ -158,27 +169,20 @@
     chunk = swap(attended)
     rows = lax.all_gather(attended, "zh", axis=0, tiled=True)
     chunk, rows = lax.optimization_barrier((chunk, rows))
-    rows = exchange(copies(rows), "x")
-    own = lax.all_gather(chunk, "zl", axis=0, tiled=True)
-    after, before = shift(own, "y", -1), shift(own, "y", 1)
-    far_own = swap_cores(own)
-    after, before, far_own = lax.optimization_barrier((after, before, far_own))
+    cols = lax.all_gather(chunk, "zl", axis=0, tiled=True)
+    cols, rows = lax.optimization_barrier((cols, rows))
+    near_cols = exchange(copies(cols), "y")
+    after, before = shift(rows, "x", -1), shift(rows, "x", 1)
     cut = after.shape[0] // 2
-    first, second, after, before = lax.optimization_barrier(
-        (after[:cut], before[cut:], after, before)
-    )
-    first, second = shift(first, "y", -1), shift(second, "y", 1)
-    far_after, far_before = swap_cores(after), swap_cores(before)
-    first, second, far_after, far_before, rows = lax.optimization_barrier(
-        (first, second, far_after, far_before, rows)
-    )
-    far_first, far_second = swap_cores(first), swap_cores(second)
-    y, core = lax.axis_index("y"), lax.axis_index("core")
-    near = jnp.stack([y, core]).astype(jnp.int32)
-    far = jnp.stack([y, 1 - core]).astype(jnp.int32)
-    hessian = hessian_half(near, rows, (own, after, first, second, before))
-    far_pieces = (far_own, far_after, far_first, far_second, far_before)
-    hessian = hessian_half(far, rows, far_pieces, hessian)
+    first, second = shift(after[:cut], "x", -1), shift(before[cut:], "x", 1)
+    rows = jnp.concatenate([rows, after, first, second, before])
+    near_cols, rows = lax.optimization_barrier((near_cols, rows))
+    far_cols = swap_cores(near_cols)
+    place = lax.axis_index("x"), lax.axis_index("core"), lax.axis_index("zh")
+    near = jnp.stack(place).astype(jnp.int32)
+    far = jnp.stack((place[0], 1 - place[1], place[2])).astype(jnp.int32)
+    hessian = hessian_half(near, rows, near_cols)
+    hessian = hessian_half(far, rows, far_cols, hessian)
     return attended, hessian
 
 

time: 135 us -> 121 us (0.90)
  starting transfers between devices: 44.1 us -> 37 us
  blocking collectives: 58.5 us -> 51.7 us
  local copies, waits for them, and re-layouts: 8.55 us -> 3.58 us
  waiting for transfers between devices: 12.3 us -> 15.4 us
  Pallas kernels: 10 us -> 12.1 us
    ppermute x5 -> x1, starting transfers between devices: 22.8 us -> 7.96 us  [swap_cores(): return lax.ppermute(value, 'core', [(0, 1), (1, 0)])]
    ppermute x4, starting transfers between devices: 11.3 us -> 18.2 us  [shift(): lax.ppermute(value, axis, [(i, (i + by) % RING) for i in range(RING)])]
    all_gather x1, blocking collectives: 27.1 us -> 20.3 us  [on_device(): cols = lax.all_gather(chunk, 'zl', axis=0, tiled=True)]
    unnamed x21 -> x5, local copies, waits for them, and re-layouts: 6.13 us -> 1.13 us
    ppermute x4, waiting for transfers between devices: 7.21 us -> 11.8 us  [shift(): lax.ppermute(value, axis, [(i, (i + by) % RING) for i in range(RING)])]
    pallas_call x2, Pallas kernels: 6.63 us -> 8.75 us  [hessian_half(): pl.pallas_call(half_kernel, out_shape=jax.ShapeDtypeStruct((width, 2 * ha...]
    ppermute x5 -> x1, waiting for transfers between devices: 1.41 us -> 0.01 us  [swap_cores(): return lax.ppermute(value, 'core', [(0, 1), (1, 0)])]
  transfers between devices with their start and end apart: 12 -> 8, of which waited for: 5 -> 4; matrix products, arithmetic and copies ran while one was open for 2% -> 2% of each run, Pallas kernels for 2% -> 4%
where the time goes in v5:
time: 121 us
  blocking collectives  51.7 us (43%)
  starting transfers between devices  37 us (31%)
  waiting for transfers between devices  15.4 us (13%)
  Pallas kernels  12.1 us (10%)
  local copies, waits for them, and re-layouts  3.58 us (3%)
    all_gather x1, blocking collectives, on_device(): rows = lax.all_gather(attended, 'zh', axis=0, tiled=True)  31.4 us
    all_gather x1, blocking collectives, on_device(): cols = lax.all_gather(chunk, 'zl', axis=0, tiled=True)  20.3 us
    ppermute x4, starting transfers between devices, shift(): lax.ppermute(value, axis, [(i, (i + by) % RING) for i in range(RING)])  18.2 us
    ppermute x4, waiting for transfers between devices, shift(): lax.ppermute(value, axis, [(i, (i + by) % RING) for i in range(RING)])  11.8 us
    all_to_all x2, starting transfers between devices, exchange(): return lax.all_to_all(value, axis, split_axis=0, concat_axis=0, tiled=True)  9.29 us
    pallas_call x2, Pallas kernels, hessian_half(): pl.pallas_call(half_kernel, out_shape=jax.ShapeDtypeStruct((width, 2 * ha...  8.75 us
    ppermute x1, starting transfers between devices, swap_cores(): return lax.ppermute(value, 'core', [(0, 1), (1, 0)])  7.96 us
    all_to_all x2, waiting for transfers between devices, exchange(): return lax.all_to_all(value, axis, split_axis=0, concat_axis=0, tiled=True)  3.69 us
  transfers between devices with their start and end apart: 8, of which 4 were waited for; matrix products, arithmetic and copies ran while one was open for 2% of the time, Pallas kernels for 4%

profile of v5, /device:TPU:1, one launch (start us, length us, event | category | flops | bytes accessed | tf_op | source)
XLA Modules:
  0.0 120.7 jit_solution(12224854773947421514)
XLA Ops:
  0.7 1.5 %pack.1 = bf16[4,272,128]{2,1,0:T(8,128)(2,1)} custom-call(s32[1]{0:T(128)} %bitcast.2.g_ref, bf16[128,1024]{1,0:T(8,128)(2,1)} %k_ref.1, bf16[128,1024]{1,0:T(8,128)(2,1)} %v_ref.1, s32[1,128]{1,0:T(1,128)} %bitcast.11), custom_call_target="tpu_custom_call" | custom-call | tf_op jit(solution)/shard_map/pack/pallas_call | solution.py:36
  2.2 4.8 %all-to-all-start = ((bf16[4,272,128]{2,1,0:T(8,128)(2,1)}), bf16[4,272,128]{2,1,0:T(8,128)(2,1)S(1)}, u32[]{:S(2)}, u32[]{:S(2)}) async-start(bf16[4,272,128]{2,1,0:T(8,128)(2,1)} %pack.1), calls=%async_computation | async-start | bytes 557056 | tf_op jit(solution)/shard_map/all_to_all | solution.py:149
  7.0 1.0 copy.8
  8.0 0.1 copy.9
  8.2 0.8 copy.10.p_ref
  9.0 3.7 %all-to-all-done.kv_ref = bf16[4,272,128]{2,1,0:T(8,128)(2,1)S(1)} async-done(((bf16[4,272,128]{2,1,0:T(8,128)(2,1)}), bf16[4,272,128]{2,1,0:T(8,128)(2,1)S(1)}, u32[]{:S(2)}, u32[]{:S(2)}) %all-to-all-start) | async-done | bytes 278560 | tf_op jit(solution)/shard_map/all_to_all | solution.py:149
  12.6 1.8 %attend.1 = bf16[128,512]{1,0:T(8,128)(2,1)} custom-call(bf16[4,128,128]{2,1,0:T(8,128)(2,1)S(1)} %bitcast.9, bf16[4,272,128]{2,1,0:T(8,128)(2,1)S(1)} %all-to-all-done.kv_ref, s32[128,1]{1,0:T(8,128)S(1)} %copy.10.p_ref), custom_call_target="tpu_custom_call" | custom-call | tf_op jit(solution)/shard_map/attend/pallas_call | solution.py:80
  14.5 1.6 %collective-permute-start = (bf16[128,512]{1,0:T(8,128)(2,1)}, bf16[128,512]{1,0:T(8,128)(2,1)S(1)}, u32[]{:S(2)}, u32[]{:S(2)}) collective-permute-start(bf16[128,512]{1,0:T(8,128)(2,1)} %attend.1), channel_id=1, source_target_pairs={{0,0},{1,32},{2,64},{3,96},{4,256},{5,288},{6,320},{7,352},{8,384}... | collective-permute-start | bytes 393224 | tf_op jit(solution)/shard_map/ppermute | solution.py:157
  16.0 31.4 %all_gather.6 = bf16[512,512]{1,0:T(8,128)(2,1)S(1)} all-gather(bf16[128,512]{1,0:T(8,128)(2,1)} %attend.1), channel_id=1, replica_groups=mesh['zl'=4,'y'=4,'core'=2,'zh'=4,'x'=4] {'zh'}, dimensions={0}, use_global_device_ids=true | all-gather | bytes 655360 | tf_op jit(solution)/shard_map/all_gather | solution.py:170
  47.5 20.3 %all_gather.7 = bf16[512,512]{1,0:T(8,128)(2,1)S(1)} all-gather(bf16[128,512]{1,0:T(8,128)(2,1)S(1)} %collective-permute-done), channel_id=1, replica_groups=mesh['zl'=4,'y'=4,'core'=2,'zh'=4,'x'=4] {'zl'}, dimensions={0}, use_global_device_ids=true | all-gather | bytes 655360 | tf_op jit(solution)/shard_map/all_gather | solution.py:172
  67.7 1.5 %broadcast_in_dim.2 = bf16[4,512,512]{2,1,0:T(8,128)(2,1)} broadcast(bf16[512,512]{1,0:T(8,128)(2,1)S(1)} %all_gather.7), dimensions={1,2} | broadcast | bytes 2621440 | tf_op jit(solution)/shard_map/broadcast_in_dim | solution.py:145
  69.2 4.5 %all-to-all-start.1 = ((bf16[4,512,512]{2,1,0:T(8,128)(2,1)}), bf16[4,512,512]{2,1,0:T(8,128)(2,1)}, u32[]{:S(2)}, u32[]{:S(2)}) async-start(bf16[4,512,512]{2,1,0:T(8,128)(2,1)} %broadcast_in_dim.2), calls=%async_computation.1 | async-start | bytes 4194304 | tf_op jit(solution)/shard_map/all_to_all | solution.py:149
  73.7 8.9 %collective-permute-start.1 = (bf16[512,512]{1,0:T(8,128)(2,1)S(1)}, bf16[512,512]{1,0:T(8,128)(2,1)S(1)}, u32[]{:S(2)}, u32[]{:S(2)}) collective-permute-start(bf16[512,512]{1,0:T(8,128)(2,1)S(1)} %all_gather.6), channel_id=1, source_target_pairs={{0,3},{1,0},{2,1},{3,2},{4,7},{5,4},{6,5},{7,6},{8,11},{9,8},{10,9... | collective-permute-start | bytes 1572872 | tf_op jit(solution)/shard_map/ppermute | solution.py:137
  82.6 1.9 %collective-permute-start.3 = (bf16[512,512]{1,0:T(8,128)(2,1)S(1)}, bf16[512,512]{1,0:T(8,128)(2,1)S(1)}, u32[]{:S(2)}, u32[]{:S(2)}) collective-permute-start(bf16[512,512]{1,0:T(8,128)(2,1)S(1)} %all_gather.6), channel_id=1, source_target_pairs={{0,1},{1,2},{2,3},{3,0},{4,5},{5,6},{6,7},{7,4},{8,9},{9,10},{10,1... | collective-permute-start | bytes 1572872 | tf_op jit(solution)/shard_map/ppermute | solution.py:137
  84.5 5.5 %collective-permute-done.1 = bf16[512,512]{1,0:T(8,128)(2,1)S(1)} collective-permute-done((bf16[512,512]{1,0:T(8,128)(2,1)S(1)}, bf16[512,512]{1,0:T(8,128)(2,1)S(1)}, u32[]{:S(2)}, u32[]{:S(2)}) %collective-permute-start.1) | collective-permute-done | bytes 524320 | tf_op jit(solution)/shard_map/ppermute | solution.py:137
  90.0 5.4 %collective-permute-start.2 = (bf16[256,512]{1,0:T(8,128)(2,1)S(1)}, bf16[256,512]{1,0:T(8,128)(2,1)S(1)}, u32[]{:S(2)}, u32[]{:S(2)}) collective-permute-start(bf16[256,512]{1,0:T(8,128)(2,1)S(1)} %slice.8), channel_id=1, source_target_pairs={{0,3},{1,0},{2,1},{3,2},{4,7},{5,4},{6,5},{7,6},{8,11},{9,8},{10,9... | collective-permute-start | bytes 786440 | tf_op jit(solution)/shard_map/ppermute | solution.py:137
  95.5 1.9 %collective-permute-start.4 = (bf16[256,512]{1,0:T(8,128)(2,1)S(1)}, bf16[256,512]{1,0:T(8,128)(2,1)S(1)}, u32[]{:S(2)}, u32[]{:S(2)}) collective-permute-start(bf16[256,512]{1,0:T(8,128)(2,1)S(1)} %slice.9), channel_id=1, source_target_pairs={{0,1},{1,2},{2,3},{3,0},{4,5},{5,6},{6,7},{7,4},{8,9},{9,10},{10,1... | collective-permute-start | bytes 786440 | tf_op jit(solution)/shard_map/ppermute | solution.py:137
  97.5 1.2 %collective-permute-done.2 = bf16[256,512]{1,0:T(8,128)(2,1)S(1)} collective-permute-done((bf16[256,512]{1,0:T(8,128)(2,1)S(1)}, bf16[256,512]{1,0:T(8,128)(2,1)S(1)}, u32[]{:S(2)}, u32[]{:S(2)}) %collective-permute-start.2) | collective-permute-done | bytes 262176 | tf_op jit(solution)/shard_map/ppermute | solution.py:137
  98.7 5.0 %collective-permute-done.4 = bf16[256,512]{1,0:T(8,128)(2,1)S(1)} collective-permute-done((bf16[256,512]{1,0:T(8,128)(2,1)S(1)}, bf16[256,512]{1,0:T(8,128)(2,1)S(1)}, u32[]{:S(2)}, u32[]{:S(2)}) %collective-permute-start.4) | collective-permute-done | bytes 262176 | tf_op jit(solution)/shard_map/ppermute | solution.py:137
  103.9 8.0 %collective-permute-start.5 = (bf16[4,512,512]{2,1,0:T(8,128)(2,1)}, bf16[4,512,512]{2,1,0:T(8,128)(2,1)}, u32[]{:S(2)}, u32[]{:S(2)}) collective-permute-start(bf16[4,512,512]{2,1,0:T(8,128)(2,1)} %all-to-all-done.1.cols_ref), channel_id=1, source_target_pairs={{0,16},{16,0},{1,17},{17,1},{2,18},{18,2},{3,19},{19,3},{4,20},{20... | collective-permute-start | bytes 6291464 | tf_op jit(solution)/shard_map/ppermute | solution.py:141
  111.8 0.1 add_add_fusion.s_ref
  111.9 0.1 add_add_fusion.1.s_ref
  112.0 4.4 %hessian_half.2.rest_0_ = f32[512,1024]{1,0:T(8,128)} custom-call(s32[3]{0:T(128)S(1)} %add_add_fusion.1.s_ref, bf16[2048,512]{1,0:T(8,128)(2,1)S(1)} %constant_dynamic-update-slice_fusion.rows_ref, bf16[4,512,512]{2,1,0:T(8,128)(2,1)} %all-to-all-done.1.cols_ref), custom_call_target="tpu_custom_call" | custom-call | tf_op jit(solution)/shard_map/hessian_half/pallas_call | solution.py:121
  116.4 4.4 %hessian_half.3 = f32[512,1024]{1,0:T(8,128)} custom-call(s32[3]{0:T(128)S(1)} %add_add_fusion.s_ref, bf16[2048,512]{1,0:T(8,128)(2,1)S(1)} %constant_dynamic-update-slice_fusion.rows_ref, bf16[4,512,512]{2,1,0:T(8,128)(2,1)} %collective-permute-done.5.cols_ref, f32[512,1024]{1,0:T(8,128)} %hessian_half.2.rest_0_), custom_call_target="tpu_custom_call", output_to_operand_aliasing={{}: (3, {})} | custom-call | tf_op jit(solution)/shard_map/hessian_half/pallas_call | solution.py:121
  (11 shorter events, 0.2 us)
Async XLA Ops:
  2.2 10.5 %all-to-all-start = ((bf16[4,272,128]{2,1,0:T(8,128)(2,1)}), bf16[4,272,128]{2,1,0:T(8,128)(2,1)S(1)}, u32[]{:S(2)}, u32[]{:S(2)}) async-start(bf16[4,272,128]{2,1,0:T(8,128)(2,1)} %pack.1), calls=%async_computation | async-start | bytes 557056 | tf_op jit(solution)/shard_map/all_to_all | solution.py:149
  14.5 33.0 %collective-permute-start = (bf16[128,512]{1,0:T(8,128)(2,1)}, bf16[128,512]{1,0:T(8,128)(2,1)S(1)}, u32[]{:S(2)}, u32[]{:S(2)}) collective-permute-start(bf16[128,512]{1,0:T(8,128)(2,1)} %attend.1), channel_id=1, source_target_pairs={{0,0},{1,32},{2,64},{3,96},{4,256},{5,288},{6,320},{7,352},{8,384}... | collective-permute-start | bytes 393224 | tf_op jit(solution)/shard_map/ppermute | solution.py:157
  69.2 34.7 %all-to-all-start.1 = ((bf16[4,512,512]{2,1,0:T(8,128)(2,1)}), bf16[4,512,512]{2,1,0:T(8,128)(2,1)}, u32[]{:S(2)}, u32[]{:S(2)}) async-start(bf16[4,512,512]{2,1,0:T(8,128)(2,1)} %broadcast_in_dim.2), calls=%async_computation.1 | async-start | bytes 4194304 | tf_op jit(solution)/shard_map/all_to_all | solution.py:149
  73.7 16.3 %collective-permute-start.1 = (bf16[512,512]{1,0:T(8,128)(2,1)S(1)}, bf16[512,512]{1,0:T(8,128)(2,1)S(1)}, u32[]{:S(2)}, u32[]{:S(2)}) collective-permute-start(bf16[512,512]{1,0:T(8,128)(2,1)S(1)} %all_gather.6), channel_id=1, source_target_pairs={{0,3},{1,0},{2,1},{3,2},{4,7},{5,4},{6,5},{7,6},{8,11},{9,8},{10,9... | collective-permute-start | bytes 1572872 | tf_op jit(solution)/shard_map/ppermute | solution.py:137
  82.6 12.8 %collective-permute-start.3 = (bf16[512,512]{1,0:T(8,128)(2,1)S(1)}, bf16[512,512]{1,0:T(8,128)(2,1)S(1)}, u32[]{:S(2)}, u32[]{:S(2)}) collective-permute-start(bf16[512,512]{1,0:T(8,128)(2,1)S(1)} %all_gather.6), channel_id=1, source_target_pairs={{0,1},{1,2},{2,3},{3,0},{4,5},{5,6},{6,7},{7,4},{8,9},{9,10},{10,1... | collective-permute-start | bytes 1572872 | tf_op jit(solution)/shard_map/ppermute | solution.py:137
  90.0 8.7 %collective-permute-start.2 = (bf16[256,512]{1,0:T(8,128)(2,1)S(1)}, bf16[256,512]{1,0:T(8,128)(2,1)S(1)}, u32[]{:S(2)}, u32[]{:S(2)}) collective-permute-start(bf16[256,512]{1,0:T(8,128)(2,1)S(1)} %slice.8), channel_id=1, source_target_pairs={{0,3},{1,0},{2,1},{3,2},{4,7},{5,4},{6,5},{7,6},{8,11},{9,8},{10,9... | collective-permute-start | bytes 786440 | tf_op jit(solution)/shard_map/ppermute | solution.py:137
  95.5 8.3 %collective-permute-start.4 = (bf16[256,512]{1,0:T(8,128)(2,1)S(1)}, bf16[256,512]{1,0:T(8,128)(2,1)S(1)}, u32[]{:S(2)}, u32[]{:S(2)}) collective-permute-start(bf16[256,512]{1,0:T(8,128)(2,1)S(1)} %slice.9), channel_id=1, source_target_pairs={{0,1},{1,2},{2,3},{3,0},{4,5},{5,6},{6,7},{7,4},{8,9},{9,10},{10,1... | collective-permute-start | bytes 786440 | tf_op jit(solution)/shard_map/ppermute | solution.py:137
  103.9 12.5 %collective-permute-start.5 = (bf16[4,512,512]{2,1,0:T(8,128)(2,1)}, bf16[4,512,512]{2,1,0:T(8,128)(2,1)}, u32[]{:S(2)}, u32[]{:S(2)}) collective-permute-start(bf16[4,512,512]{2,1,0:T(8,128)(2,1)} %all-to-all-done.1.cols_ref), channel_id=1, source_target_pairs={{0,16},{16,0},{1,17},{17,1},{2,18},{18,2},{3,19},{19,3},{4,20},{20... | collective-permute-start | bytes 6291464 | tf_op jit(solution)/shard_map/ppermute | solution.py:141

commit v6 on v5

--- a/solution.py
+++ b/solution.py
@@ -12,6 +12,7 @@
 KVH = 8
 HD = 128
 RING = 4
+STEPS = 2
 AXES = ("zl", "y", "core", "zh", "x")
 HEAD = ("zl", "y", "core")
 SEQ = ("zh", "x")
@@ -110,7 +111,7 @@
     half = cols.shape[2]
     whole = [
         pl.BlockSpec(rows.shape, lambda i, s: (0, 0)),
-        pl.BlockSpec(cols.shape, lambda i, s: (0, 0, 0)),
+        pl.BlockSpec((*cols.shape[:2], half // STEPS), lambda i, s: (0, 0, i)),
     ]
     args = [scalars, rows, cols]
     aliases = {}
@@ -123,9 +124,9 @@
         out_shape=jax.ShapeDtypeStruct((width, 2 * half), jnp.float32),
         grid_spec=pltpu.PrefetchScalarGridSpec(
             num_scalar_prefetch=1,
-            grid=(1,),
+            grid=(STEPS,),
             in_specs=whole,
-            out_specs=pl.BlockSpec((width, half), lambda i, s: (0, s[1])),
+            out_specs=pl.BlockSpec((width, half // STEPS), lambda i, s: (0, s[1] * STEPS + i)),
         ),
         input_output_aliases=aliases,
         compiler_params=pltpu.CompilerParams(vmem_limit_bytes=VMEM),
@@ -170,9 +171,9 @@
     rows = lax.all_gather(attended, "zh", axis=0, tiled=True)
     chunk, rows = lax.optimization_barrier((chunk, rows))
     cols = lax.all_gather(chunk, "zl", axis=0, tiled=True)
-    cols, rows = lax.optimization_barrier((cols, rows))
+    after, before = shift(rows, "x", -1), shift(rows, "x", 1)
+    cols, after, before = lax.optimization_barrier((cols, after, before))
     near_cols = exchange(copies(cols), "y")
-    after, before = shift(rows, "x", -1), shift(rows, "x", 1)
     cut = after.shape[0] // 2
     first, second = shift(after[:cut], "x", -1), shift(before[cut:], "x", 1)
     rows = jnp.concatenate([rows, after, first, second, before])

time: 121 us -> 122 us (level)
  starting transfers between devices: 37 us -> 29 us
  blocking collectives: 51.7 us -> 56.9 us
  waiting for transfers between devices: 15.4 us -> 18.7 us
    all_to_all x2, waiting for transfers between devices: 3.69 us -> 13.1 us  [exchange(): return lax.all_to_all(value, axis, split_axis=0, concat_axis=0, tiled=True)]
    ppermute x4, starting transfers between devices: 18.2 us -> 11.1 us  [shift(): lax.ppermute(value, axis, [(i, (i + by) % RING) for i in range(RING)])]
    ppermute x4, waiting for transfers between devices: 11.8 us -> 5.66 us  [shift(): lax.ppermute(value, axis, [(i, (i + by) % RING) for i in range(RING)])]
    all_gather x1, blocking collectives: 20.3 us -> 25.5 us  [on_device(): cols = lax.all_gather(chunk, 'zl', axis=0, tiled=True)]
  transfers between devices with their start and end apart: 8 -> 8, of which waited for: 4 -> 4; matrix products, arithmetic and copies ran while one was open for 2% -> 3% of each run, Pallas kernels for 4% -> 3%
where the time goes in v6:
time: 122 us
  blocking collectives  56.9 us (47%)
  starting transfers between devices  29 us (24%)
  waiting for transfers between devices  18.7 us (15%)
  Pallas kernels  11.6 us (10%)
  local copies, waits for them, and re-layouts  4.63 us (4%)
    all_gather x1, blocking collectives, on_device(): rows = lax.all_gather(attended, 'zh', axis=0, tiled=True)  31.4 us
    all_gather x1, blocking collectives, on_device(): cols = lax.all_gather(chunk, 'zl', axis=0, tiled=True)  25.5 us
    all_to_all x2, waiting for transfers between devices, exchange(): return lax.all_to_all(value, axis, split_axis=0, concat_axis=0, tiled=True)  13.1 us
    ppermute x4, starting transfers between devices, shift(): lax.ppermute(value, axis, [(i, (i + by) % RING) for i in range(RING)])  11.1 us
    all_to_all x2, starting transfers between devices, exchange(): return lax.all_to_all(value, axis, split_axis=0, concat_axis=0, tiled=True)  9.29 us
    pallas_call x2, Pallas kernels, hessian_half(): pl.pallas_call(half_kernel, out_shape=jax.ShapeDtypeStruct((width, 2 * ha...  8.21 us
    ppermute x1, starting transfers between devices, swap_cores(): return lax.ppermute(value, 'core', [(0, 1), (1, 0)])  7.04 us
    ppermute x4, waiting for transfers between devices, shift(): lax.ppermute(value, axis, [(i, (i + by) % RING) for i in range(RING)])  5.66 us
  transfers between devices with their start and end apart: 8, of which 4 were waited for; matrix products, arithmetic and copies ran while one was open for 3% of the time, Pallas kernels for 3%

profile of v6, /device:TPU:1, one launch (start us, length us, event | category | flops | bytes accessed | tf_op | source)
XLA Modules:
  0.0 121.8 jit_solution(13048515617830708418)
XLA Ops:
  0.7 1.5 %pack.1 = bf16[4,272,128]{2,1,0:T(8,128)(2,1)} custom-call(s32[1]{0:T(128)} %bitcast.2.g_ref, bf16[128,1024]{1,0:T(8,128)(2,1)} %k_ref.1, bf16[128,1024]{1,0:T(8,128)(2,1)} %v_ref.1, s32[1,128]{1,0:T(1,128)} %bitcast.11), custom_call_target="tpu_custom_call" | custom-call | tf_op jit(solution)/shard_map/pack/pallas_call | solution.py:37
  2.2 4.8 %all-to-all-start = ((bf16[4,272,128]{2,1,0:T(8,128)(2,1)}), bf16[4,272,128]{2,1,0:T(8,128)(2,1)S(1)}, u32[]{:S(2)}, u32[]{:S(2)}) async-start(bf16[4,272,128]{2,1,0:T(8,128)(2,1)} %pack.1), calls=%async_computation | async-start | bytes 557056 | tf_op jit(solution)/shard_map/all_to_all | solution.py:150
  7.0 1.0 copy.8
  8.0 0.1 copy.9
  8.2 0.8 copy.10.p_ref
  9.0 3.7 %all-to-all-done.kv_ref = bf16[4,272,128]{2,1,0:T(8,128)(2,1)S(1)} async-done(((bf16[4,272,128]{2,1,0:T(8,128)(2,1)}), bf16[4,272,128]{2,1,0:T(8,128)(2,1)S(1)}, u32[]{:S(2)}, u32[]{:S(2)}) %all-to-all-start) | async-done | bytes 278560 | tf_op jit(solution)/shard_map/all_to_all | solution.py:150
  12.6 1.8 %attend.1 = bf16[128,512]{1,0:T(8,128)(2,1)} custom-call(bf16[4,128,128]{2,1,0:T(8,128)(2,1)S(1)} %bitcast.9, bf16[4,272,128]{2,1,0:T(8,128)(2,1)S(1)} %all-to-all-done.kv_ref, s32[128,1]{1,0:T(8,128)S(1)} %copy.10.p_ref), custom_call_target="tpu_custom_call" | custom-call | tf_op jit(solution)/shard_map/attend/pallas_call | solution.py:81
  14.5 1.6 %collective-permute-start = (bf16[128,512]{1,0:T(8,128)(2,1)}, bf16[128,512]{1,0:T(8,128)(2,1)S(1)}, u32[]{:S(2)}, u32[]{:S(2)}) collective-permute-start(bf16[128,512]{1,0:T(8,128)(2,1)} %attend.1), channel_id=1, source_target_pairs={{0,0},{1,32},{2,64},{3,96},{4,256},{5,288},{6,320},{7,352},{8,384}... | collective-permute-start | bytes 393224 | tf_op jit(solution)/shard_map/ppermute | solution.py:158
  16.0 31.4 %all_gather.6 = bf16[512,512]{1,0:T(8,128)(2,1)S(1)} all-gather(bf16[128,512]{1,0:T(8,128)(2,1)} %attend.1), channel_id=1, replica_groups=mesh['zl'=4,'y'=4,'core'=2,'zh'=4,'x'=4] {'zh'}, dimensions={0}, use_global_device_ids=true | all-gather | bytes 655360 | tf_op jit(solution)/shard_map/all_gather | solution.py:171
  47.5 1.9 %collective-permute-start.1 = (bf16[512,512]{1,0:T(8,128)(2,1)S(1)}, bf16[512,512]{1,0:T(8,128)(2,1)S(1)}, u32[]{:S(2)}, u32[]{:S(2)}) collective-permute-start(bf16[512,512]{1,0:T(8,128)(2,1)S(1)} %all_gather.6), channel_id=1, source_target_pairs={{0,3},{1,0},{2,1},{3,2},{4,7},{5,4},{6,5},{7,6},{8,11},{9,8},{10,9... | collective-permute-start | bytes 1572872 | tf_op jit(solution)/shard_map/ppermute | solution.py:138
  49.4 3.4 %collective-permute-start.2 = (bf16[512,512]{1,0:T(8,128)(2,1)S(1)}, bf16[512,512]{1,0:T(8,128)(2,1)S(1)}, u32[]{:S(2)}, u32[]{:S(2)}) collective-permute-start(bf16[512,512]{1,0:T(8,128)(2,1)S(1)} %all_gather.6), channel_id=1, source_target_pairs={{0,1},{1,2},{2,3},{3,0},{4,5},{5,6},{6,7},{7,4},{8,9},{9,10},{10,1... | collective-permute-start | bytes 1572872 | tf_op jit(solution)/shard_map/ppermute | solution.py:138
  52.7 25.5 %all_gather.7 = bf16[512,512]{1,0:T(8,128)(2,1)S(1)} all-gather(bf16[128,512]{1,0:T(8,128)(2,1)S(1)} %collective-permute-done), channel_id=1, replica_groups=mesh['zl'=4,'y'=4,'core'=2,'zh'=4,'x'=4] {'zl'}, dimensions={0}, use_global_device_ids=true | all-gather | bytes 655360 | tf_op jit(solution)/shard_map/all_gather | solution.py:173
  78.2 1.5 %broadcast_in_dim.2 = bf16[4,512,512]{2,1,0:T(8,128)(2,1)} broadcast(bf16[512,512]{1,0:T(8,128)(2,1)S(1)} %all_gather.7), dimensions={1,2} | broadcast | bytes 2621440 | tf_op jit(solution)/shard_map/broadcast_in_dim | solution.py:146
  79.7 4.4 %all-to-all-start.1 = ((bf16[4,512,512]{2,1,0:T(8,128)(2,1)}), bf16[4,512,512]{2,1,0:T(8,128)(2,1)}, u32[]{:S(2)}, u32[]{:S(2)}) async-start(bf16[4,512,512]{2,1,0:T(8,128)(2,1)} %broadcast_in_dim.2), calls=%async_computation.1 | async-start | bytes 4194304 | tf_op jit(solution)/shard_map/all_to_all | solution.py:150
  84.2 3.9 %collective-permute-start.3 = (bf16[256,512]{1,0:T(8,128)(2,1)S(1)}, bf16[256,512]{1,0:T(8,128)(2,1)S(1)}, u32[]{:S(2)}, u32[]{:S(2)}) collective-permute-start(bf16[256,512]{1,0:T(8,128)(2,1)S(1)} %slice.6), channel_id=1, source_target_pairs={{0,3},{1,0},{2,1},{3,2},{4,7},{5,4},{6,5},{7,6},{8,11},{9,8},{10,9... | collective-permute-start | bytes 786440 | tf_op jit(solution)/shard_map/ppermute | solution.py:138
  88.2 1.9 %collective-permute-start.4 = (bf16[256,512]{1,0:T(8,128)(2,1)S(1)}, bf16[256,512]{1,0:T(8,128)(2,1)S(1)}, u32[]{:S(2)}, u32[]{:S(2)}) collective-permute-start(bf16[256,512]{1,0:T(8,128)(2,1)S(1)} %slice.7), channel_id=1, source_target_pairs={{0,1},{1,2},{2,3},{3,0},{4,5},{5,6},{6,7},{7,4},{8,9},{9,10},{10,1... | collective-permute-start | bytes 786440 | tf_op jit(solution)/shard_map/ppermute | solution.py:138
  90.2 1.1 constant_dynamic-update-slice_fusion.3
  91.2 0.2 collective-permute-done.3
  91.5 5.4 %collective-permute-done.4 = bf16[256,512]{1,0:T(8,128)(2,1)S(1)} collective-permute-done((bf16[256,512]{1,0:T(8,128)(2,1)S(1)}, bf16[256,512]{1,0:T(8,128)(2,1)S(1)}, u32[]{:S(2)}, u32[]{:S(2)}) %collective-permute-start.4) | collective-permute-done | bytes 262176 | tf_op jit(solution)/shard_map/ppermute | solution.py:138
  97.0 9.4 %all-to-all-done.1.cols_ref = bf16[4,512,512]{2,1,0:T(8,128)(2,1)} async-done(((bf16[4,512,512]{2,1,0:T(8,128)(2,1)}), bf16[4,512,512]{2,1,0:T(8,128)(2,1)}, u32[]{:S(2)}, u32[]{:S(2)}) %all-to-all-start.1) | async-done | bytes 2097184 | tf_op jit(solution)/shard_map/all_to_all | solution.py:150
  106.4 7.0 %collective-permute-start.5 = (bf16[4,512,512]{2,1,0:T(8,128)(2,1)}, bf16[4,512,512]{2,1,0:T(8,128)(2,1)}, u32[]{:S(2)}, u32[]{:S(2)}) collective-permute-start(bf16[4,512,512]{2,1,0:T(8,128)(2,1)} %all-to-all-done.1.cols_ref), channel_id=1, source_target_pairs={{0,16},{16,0},{1,17},{17,1},{2,18},{18,2},{3,19},{19,3},{4,20},{20... | collective-permute-start | bytes 6291464 | tf_op jit(solution)/shard_map/ppermute | solution.py:142
  113.4 0.1 add_add_fusion.s_ref
  113.6 4.1 %hessian_half.2.rest_0_ = f32[512,1024]{1,0:T(8,128)} custom-call(s32[3]{0:T(128)S(1)} %add_add_fusion.1.s_ref, bf16[2048,512]{1,0:T(8,128)(2,1)S(1)} %constant_dynamic-update-slice_fusion.rows_ref, bf16[4,512,512]{2,1,0:T(8,128)(2,1)} %all-to-all-done.1.cols_ref), custom_call_target="tpu_custom_call" | custom-call | tf_op jit(solution)/shard_map/hessian_half/pallas_call | solution.py:122
  117.7 4.1 %hessian_half.3 = f32[512,1024]{1,0:T(8,128)} custom-call(s32[3]{0:T(128)S(1)} %add_add_fusion.s_ref, bf16[2048,512]{1,0:T(8,128)(2,1)S(1)} %constant_dynamic-update-slice_fusion.rows_ref, bf16[4,512,512]{2,1,0:T(8,128)(2,1)} %collective-permute-done.5.cols_ref, f32[512,1024]{1,0:T(8,128)} %hessian_half.2.rest_0_), custom_call_target="tpu_custom_call", output_to_operand_aliasing={{}: (3, {})} | custom-call | tf_op jit(solution)/shard_map/hessian_half/pallas_call | solution.py:122
  (13 shorter events, 0.2 us)
Async XLA Ops:
  2.2 10.5 %all-to-all-start = ((bf16[4,272,128]{2,1,0:T(8,128)(2,1)}), bf16[4,272,128]{2,1,0:T(8,128)(2,1)S(1)}, u32[]{:S(2)}, u32[]{:S(2)}) async-start(bf16[4,272,128]{2,1,0:T(8,128)(2,1)} %pack.1), calls=%async_computation | async-start | bytes 557056 | tf_op jit(solution)/shard_map/all_to_all | solution.py:150
  14.5 33.0 %collective-permute-start = (bf16[128,512]{1,0:T(8,128)(2,1)}, bf16[128,512]{1,0:T(8,128)(2,1)S(1)}, u32[]{:S(2)}, u32[]{:S(2)}) collective-permute-start(bf16[128,512]{1,0:T(8,128)(2,1)} %attend.1), channel_id=1, source_target_pairs={{0,0},{1,32},{2,64},{3,96},{4,256},{5,288},{6,320},{7,352},{8,384}... | collective-permute-start | bytes 393224 | tf_op jit(solution)/shard_map/ppermute | solution.py:158
  47.5 30.8 %collective-permute-start.1 = (bf16[512,512]{1,0:T(8,128)(2,1)S(1)}, bf16[512,512]{1,0:T(8,128)(2,1)S(1)}, u32[]{:S(2)}, u32[]{:S(2)}) collective-permute-start(bf16[512,512]{1,0:T(8,128)(2,1)S(1)} %all_gather.6), channel_id=1, source_target_pairs={{0,3},{1,0},{2,1},{3,2},{4,7},{5,4},{6,5},{7,6},{8,11},{9,8},{10,9... | collective-permute-start | bytes 1572872 | tf_op jit(solution)/shard_map/ppermute | solution.py:138
  49.4 28.9 %collective-permute-start.2 = (bf16[512,512]{1,0:T(8,128)(2,1)S(1)}, bf16[512,512]{1,0:T(8,128)(2,1)S(1)}, u32[]{:S(2)}, u32[]{:S(2)}) collective-permute-start(bf16[512,512]{1,0:T(8,128)(2,1)S(1)} %all_gather.6), channel_id=1, source_target_pairs={{0,1},{1,2},{2,3},{3,0},{4,5},{5,6},{6,7},{7,4},{8,9},{9,10},{10,1... | collective-permute-start | bytes 1572872 | tf_op jit(solution)/shard_map/ppermute | solution.py:138
  78.2 5.9 %copy-start = (bf16[512,512]{1,0:T(8,128)(2,1)}, bf16[512,512]{1,0:T(8,128)(2,1)S(1)}, u32[]{:S(2)}) copy-start(bf16[512,512]{1,0:T(8,128)(2,1)S(1)} %collective-permute-done.1) | copy-start | bytes 1572868
  79.7 26.7 %all-to-all-start.1 = ((bf16[4,512,512]{2,1,0:T(8,128)(2,1)}), bf16[4,512,512]{2,1,0:T(8,128)(2,1)}, u32[]{:S(2)}, u32[]{:S(2)}) async-start(bf16[4,512,512]{2,1,0:T(8,128)(2,1)} %broadcast_in_dim.2), calls=%async_computation.1 | async-start | bytes 4194304 | tf_op jit(solution)/shard_map/all_to_all | solution.py:150
  84.2 7.3 %collective-permute-start.3 = (bf16[256,512]{1,0:T(8,128)(2,1)S(1)}, bf16[256,512]{1,0:T(8,128)(2,1)S(1)}, u32[]{:S(2)}, u32[]{:S(2)}) collective-permute-start(bf16[256,512]{1,0:T(8,128)(2,1)S(1)} %slice.6), channel_id=1, source_target_pairs={{0,3},{1,0},{2,1},{3,2},{4,7},{5,4},{6,5},{7,6},{8,11},{9,8},{10,9... | collective-permute-start | bytes 786440 | tf_op jit(solution)/shard_map/ppermute | solution.py:138
  88.2 8.7 %collective-permute-start.4 = (bf16[256,512]{1,0:T(8,128)(2,1)S(1)}, bf16[256,512]{1,0:T(8,128)(2,1)S(1)}, u32[]{:S(2)}, u32[]{:S(2)}) collective-permute-start(bf16[256,512]{1,0:T(8,128)(2,1)S(1)} %slice.7), channel_id=1, source_target_pairs={{0,1},{1,2},{2,3},{3,0},{4,5},{5,6},{6,7},{7,4},{8,9},{9,10},{10,1... | collective-permute-start | bytes 786440 | tf_op jit(solution)/shard_map/ppermute | solution.py:138
  106.4 11.3 %collective-permute-start.5 = (bf16[4,512,512]{2,1,0:T(8,128)(2,1)}, bf16[4,512,512]{2,1,0:T(8,128)(2,1)}, u32[]{:S(2)}, u32[]{:S(2)}) collective-permute-start(bf16[4,512,512]{2,1,0:T(8,128)(2,1)} %all-to-all-done.1.cols_ref), channel_id=1, source_target_pairs={{0,16},{16,0},{1,17},{17,1},{2,18},{18,2},{3,19},{19,3},{4,20},{20... | collective-permute-start | bytes 6291464 | tf_op jit(solution)/shard_map/ppermute | solution.py:142

commit v7 on v6

--- a/solution.py
+++ b/solution.py
@@ -87,55 +87,71 @@
 
 
 LANDING = ((0, 2, 3, 1), (2, 1, 3, 0), (3, 0, 2, 1), (2, 0, 1, 3))
+TAKEN = tuple(tuple(line.index(k) for k in range(RING)) for line in LANDING)
 CONTRACT = (((0,), (0,)), ((), ()))
 
 
-def half_kernel(s_ref, rows_ref, cols_ref, *rest):
-    o_ref = rest[-1]
-    x, zh = s_ref[0], s_ref[2]
-    tok = cols_ref.shape[1] // RING
-    blocks = []
-    for d in range(RING):
-        for span in range(RING):
-            place = jnp.int32(LANDING[0][span])
-            for group in range(1, RING):
-                place = jnp.where(zh == group, LANDING[group][span], place)
-            part = pl.ds(pl.multiple_of(place * tok, tok), tok)
-            blocks.append(cols_ref[(x + d) & (RING - 1), part])
-    cols = jnp.concatenate(blocks, axis=0)
-    o_ref[...] = lax.dot_general(rows_ref[...], cols, CONTRACT, preferred_element_type=jnp.float32)
-
-
-def hessian_half(scalars, rows, cols, filled=None):
-    width = rows.shape[1]
-    half = cols.shape[2]
-    whole = [
-        pl.BlockSpec(rows.shape, lambda i, s: (0, 0)),
-        pl.BlockSpec((*cols.shape[:2], half // STEPS), lambda i, s: (0, 0, i)),
-    ]
-    args = [scalars, rows, cols]
-    aliases = {}
-    if filled is not None:
-        aliases = {len(args): 0}
-        whole.append(pl.BlockSpec(memory_space=pl.ANY))
-        args.append(filled)
-    return pl.pallas_call(
-        half_kernel,
+def ordered_kernel(s_ref, v_ref, o_ref):
+    for copy in range(RING):
+        o_ref[copy] = v_ref[...]
+
+
+def ordered_copies(order, value):
+    depth, width = value.shape
+    part = depth // RING
+    return pl.pallas_call(
+        ordered_kernel,
+        out_shape=jax.ShapeDtypeStruct((RING, depth, width), value.dtype),
+        grid_spec=pltpu.PrefetchScalarGridSpec(
+            num_scalar_prefetch=1,
+            grid=(RING,),
+            in_specs=[pl.BlockSpec((part, width), lambda i, s: (s[i], 0))],
+            out_specs=pl.BlockSpec((RING, part, width), lambda i, s: (0, i, 0)),
+        ),
+        name="ordered_copies",
+    )(order, value)
+
+
+def hessian_kernel(s_ref, rows_ref, near_ref, far_ref, o_ref):
+    step = pl.program_id(0)
+
+    def product(cols_ref):
+        cols = cols_ref[...].reshape(rows_ref.shape[0], cols_ref.shape[2])
+        o_ref[...] = lax.dot_general(
+            rows_ref[...], cols, CONTRACT, preferred_element_type=jnp.float32
+        )
+
+    @pl.when(step < STEPS)
+    def _():
+        product(near_ref)
+
+    @pl.when(step >= STEPS)
+    def _():
+        product(far_ref)
+
+
+def hessian_of(core, rows, near, far):
+    depth, width = rows.shape
+    ring, part, half = near.shape
+    block = (ring, part, half // STEPS)
+    return pl.pallas_call(
+        hessian_kernel,
         out_shape=jax.ShapeDtypeStruct((width, 2 * half), jnp.float32),
         grid_spec=pltpu.PrefetchScalarGridSpec(
             num_scalar_prefetch=1,
-            grid=(STEPS,),
-            in_specs=whole,
-            out_specs=pl.BlockSpec((width, half // STEPS), lambda i, s: (0, s[1] * STEPS + i)),
+            grid=(2 * STEPS,),
+            in_specs=[
+                pl.BlockSpec((depth, width), lambda i, s: (0, 0)),
+                pl.BlockSpec(block, lambda i, s: (0, 0, jnp.minimum(i, STEPS - 1))),
+                pl.BlockSpec(block, lambda i, s: (0, 0, jnp.maximum(i - STEPS, 0))),
+            ],
+            out_specs=pl.BlockSpec(
+                (width, half // STEPS), lambda i, s: (0, (i + s[0] * STEPS) % (2 * STEPS))
+            ),
         ),
-        input_output_aliases=aliases,
         compiler_params=pltpu.CompilerParams(vmem_limit_bytes=VMEM),
-        name="hessian_half",
-    )(*args)
-
-
-def shift(value, axis, by):
-    return lax.ppermute(value, axis, [(i, (i + by) % RING) for i in range(RING)])
+        name="hessian",
+    )(core, rows, near, far)
 
 
 def swap_cores(value):
@@ -168,22 +184,16 @@
     queries = jnp.transpose(query_rows.reshape(tok, local_heads, HD), (1, 0, 2))
     attended = attend(queries, gathered, positions)
     chunk = swap(attended)
-    rows = lax.all_gather(attended, "zh", axis=0, tiled=True)
-    chunk, rows = lax.optimization_barrier((chunk, rows))
     cols = lax.all_gather(chunk, "zl", axis=0, tiled=True)
-    after, before = shift(rows, "x", -1), shift(rows, "x", 1)
-    cols, after, before = lax.optimization_barrier((cols, after, before))
-    near_cols = exchange(copies(cols), "y")
-    cut = after.shape[0] // 2
-    first, second = shift(after[:cut], "x", -1), shift(before[cut:], "x", 1)
-    rows = jnp.concatenate([rows, after, first, second, before])
-    near_cols, rows = lax.optimization_barrier((near_cols, rows))
-    far_cols = swap_cores(near_cols)
-    place = lax.axis_index("x"), lax.axis_index("core"), lax.axis_index("zh")
-    near = jnp.stack(place).astype(jnp.int32)
-    far = jnp.stack((place[0], 1 - place[1], place[2])).astype(jnp.int32)
-    hessian = hessian_half(near, rows, near_cols)
-    hessian = hessian_half(far, rows, far_cols, hessian)
+    cols, mine = lax.optimization_barrier((cols, attended))
+    near = exchange(copies(cols), "y")
+    rows = lax.all_gather(mine, "zh", axis=0, tiled=True)
+    order = jnp.asarray(TAKEN, jnp.int32)[lax.axis_index("zh")]
+    near, rows = lax.optimization_barrier((near, ordered_copies(order, rows)))
+    rows = exchange(rows, "x")
+    far = swap_cores(near)
+    core = lax.axis_index("core").astype(jnp.int32).reshape(1)
+    hessian = hessian_of(core, rows.reshape(-1, rows.shape[2]), near, far)
     return attended, hessian
 
 

time: 122 us -> 132 us (1.082)
  blocking collectives: 56.9 us -> 89.2 us
  waiting for transfers between devices: 18.7 us -> 3.7 us
  starting transfers between devices: 29 us -> 21.5 us
    all_to_all x0 -> x1, blocking collectives: none -> 29.8 us  [exchange(): return lax.all_to_all(value, axis, split_axis=0, concat_axis=0, tiled=True)]
    ppermute x4 -> x0, starting transfers between devices: 11.1 us -> none  [shift(): lax.ppermute(value, axis, [(i, (i + by) % RING) for i in range(RING)])]
    all_to_all x2, waiting for transfers between devices: 13.1 us -> 3.69 us  [exchange(): return lax.all_to_all(value, axis, split_axis=0, concat_axis=0, tiled=True)]
    ppermute x4 -> x0, waiting for transfers between devices: 5.66 us -> none  [shift(): lax.ppermute(value, axis, [(i, (i + by) % RING) for i in range(RING)])]
    all_gather x1, blocking collectives: 25.5 us -> 28.2 us  [on_device(): cols = lax.all_gather(chunk, 'zl', axis=0, tiled=True)]
    all_to_all x2, starting transfers between devices: 9.29 us -> 11.9 us  [exchange(): return lax.all_to_all(value, axis, split_axis=0, concat_axis=0, tiled=True)]
  transfers between devices with their start and end apart: 8 -> 4, of which waited for: 4 -> 1; matrix products, arithmetic and copies ran while one was open for 3% -> 2% of each run, Pallas kernels for 3% -> 3%
where the time goes in v7:
time: 132 us
  blocking collectives  89.2 us (68%)
  starting transfers between devices  21.5 us (16%)
  Pallas kernels  11.8 us (9%)
  local copies, waits for them, and re-layouts  4.7 us (4%)
  waiting for transfers between devices  3.7 us (3%)
    all_gather x1, blocking collectives, on_device(): rows = lax.all_gather(mine, 'zh', axis=0, tiled=True)  31.2 us
    all_to_all x1, blocking collectives, exchange(): return lax.all_to_all(value, axis, split_axis=0, concat_axis=0, tiled=True)  29.8 us
    all_gather x1, blocking collectives, on_device(): cols = lax.all_gather(chunk, 'zl', axis=0, tiled=True)  28.2 us
    all_to_all x2, starting transfers between devices, exchange(): return lax.all_to_all(value, axis, split_axis=0, concat_axis=0, tiled=True)  11.9 us
    ppermute x1, starting transfers between devices, swap_cores(): return lax.ppermute(value, 'core', [(0, 1), (1, 0)])  8.03 us
    pallas_call x1, Pallas kernels, hessian_of(): pl.pallas_call(hessian_kernel, out_shape=jax.ShapeDtypeStruct((width, 2 *...  4.3 us
    pallas_call x1, Pallas kernels, ordered_copies(): pl.pallas_call(ordered_kernel, out_shape=jax.ShapeDtypeStruct((RING, dept...  4.15 us
    all_to_all x2, waiting for transfers between devices, exchange(): return lax.all_to_all(value, axis, split_axis=0, concat_axis=0, tiled=True)  3.69 us
  transfers between devices with their start and end apart: 4, of which 1 were waited for; matrix products, arithmetic and copies ran while one was open for 2% of the time, Pallas kernels for 3%

profile of v7, /device:TPU:1, one launch (start us, length us, event | category | flops | bytes accessed | tf_op | source)
XLA Modules:
  0.0 131.6 jit_solution(4046757514592102508)
XLA Ops:
  0.7 1.5 %pack.1 = bf16[4,272,128]{2,1,0:T(8,128)(2,1)} custom-call(s32[1]{0:T(128)} %bitcast.2.g_ref, bf16[128,1024]{1,0:T(8,128)(2,1)} %k_ref.1, bf16[128,1024]{1,0:T(8,128)(2,1)} %v_ref.1, s32[1,128]{1,0:T(1,128)} %bitcast.12), custom_call_target="tpu_custom_call" | custom-call | tf_op jit(solution)/shard_map/pack/pallas_call | solution.py:37
  2.2 4.8 %all-to-all-start = ((bf16[4,272,128]{2,1,0:T(8,128)(2,1)}), bf16[4,272,128]{2,1,0:T(8,128)(2,1)S(1)}, u32[]{:S(2)}, u32[]{:S(2)}) async-start(bf16[4,272,128]{2,1,0:T(8,128)(2,1)} %pack.1), calls=%async_computation | async-start | bytes 557056 | tf_op jit(solution)/shard_map/all_to_all | solution.py:166
  7.0 0.8 copy.10.p_ref
  7.8 1.0 copy.8
  8.8 0.1 copy.9
  8.9 3.7 %all-to-all-done.kv_ref = bf16[4,272,128]{2,1,0:T(8,128)(2,1)S(1)} async-done(((bf16[4,272,128]{2,1,0:T(8,128)(2,1)}), bf16[4,272,128]{2,1,0:T(8,128)(2,1)S(1)}, u32[]{:S(2)}, u32[]{:S(2)}) %all-to-all-start) | async-done | bytes 278560 | tf_op jit(solution)/shard_map/all_to_all | solution.py:166
  12.6 1.9 %attend.1 = bf16[128,512]{1,0:T(8,128)(2,1)} custom-call(bf16[4,128,128]{2,1,0:T(8,128)(2,1)S(1)} %bitcast.10, bf16[4,272,128]{2,1,0:T(8,128)(2,1)S(1)} %all-to-all-done.kv_ref, s32[128,1]{1,0:T(8,128)S(1)} %copy.10.p_ref), custom_call_target="tpu_custom_call" | custom-call | tf_op jit(solution)/shard_map/attend/pallas_call | solution.py:81
  14.5 1.6 %collective-permute-start = (bf16[128,512]{1,0:T(8,128)(2,1)}, bf16[128,512]{1,0:T(8,128)(2,1)S(1)}, u32[]{:S(2)}, u32[]{:S(2)}) collective-permute-start(bf16[128,512]{1,0:T(8,128)(2,1)} %attend.1), channel_id=1, source_target_pairs={{0,0},{1,32},{2,64},{3,96},{4,256},{5,288},{6,320},{7,352},{8,384}... | collective-permute-start | bytes 393224 | tf_op jit(solution)/shard_map/ppermute | solution.py:174
  16.0 0.0 collective-permute-done
  16.0 28.2 %all_gather.6 = bf16[512,512]{1,0:T(8,128)(2,1)S(1)} all-gather(bf16[128,512]{1,0:T(8,128)(2,1)S(1)} %collective-permute-done), channel_id=1, replica_groups=mesh['zl'=4,'y'=4,'core'=2,'zh'=4,'x'=4] {'zl'}, dimensions={0}, use_global_device_ids=true | all-gather | bytes 655360 | tf_op jit(solution)/shard_map/all_gather | solution.py:187
  44.3 1.5 %broadcast_in_dim.2 = bf16[4,512,512]{2,1,0:T(8,128)(2,1)} broadcast(bf16[512,512]{1,0:T(8,128)(2,1)S(1)} %all_gather.6), dimensions={1,2} | broadcast | bytes 2621440 | tf_op jit(solution)/shard_map/broadcast_in_dim | solution.py:162
  45.8 0.0 copy-start
  45.8 7.1 %all-to-all-start.1 = ((bf16[4,512,512]{2,1,0:T(8,128)(2,1)}), bf16[4,512,512]{2,1,0:T(8,128)(2,1)S(1)}, u32[]{:S(2)}, u32[]{:S(2)}) async-start(bf16[4,512,512]{2,1,0:T(8,128)(2,1)} %broadcast_in_dim.2), calls=%async_computation.1 | async-start | bytes 4194304 | tf_op jit(solution)/shard_map/all_to_all | solution.py:166
  52.9 1.3 dynamic-slice_bitcast_fusion.s_ref
  54.1 0.0 copy-done
  54.1 31.2 %all_gather.7.v_ref = bf16[512,512]{1,0:T(8,128)(2,1)} all-gather(bf16[128,512]{1,0:T(8,128)(2,1)S(1)} %copy-done), channel_id=1, replica_groups=mesh['zl'=4,'y'=4,'core'=2,'zh'=4,'x'=4] {'zh'}, dimensions={0}, use_global_device_ids=true | all-gather | bytes 655360 | tf_op jit(solution)/shard_map/all_gather | solution.py:190
  85.3 4.2 %ordered_copies.1 = bf16[4,512,512]{2,1,0:T(8,128)(2,1)} custom-call(s32[4]{0:T(128)} %dynamic-slice_bitcast_fusion.s_ref, bf16[512,512]{1,0:T(8,128)(2,1)} %all_gather.7.v_ref), custom_call_target="tpu_custom_call" | custom-call | tf_op jit(solution)/shard_map/ordered_copies/pallas_call | solution.py:102
  89.5 0.0 all-to-all-done.1.near_ref
  89.5 8.0 %collective-permute-start.1 = (bf16[4,512,512]{2,1,0:T(8,128)(2,1)S(1)}, bf16[4,512,512]{2,1,0:T(8,128)(2,1)S(1)}, u32[]{:S(2)}, u32[]{:S(2)}) collective-permute-start(bf16[4,512,512]{2,1,0:T(8,128)(2,1)S(1)} %all-to-all-done.1.near_ref), channel_id=1, source_target_pairs={{0,16},{16,0},{1,17},{17,1},{2,18},{18,2},{3,19},{19,3},{4,20},{20... | collective-permute-start | bytes 6291464 | tf_op jit(solution)/shard_map/ppermute | solution.py:158
  97.5 29.8 %all_to_all.15 = bf16[4,512,512]{2,1,0:T(8,128)(2,1)S(1)} all-to-all(bf16[4,512,512]{2,1,0:T(8,128)(2,1)} %ordered_copies.1), channel_id=1, replica_groups=mesh['zl'=4,'y'=4,'core'=2,'zh'=4,'x'=4] {'x'}, dimensions={0} | all-to-all | bytes 4194304 | tf_op jit(solution)/shard_map/all_to_all | solution.py:166
  127.3 0.0 collective-permute-done.1.far_ref
  127.3 4.3 %hessian.1 = f32[512,1024]{1,0:T(8,128)} custom-call(s32[1]{0:T(128)} %bitcast.5.s_ref, bf16[2048,512]{1,0:T(8,128)(2,1)S(1)} %bitcast.9, bf16[4,512,512]{2,1,0:T(8,128)(2,1)S(1)} %all-to-all-done.1.near_ref, bf16[4,512,512]{2,1,0:T(8,128)(2,1)S(1)} %collective-permute-done.1.far_ref), custom_call_target="tpu_custom_call" | custom-call | tf_op jit(solution)/shard_map/hessian/pallas_call | solution.py:137
Async XLA Ops:
  2.2 10.5 %all-to-all-start = ((bf16[4,272,128]{2,1,0:T(8,128)(2,1)}), bf16[4,272,128]{2,1,0:T(8,128)(2,1)S(1)}, u32[]{:S(2)}, u32[]{:S(2)}) async-start(bf16[4,272,128]{2,1,0:T(8,128)(2,1)} %pack.1), calls=%async_computation | async-start | bytes 557056 | tf_op jit(solution)/shard_map/all_to_all | solution.py:166
  14.5 1.6 %collective-permute-start = (bf16[128,512]{1,0:T(8,128)(2,1)}, bf16[128,512]{1,0:T(8,128)(2,1)S(1)}, u32[]{:S(2)}, u32[]{:S(2)}) collective-permute-start(bf16[128,512]{1,0:T(8,128)(2,1)} %attend.1), channel_id=1, source_target_pairs={{0,0},{1,32},{2,64},{3,96},{4,256},{5,288},{6,320},{7,352},{8,384}... | collective-permute-start | bytes 393224 | tf_op jit(solution)/shard_map/ppermute | solution.py:174
  45.8 8.3 %copy-start = (bf16[128,512]{1,0:T(8,128)(2,1)S(1)}, bf16[128,512]{1,0:T(8,128)(2,1)}, u32[]{:S(2)}) copy-start(bf16[128,512]{1,0:T(8,128)(2,1)} %attend.1) | copy-start | bytes 393220
  45.8 43.7 %all-to-all-start.1 = ((bf16[4,512,512]{2,1,0:T(8,128)(2,1)}), bf16[4,512,512]{2,1,0:T(8,128)(2,1)S(1)}, u32[]{:S(2)}, u32[]{:S(2)}) async-start(bf16[4,512,512]{2,1,0:T(8,128)(2,1)} %broadcast_in_dim.2), calls=%async_computation.1 | async-start | bytes 4194304 | tf_op jit(solution)/shard_map/all_to_all | solution.py:166
  89.5 37.8 %collective-permute-start.1 = (bf16[4,512,512]{2,1,0:T(8,128)(2,1)S(1)}, bf16[4,512,512]{2,1,0:T(8,128)(2,1)S(1)}, u32[]{:S(2)}, u32[]{:S(2)}) collective-permute-start(bf16[4,512,512]{2,1,0:T(8,128)(2,1)S(1)} %all-to-all-done.1.near_ref), channel_id=1, source_target_pairs={{0,16},{16,0},{1,17},{17,1},{2,18},{18,2},{3,19},{19,3},{4,20},{20... | collective-permute-start | bytes 6291464 | tf_op jit(solution)/shard_map/ppermute | solution.py:158

commit v8 on v6

--- a/solution.py
+++ b/solution.py
@@ -86,38 +86,29 @@
     )(queries, gathered, positions.reshape(tok, 1))
 
 
-LANDING = ((0, 2, 3, 1), (2, 1, 3, 0), (3, 0, 2, 1), (2, 0, 1, 3))
+LANDING = ((0, 2, 3, 1), (1, 3, 2, 0), (3, 1, 0, 2), (2, 0, 1, 3))
 CONTRACT = (((0,), (0,)), ((), ()))
 
 
 def half_kernel(s_ref, rows_ref, cols_ref, *rest):
     o_ref = rest[-1]
-    x, zh = s_ref[0], s_ref[2]
-    tok = cols_ref.shape[1] // RING
-    blocks = []
-    for d in range(RING):
-        for span in range(RING):
-            place = jnp.int32(LANDING[0][span])
-            for group in range(1, RING):
-                place = jnp.where(zh == group, LANDING[group][span], place)
-            part = pl.ds(pl.multiple_of(place * tok, tok), tok)
-            blocks.append(cols_ref[(x + d) & (RING - 1), part])
-    cols = jnp.concatenate(blocks, axis=0)
-    o_ref[...] = lax.dot_general(rows_ref[...], cols, CONTRACT, preferred_element_type=jnp.float32)
-
-
-def hessian_half(scalars, rows, cols, filled=None):
-    width = rows.shape[1]
-    half = cols.shape[2]
-    whole = [
-        pl.BlockSpec(rows.shape, lambda i, s: (0, 0)),
-        pl.BlockSpec((*cols.shape[:2], half // STEPS), lambda i, s: (0, 0, i)),
+    o_ref[...] = lax.dot_general(
+        rows_ref[...], cols_ref[...], CONTRACT, preferred_element_type=jnp.float32
+    )
+
+
+def hessian_half(place, rows, cols, filled=None):
+    depth, width = rows.shape
+    half = cols.shape[1]
+    specs = [
+        pl.BlockSpec((depth, width), lambda i, s: (0, 0)),
+        pl.BlockSpec((depth, half // STEPS), lambda i, s: (0, i)),
     ]
-    args = [scalars, rows, cols]
+    args = [place, rows, cols]
     aliases = {}
     if filled is not None:
         aliases = {len(args): 0}
-        whole.append(pl.BlockSpec(memory_space=pl.ANY))
+        specs.append(pl.BlockSpec(memory_space=pl.ANY))
         args.append(filled)
     return pl.pallas_call(
         half_kernel,
@@ -125,8 +116,8 @@
         grid_spec=pltpu.PrefetchScalarGridSpec(
             num_scalar_prefetch=1,
             grid=(STEPS,),
-            in_specs=whole,
-            out_specs=pl.BlockSpec((width, half // STEPS), lambda i, s: (0, s[1] * STEPS + i)),
+            in_specs=specs,
+            out_specs=pl.BlockSpec((width, half // STEPS), lambda i, s: (0, s[0] * STEPS + i)),
         ),
         input_output_aliases=aliases,
         compiler_params=pltpu.CompilerParams(vmem_limit_bytes=VMEM),
@@ -134,16 +125,28 @@
     )(*args)
 
 
-def shift(value, axis, by):
-    return lax.ppermute(value, axis, [(i, (i + by) % RING) for i in range(RING)])
+def turn(value, axis, by):
+    at = lambda core, i: core * RING + i if axis == "x" else i * 2 + core
+    axes = ("core", axis) if axis == "x" else (axis, "core")
+    steps = ((0, by), (1, -by))
+    pairs = [(at(c, i), at(c, (i + d) % RING)) for c, d in steps for i in range(RING)]
+    return lax.ppermute(value, axes, pairs)
+
+
+def joined(axis, own, got, across):
+    me = lax.axis_index(axis)
+    ahead = jnp.where(lax.axis_index("core") == 0, RING - 1, 1)
+    depth, width = own.shape
+    slots = (me, me + ahead, me - ahead, me + 2, me + 2)
+    whole = jnp.zeros((RING * depth, width), own.dtype)
+    for slot, piece, shift in zip(slots, (own, *got, *across), (0, 0, 0, 0, depth // 2)):
+        start = (slot & (RING - 1)) * depth + shift
+        whole = lax.dynamic_update_slice(whole, piece, (start, 0))
+    return whole
 
 
 def swap_cores(value):
     return lax.ppermute(value, "core", [(0, 1), (1, 0)])
-
-
-def copies(value):
-    return jnp.broadcast_to(value[None], (RING,) + value.shape)
 
 
 def exchange(value, axis):
@@ -170,20 +173,23 @@
     chunk = swap(attended)
     rows = lax.all_gather(attended, "zh", axis=0, tiled=True)
     chunk, rows = lax.optimization_barrier((chunk, rows))
-    cols = lax.all_gather(chunk, "zl", axis=0, tiled=True)
-    after, before = shift(rows, "x", -1), shift(rows, "x", 1)
-    cols, after, before = lax.optimization_barrier((cols, after, before))
-    near_cols = exchange(copies(cols), "y")
-    cut = after.shape[0] // 2
-    first, second = shift(after[:cut], "x", -1), shift(before[cut:], "x", 1)
-    rows = jnp.concatenate([rows, after, first, second, before])
-    near_cols, rows = lax.optimization_barrier((near_cols, rows))
-    far_cols = swap_cores(near_cols)
-    place = lax.axis_index("x"), lax.axis_index("core"), lax.axis_index("zh")
-    near = jnp.stack(place).astype(jnp.int32)
-    far = jnp.stack((place[0], 1 - place[1], place[2])).astype(jnp.int32)
-    hessian = hessian_half(near, rows, near_cols)
-    hessian = hessian_half(far, rows, far_cols, hessian)
+    landed = [[place * RING + group for place in LANDING[group]] for group in range(RING)]
+    cols = lax.all_gather(chunk, ("zl", "zh"), axis=0, tiled=True, axis_index_groups=landed)
+    cols, rows = lax.optimization_barrier((cols, rows))
+    ways = ((rows, "x"), (cols, "y"))
+    got = [[turn(v, axis, by) for v, axis in ways] for by in (1, -1)]
+    half = rows.shape[0] // 2
+    cut = lax.optimization_barrier([[v[:half] for v in got[0]], [v[half:] for v in got[1]]])
+    across = [[turn(v, "xy"[k], by) for k, v in enumerate(c)] for c, by in zip(cut, (1, -1))]
+    rows, near = (
+        joined("xy"[k], v, (got[0][k], got[1][k]), (across[0][k], across[1][k]))
+        for k, v in enumerate((rows, cols))
+    )
+    near, rows = lax.optimization_barrier((near, rows))
+    far = swap_cores(near)
+    core = lax.axis_index("core").astype(jnp.int32).reshape(1)
+    hessian = hessian_half(core, rows, near)
+    hessian = hessian_half(1 - core, rows, far, hessian)
     return attended, hessian
 
 

time: 122 us -> 127 us (1.041)
  starting transfers between devices: 29 us -> 38.2 us
  waiting for transfers between devices: 18.7 us -> 24.8 us
  blocking collectives: 56.9 us -> 51.2 us
  Pallas kernels: 11.6 us -> 8.34 us
  local copies, waits for them, and re-layouts: 4.63 us -> 2.61 us
    ppermute x4 -> x8, waiting for transfers between devices: 5.66 us -> 19.8 us  [turn(): return lax.ppermute(value, axes, pairs)]
    ppermute x4 -> x8, starting transfers between devices: 11.1 us -> 23.9 us  [turn(): return lax.ppermute(value, axes, pairs)]
    all_to_all x2 -> x1, waiting for transfers between devices: 13.1 us -> 3.69 us  [exchange(): return lax.all_to_all(value, axis, split_axis=0, concat_axis=0, tiled=True)]
    all_gather x1, blocking collectives: 25.5 us -> 18.6 us  [on_device(): lax.all_gather(chunk, ('zl', 'zh'), axis=0, tiled=True, axis_index_groups...]
    all_to_all x2 -> x1, starting transfers between devices: 9.29 us -> 4.84 us  [exchange(): return lax.all_to_all(value, axis, split_axis=0, concat_axis=0, tiled=True)]
    pallas_call x2, Pallas kernels: 8.21 us -> 4.97 us  [hessian_half(): pl.pallas_call(half_kernel, out_shape=jax.ShapeDtypeStruct((width, 2 * ha...]
    broadcast_in_dim x1 -> x0, local copies, waits for them, and re-layouts: 1.48 us -> none  [copies(): return jnp.broadcast_to(value[None], (RING,) + value.shape)]
  transfers between devices with their start and end apart: 8 -> 11, of which waited for: 4 -> 8; matrix products, arithmetic and copies ran while one was open for 3% -> 2% of each run, Pallas kernels for 3% -> 2%
where the time goes in v8:
time: 127 us; the launch traced here: 126 us
  blocking collectives  51.2 us (40%)
  starting transfers between devices  38.2 us (30%)
  waiting for transfers between devices  24.8 us (20%)
  Pallas kernels  8.34 us (7%)
  local copies, waits for them, and re-layouts  2.61 us (2%)
    all_gather x1, blocking collectives, on_device(): rows = lax.all_gather(attended, 'zh', axis=0, tiled=True)  32.7 us
    ppermute x8, starting transfers between devices, turn(): return lax.ppermute(value, axes, pairs)  23.9 us
    ppermute x8, waiting for transfers between devices, turn(): return lax.ppermute(value, axes, pairs)  19.8 us
    all_gather x1, blocking collectives, on_device(): lax.all_gather(chunk, ('zl', 'zh'), axis=0, tiled=True, axis_index_groups...  18.6 us
    ppermute x1, starting transfers between devices, swap_cores(): return lax.ppermute(value, 'core', [(0, 1), (1, 0)])  7.95 us
    pallas_call x2, Pallas kernels, hessian_half(): pl.pallas_call(half_kernel, out_shape=jax.ShapeDtypeStruct((width, 2 * ha...  4.97 us
    all_to_all x1, starting transfers between devices, exchange(): return lax.all_to_all(value, axis, split_axis=0, concat_axis=0, tiled=True)  4.84 us
    all_to_all x1, waiting for transfers between devices, exchange(): return lax.all_to_all(value, axis, split_axis=0, concat_axis=0, tiled=True)  3.69 us
  transfers between devices with their start and end apart: 11, of which 8 were waited for; matrix products, arithmetic and copies ran while one was open for 2% of the time, Pallas kernels for 2%

profile of v8, /device:TPU:1, one launch (start us, length us, event | category | flops | bytes accessed | tf_op | source)
XLA Modules:
  0.0 126.1 jit_solution(15416213098964315867)
XLA Ops:
  0.7 1.5 %pack.1 = bf16[4,272,128]{2,1,0:T(8,128)(2,1)} custom-call(s32[1]{0:T(128)} %bitcast.2.g_ref, bf16[128,1024]{1,0:T(8,128)(2,1)} %k_ref.1, bf16[128,1024]{1,0:T(8,128)(2,1)} %v_ref.1, s32[1,128]{1,0:T(1,128)} %bitcast.8), custom_call_target="tpu_custom_call" | custom-call | tf_op jit(solution)/shard_map/pack/pallas_call | solution.py:37
  2.2 4.8 %all-to-all-start = ((bf16[4,272,128]{2,1,0:T(8,128)(2,1)}), bf16[4,272,128]{2,1,0:T(8,128)(2,1)S(1)}, u32[]{:S(2)}, u32[]{:S(2)}) async-start(bf16[4,272,128]{2,1,0:T(8,128)(2,1)} %pack.1), calls=%async_computation | async-start | bytes 557056 | tf_op jit(solution)/shard_map/all_to_all | solution.py:153
  9.0 3.7 %all-to-all-done.kv_ref = bf16[4,272,128]{2,1,0:T(8,128)(2,1)S(1)} async-done(((bf16[4,272,128]{2,1,0:T(8,128)(2,1)}), bf16[4,272,128]{2,1,0:T(8,128)(2,1)S(1)}, u32[]{:S(2)}, u32[]{:S(2)}) %all-to-all-start) | async-done | bytes 278560 | tf_op jit(solution)/shard_map/all_to_all | solution.py:153
  12.6 1.8 %attend.1 = bf16[128,512]{1,0:T(8,128)(2,1)} custom-call(bf16[4,128,128]{2,1,0:T(8,128)(2,1)S(1)} %bitcast.6, bf16[4,272,128]{2,1,0:T(8,128)(2,1)S(1)} %all-to-all-done.kv_ref, s32[128,1]{1,0:T(8,128)S(1)} %copy.10.p_ref), custom_call_target="tpu_custom_call" | custom-call | tf_op jit(solution)/shard_map/attend/pallas_call | solution.py:81
  14.5 1.6 %collective-permute-start = (bf16[128,512]{1,0:T(8,128)(2,1)}, bf16[128,512]{1,0:T(8,128)(2,1)S(1)}, u32[]{:S(2)}, u32[]{:S(2)}) collective-permute-start(bf16[128,512]{1,0:T(8,128)(2,1)} %attend.1), channel_id=1, source_target_pairs={{0,0},{1,32},{2,64},{3,96},{4,256},{5,288},{6,320},{7,352},{8,384}... | collective-permute-start | bytes 393224 | tf_op jit(solution)/shard_map/ppermute | solution.py:161
  16.0 32.7 %all_gather.6 = bf16[512,512]{1,0:T(8,128)(2,1)S(1)} all-gather(bf16[128,512]{1,0:T(8,128)(2,1)} %attend.1), channel_id=1, replica_groups=mesh['zl'=4,'y'=4,'core'=2,'zh'=4,'x'=4] {'zh'}, dimensions={0}, use_global_device_ids=true | all-gather | bytes 655360 | tf_op jit(solution)/shard_map/all_gather | solution.py:174
  48.7 18.6 %all_gather.7 = bf16[512,512]{1,0:T(8,128)(2,1)S(1)} all-gather(bf16[128,512]{1,0:T(8,128)(2,1)S(1)} %collective-permute-done), channel_id=1, replica_groups={{0,256,384,128},{132,388,260,4},{392,136,8,264},{268,12,140,396},{1,257..., dimensions={0}, use_global_device_ids=true | all-gather | bytes 655360 | tf_op jit(solution)/shard_map/all_gather | solution.py:177
  67.3 6.1 %collective-permute-start.3 = (bf16[512,512]{1,0:T(8,128)(2,1)S(1)}, bf16[512,512]{1,0:T(8,128)(2,1)S(1)}, u32[]{:S(2)}, u32[]{:S(2)}) collective-permute-start(bf16[512,512]{1,0:T(8,128)(2,1)S(1)} %all_gather.6), channel_id=1, source_target_pairs={{0,1},{1,2},{2,3},{3,0},{16,19},{17,16},{18,17},{19,18},{4,5},{5,6... | collective-permute-start | bytes 1572872 | tf_op jit(solution)/shard_map/ppermute | solution.py:133
  73.4 1.9 %collective-permute-start.1 = (bf16[512,512]{1,0:T(8,128)(2,1)S(1)}, bf16[512,512]{1,0:T(8,128)(2,1)S(1)}, u32[]{:S(2)}, u32[]{:S(2)}) collective-permute-start(bf16[512,512]{1,0:T(8,128)(2,1)S(1)} %all_gather.7), channel_id=1, source_target_pairs={{0,32},{32,64},{64,96},{96,0},{16,112},{48,16},{80,48},{112,80},{1... | collective-permute-start | bytes 1572872 | tf_op jit(solution)/shard_map/ppermute | solution.py:133
  75.3 2.0 %collective-permute-start.4 = (bf16[512,512]{1,0:T(8,128)(2,1)S(1)}, bf16[512,512]{1,0:T(8,128)(2,1)S(1)}, u32[]{:S(2)}, u32[]{:S(2)}) collective-permute-start(bf16[512,512]{1,0:T(8,128)(2,1)S(1)} %all_gather.6), channel_id=1, source_target_pairs={{0,3},{1,0},{2,1},{3,2},{16,17},{17,18},{18,19},{19,16},{4,7},{5,4... | collective-permute-start | bytes 1572872 | tf_op jit(solution)/shard_map/ppermute | solution.py:133
  77.3 3.3 %collective-permute-start.2 = (bf16[512,512]{1,0:T(8,128)(2,1)S(1)}, bf16[512,512]{1,0:T(8,128)(2,1)S(1)}, u32[]{:S(2)}, u32[]{:S(2)}) collective-permute-start(bf16[512,512]{1,0:T(8,128)(2,1)S(1)} %all_gather.7), channel_id=1, source_target_pairs={{0,96},{32,0},{64,32},{96,64},{16,48},{48,80},{80,112},{112,16},{1... | collective-permute-start | bytes 1572872 | tf_op jit(solution)/shard_map/ppermute | solution.py:133
  81.1 2.5 %collective-permute-done.1 = bf16[512,512]{1,0:T(8,128)(2,1)S(1)} collective-permute-done((bf16[512,512]{1,0:T(8,128)(2,1)S(1)}, bf16[512,512]{1,0:T(8,128)(2,1)S(1)}, u32[]{:S(2)}, u32[]{:S(2)}) %collective-permute-start.1) | collective-permute-done | bytes 524320 | tf_op jit(solution)/shard_map/ppermute | solution.py:133
  83.6 7.6 %collective-permute-done.4 = bf16[512,512]{1,0:T(8,128)(2,1)S(1)} collective-permute-done((bf16[512,512]{1,0:T(8,128)(2,1)S(1)}, bf16[512,512]{1,0:T(8,128)(2,1)S(1)}, u32[]{:S(2)}, u32[]{:S(2)}) %collective-permute-start.4) | collective-permute-done | bytes 524320 | tf_op jit(solution)/shard_map/ppermute | solution.py:133
  91.2 2.9 %collective-permute-done.2 = bf16[512,512]{1,0:T(8,128)(2,1)S(1)} collective-permute-done((bf16[512,512]{1,0:T(8,128)(2,1)S(1)}, bf16[512,512]{1,0:T(8,128)(2,1)S(1)}, u32[]{:S(2)}, u32[]{:S(2)}) %collective-permute-start.2) | collective-permute-done | bytes 524320 | tf_op jit(solution)/shard_map/ppermute | solution.py:133
  94.2 1.9 %collective-permute-start.5 = (bf16[256,512]{1,0:T(8,128)(2,1)S(1)}, bf16[256,512]{1,0:T(8,128)(2,1)S(1)}, u32[]{:S(2)}, u32[]{:S(2)}) collective-permute-start(bf16[256,512]{1,0:T(8,128)(2,1)S(1)} %slice.17), channel_id=1, source_target_pairs={{0,32},{32,64},{64,96},{96,0},{16,112},{48,16},{80,48},{112,80},{1... | collective-permute-start | bytes 786440 | tf_op jit(solution)/shard_map/ppermute | solution.py:133
  96.1 3.4 %collective-permute-start.6 = (bf16[256,512]{1,0:T(8,128)(2,1)S(1)}, bf16[256,512]{1,0:T(8,128)(2,1)S(1)}, u32[]{:S(2)}, u32[]{:S(2)}) collective-permute-start(bf16[256,512]{1,0:T(8,128)(2,1)S(1)} %slice.19), channel_id=1, source_target_pairs={{0,96},{32,0},{64,32},{96,64},{16,48},{48,80},{80,112},{112,16},{1... | collective-permute-start | bytes 786440 | tf_op jit(solution)/shard_map/ppermute | solution.py:133
  99.5 3.2 %collective-permute-start.7 = (bf16[256,512]{1,0:T(8,128)(2,1)S(1)}, bf16[256,512]{1,0:T(8,128)(2,1)S(1)}, u32[]{:S(2)}, u32[]{:S(2)}) collective-permute-start(bf16[256,512]{1,0:T(8,128)(2,1)S(1)} %slice.16), channel_id=1, source_target_pairs={{0,1},{1,2},{2,3},{3,0},{16,19},{17,16},{18,17},{19,18},{4,5},{5,6... | collective-permute-start | bytes 786440 | tf_op jit(solution)/shard_map/ppermute | solution.py:133
  102.7 2.0 %collective-permute-start.8 = (bf16[256,512]{1,0:T(8,128)(2,1)S(1)}, bf16[256,512]{1,0:T(8,128)(2,1)S(1)}, u32[]{:S(2)}, u32[]{:S(2)}) collective-permute-start(bf16[256,512]{1,0:T(8,128)(2,1)S(1)} %slice.18), channel_id=1, source_target_pairs={{0,3},{1,0},{2,1},{3,2},{16,17},{17,18},{18,19},{19,16},{4,7},{5,4... | collective-permute-start | bytes 786440 | tf_op jit(solution)/shard_map/ppermute | solution.py:133
  105.7 1.2 collective-permute-done.7
  106.9 5.0 %collective-permute-done.8 = bf16[256,512]{1,0:T(8,128)(2,1)S(1)} collective-permute-done((bf16[256,512]{1,0:T(8,128)(2,1)S(1)}, bf16[256,512]{1,0:T(8,128)(2,1)S(1)}, u32[]{:S(2)}, u32[]{:S(2)}) %collective-permute-start.8) | collective-permute-done | bytes 262176 | tf_op jit(solution)/shard_map/ppermute | solution.py:133
  111.9 7.9 %collective-permute-start.9 = (bf16[2048,512]{1,0:T(8,128)(2,1)S(1)}, bf16[2048,512]{1,0:T(8,128)(2,1)S(1)}, u32[]{:S(2)}, u32[]{:S(2)}) collective-permute-start(bf16[2048,512]{1,0:T(8,128)(2,1)S(1)} %constant_dynamic-update-slice_fusion.5.cols_ref), channel_id=1, source_target_pairs={{0,16},{16,0},{1,17},{17,1},{2,18},{18,2},{3,19},{19,3},{4,20},{20... | collective-permute-start | bytes 6291464 | tf_op jit(solution)/shard_map/ppermute | solution.py:149
  119.8 2.5 %hessian_half.2.rest_0_ = f32[512,1024]{1,0:T(8,128)} custom-call(s32[1]{0:T(128)} %bitcast.5.s_ref, bf16[2048,512]{1,0:T(8,128)(2,1)S(1)} %constant_dynamic-update-slice_fusion.rows_ref, bf16[2048,512]{1,0:T(8,128)(2,1)S(1)} %constant_dynamic-update-slice_fusion.5.cols_ref), custom_call_target="tpu_custom_call" | custom-call | tf_op jit(solution)/shard_map/hessian_half/pallas_call | solution.py:113
  122.3 1.3 %collective-permute-done.9.cols_ref = bf16[2048,512]{1,0:T(8,128)(2,1)S(1)} collective-permute-done((bf16[2048,512]{1,0:T(8,128)(2,1)S(1)}, bf16[2048,512]{1,0:T(8,128)(2,1)S(1)}, u32[]{:S(2)}, u32[]{:S(2)}) %collective-permute-start.9) | collective-permute-done | bytes 2097184 | tf_op jit(solution)/shard_map/ppermute | solution.py:149
  123.6 2.5 %hessian_half.3 = f32[512,1024]{1,0:T(8,128)} custom-call(s32[1]{0:T(128)S(6)} %sub.14.s_ref, bf16[2048,512]{1,0:T(8,128)(2,1)S(1)} %constant_dynamic-update-slice_fusion.rows_ref, bf16[2048,512]{1,0:T(8,128)(2,1)S(1)} %collective-permute-done.9.cols_ref, f32[512,1024]{1,0:T(8,128)} %hessian_half.2.rest_0_), custom_call_target="tpu_custom_call", output_to_operand_aliasing={{}: (3, {})} | custom-call | tf_op jit(solution)/shard_map/hessian_half/pallas_call | solution.py:113
  (23 shorter events, 3.3 us)
Async XLA Ops:
  2.2 10.5 %all-to-all-start = ((bf16[4,272,128]{2,1,0:T(8,128)(2,1)}), bf16[4,272,128]{2,1,0:T(8,128)(2,1)S(1)}, u32[]{:S(2)}, u32[]{:S(2)}) async-start(bf16[4,272,128]{2,1,0:T(8,128)(2,1)} %pack.1), calls=%async_computation | async-start | bytes 557056 | tf_op jit(solution)/shard_map/all_to_all | solution.py:153
  14.5 34.2 %collective-permute-start = (bf16[128,512]{1,0:T(8,128)(2,1)}, bf16[128,512]{1,0:T(8,128)(2,1)S(1)}, u32[]{:S(2)}, u32[]{:S(2)}) collective-permute-start(bf16[128,512]{1,0:T(8,128)(2,1)} %attend.1), channel_id=1, source_target_pairs={{0,0},{1,32},{2,64},{3,96},{4,256},{5,288},{6,320},{7,352},{8,384}... | collective-permute-start | bytes 393224 | tf_op jit(solution)/shard_map/ppermute | solution.py:161
  67.3 13.8 %collective-permute-start.3 = (bf16[512,512]{1,0:T(8,128)(2,1)S(1)}, bf16[512,512]{1,0:T(8,128)(2,1)S(1)}, u32[]{:S(2)}, u32[]{:S(2)}) collective-permute-start(bf16[512,512]{1,0:T(8,128)(2,1)S(1)} %all_gather.6), channel_id=1, source_target_pairs={{0,1},{1,2},{2,3},{3,0},{16,19},{17,16},{18,17},{19,18},{4,5},{5,6... | collective-permute-start | bytes 1572872 | tf_op jit(solution)/shard_map/ppermute | solution.py:133
  73.4 10.2 %collective-permute-start.1 = (bf16[512,512]{1,0:T(8,128)(2,1)S(1)}, bf16[512,512]{1,0:T(8,128)(2,1)S(1)}, u32[]{:S(2)}, u32[]{:S(2)}) collective-permute-start(bf16[512,512]{1,0:T(8,128)(2,1)S(1)} %all_gather.7), channel_id=1, source_target_pairs={{0,32},{32,64},{64,96},{96,0},{16,112},{48,16},{80,48},{112,80},{1... | collective-permute-start | bytes 1572872 | tf_op jit(solution)/shard_map/ppermute | solution.py:133
  75.3 15.9 %collective-permute-start.4 = (bf16[512,512]{1,0:T(8,128)(2,1)S(1)}, bf16[512,512]{1,0:T(8,128)(2,1)S(1)}, u32[]{:S(2)}, u32[]{:S(2)}) collective-permute-start(bf16[512,512]{1,0:T(8,128)(2,1)S(1)} %all_gather.6), channel_id=1, source_target_pairs={{0,3},{1,0},{2,1},{3,2},{16,17},{17,18},{18,19},{19,16},{4,7},{5,4... | collective-permute-start | bytes 1572872 | tf_op jit(solution)/shard_map/ppermute | solution.py:133
  77.3 16.9 %collective-permute-start.2 = (bf16[512,512]{1,0:T(8,128)(2,1)S(1)}, bf16[512,512]{1,0:T(8,128)(2,1)S(1)}, u32[]{:S(2)}, u32[]{:S(2)}) collective-permute-start(bf16[512,512]{1,0:T(8,128)(2,1)S(1)} %all_gather.7), channel_id=1, source_target_pairs={{0,96},{32,0},{64,32},{96,64},{16,48},{48,80},{80,112},{112,16},{1... | collective-permute-start | bytes 1572872 | tf_op jit(solution)/shard_map/ppermute | solution.py:133
  94.2 10.8 %collective-permute-start.5 = (bf16[256,512]{1,0:T(8,128)(2,1)S(1)}, bf16[256,512]{1,0:T(8,128)(2,1)S(1)}, u32[]{:S(2)}, u32[]{:S(2)}) collective-permute-start(bf16[256,512]{1,0:T(8,128)(2,1)S(1)} %slice.17), channel_id=1, source_target_pairs={{0,32},{32,64},{64,96},{96,0},{16,112},{48,16},{80,48},{112,80},{1... | collective-permute-start | bytes 786440 | tf_op jit(solution)/shard_map/ppermute | solution.py:133
  96.1 9.6 %collective-permute-start.6 = (bf16[256,512]{1,0:T(8,128)(2,1)S(1)}, bf16[256,512]{1,0:T(8,128)(2,1)S(1)}, u32[]{:S(2)}, u32[]{:S(2)}) collective-permute-start(bf16[256,512]{1,0:T(8,128)(2,1)S(1)} %slice.19), channel_id=1, source_target_pairs={{0,96},{32,0},{64,32},{96,64},{16,48},{48,80},{80,112},{112,16},{1... | collective-permute-start | bytes 786440 | tf_op jit(solution)/shard_map/ppermute | solution.py:133
  99.5 7.4 %collective-permute-start.7 = (bf16[256,512]{1,0:T(8,128)(2,1)S(1)}, bf16[256,512]{1,0:T(8,128)(2,1)S(1)}, u32[]{:S(2)}, u32[]{:S(2)}) collective-permute-start(bf16[256,512]{1,0:T(8,128)(2,1)S(1)} %slice.16), channel_id=1, source_target_pairs={{0,1},{1,2},{2,3},{3,0},{16,19},{17,16},{18,17},{19,18},{4,5},{5,6... | collective-permute-start | bytes 786440 | tf_op jit(solution)/shard_map/ppermute | solution.py:133
  102.7 9.1 %collective-permute-start.8 = (bf16[256,512]{1,0:T(8,128)(2,1)S(1)}, bf16[256,512]{1,0:T(8,128)(2,1)S(1)}, u32[]{:S(2)}, u32[]{:S(2)}) collective-permute-start(bf16[256,512]{1,0:T(8,128)(2,1)S(1)} %slice.18), channel_id=1, source_target_pairs={{0,3},{1,0},{2,1},{3,2},{16,17},{17,18},{18,19},{19,16},{4,7},{5,4... | collective-permute-start | bytes 786440 | tf_op jit(solution)/shard_map/ppermute | solution.py:133
  111.9 11.7 %collective-permute-start.9 = (bf16[2048,512]{1,0:T(8,128)(2,1)S(1)}, bf16[2048,512]{1,0:T(8,128)(2,1)S(1)}, u32[]{:S(2)}, u32[]{:S(2)}) collective-permute-start(bf16[2048,512]{1,0:T(8,128)(2,1)S(1)} %constant_dynamic-update-slice_fusion.5.cols_ref), channel_id=1, source_target_pairs={{0,16},{16,0},{1,17},{17,1},{2,18},{18,2},{3,19},{19,3},{4,20},{20... | collective-permute-start | bytes 6291464 | tf_op jit(solution)/shard_map/ppermute | solution.py:149

commit v9 on v7

--- a/solution.py
+++ b/solution.py
@@ -86,30 +86,8 @@
     )(queries, gathered, positions.reshape(tok, 1))
 
 
-LANDING = ((0, 2, 3, 1), (2, 1, 3, 0), (3, 0, 2, 1), (2, 0, 1, 3))
-TAKEN = tuple(tuple(line.index(k) for k in range(RING)) for line in LANDING)
+LANDING = ((0, 2, 3, 1), (1, 3, 2, 0), (3, 1, 0, 2), (2, 0, 1, 3))
 CONTRACT = (((0,), (0,)), ((), ()))
-
-
-def ordered_kernel(s_ref, v_ref, o_ref):
-    for copy in range(RING):
-        o_ref[copy] = v_ref[...]
-
-
-def ordered_copies(order, value):
-    depth, width = value.shape
-    part = depth // RING
-    return pl.pallas_call(
-        ordered_kernel,
-        out_shape=jax.ShapeDtypeStruct((RING, depth, width), value.dtype),
-        grid_spec=pltpu.PrefetchScalarGridSpec(
-            num_scalar_prefetch=1,
-            grid=(RING,),
-            in_specs=[pl.BlockSpec((part, width), lambda i, s: (s[i], 0))],
-            out_specs=pl.BlockSpec((RING, part, width), lambda i, s: (0, i, 0)),
-        ),
-        name="ordered_copies",
-    )(order, value)
 
 
 def hessian_kernel(s_ref, rows_ref, near_ref, far_ref, o_ref):
@@ -154,12 +132,27 @@
     )(core, rows, near, far)
 
 
+def shift(value, axis, by):
+    return lax.ppermute(value, axis, [(i, (i + by) % RING) for i in range(RING)])
+
+
+def joined(axis, own, after, before, across):
+    me = lax.axis_index(axis)
+    depth, width = own.shape
+    pieces = ((own, 0, 0), (after, 1, 0), (before, 3, 0), (across[0], 2, 0), (across[1], 2, depth // 2))
+    whole = jnp.zeros((RING * depth, width), own.dtype)
+    for piece, ahead, more in pieces:
+        start = ((me + ahead) & (RING - 1)) * depth + more
+        whole = lax.dynamic_update_slice(whole, piece, (start, 0))
+    return whole
+
+
+def copies(value):
+    return jnp.broadcast_to(value[None], (RING,) + value.shape)
+
+
 def swap_cores(value):
     return lax.ppermute(value, "core", [(0, 1), (1, 0)])
-
-
-def copies(value):
-    return jnp.broadcast_to(value[None], (RING,) + value.shape)
 
 
 def exchange(value, axis):
@@ -184,16 +177,21 @@
     queries = jnp.transpose(query_rows.reshape(tok, local_heads, HD), (1, 0, 2))
     attended = attend(queries, gathered, positions)
     chunk = swap(attended)
-    cols = lax.all_gather(chunk, "zl", axis=0, tiled=True)
-    cols, mine = lax.optimization_barrier((cols, attended))
+    rows = lax.all_gather(attended, "zh", axis=0, tiled=True)
+    chunk, rows = lax.optimization_barrier((chunk, rows))
+    landed = [[place * RING + group for place in LANDING[group]] for group in range(RING)]
+    cols = lax.all_gather(chunk, ("zl", "zh"), axis=0, tiled=True, axis_index_groups=landed)
+    cols, rows = lax.optimization_barrier((cols, rows))
     near = exchange(copies(cols), "y")
-    rows = lax.all_gather(mine, "zh", axis=0, tiled=True)
-    order = jnp.asarray(TAKEN, jnp.int32)[lax.axis_index("zh")]
-    near, rows = lax.optimization_barrier((near, ordered_copies(order, rows)))
-    rows = exchange(rows, "x")
+    after, before = shift(rows, "x", -1), shift(rows, "x", 1)
+    cut = after.shape[0] // 2
+    across = shift(after[:cut], "x", -1), shift(before[cut:], "x", 1)
+    near, _, _ = lax.optimization_barrier((near, after, before))
     far = swap_cores(near)
+    across, far = lax.optimization_barrier((across, far))
+    rows = joined("x", rows, after, before, across)
     core = lax.axis_index("core").astype(jnp.int32).reshape(1)
-    hessian = hessian_of(core, rows.reshape(-1, rows.shape[2]), near, far)
+    hessian = hessian_of(core, rows, near, far)
     return attended, hessian
 
 

time: 132 us -> 124 us (0.939)
  blocking collectives: 89.2 us -> 50.8 us
  waiting for transfers between devices: 3.7 us -> 23.6 us
  starting transfers between devices: 21.5 us -> 33.1 us
  Pallas kernels: 11.8 us -> 9.26 us
    all_to_all x1 -> x0, blocking collectives: 29.8 us -> none  [exchange(): return lax.all_to_all(value, axis, split_axis=0, concat_axis=0, tiled=True)]
    ppermute x0 -> x4, starting transfers between devices: none -> 15.1 us  [shift(): lax.ppermute(value, axis, [(i, (i + by) % RING) for i in range(RING)])]
    ppermute x0 -> x4, waiting for transfers between devices: none -> 12.8 us  [shift(): lax.ppermute(value, axis, [(i, (i + by) % RING) for i in range(RING)])]
    all_gather x2, blocking collectives: 59.4 us -> 50.8 us  [the longest x1 32.7 us: on_device(): rows = lax.all_gather(attended, 'zh', axis=0, tiled=True)]
    all_to_all x2, waiting for transfers between devices: 3.69 us -> 10.8 us  [exchange(): return lax.all_to_all(value, axis, split_axis=0, concat_axis=0, tiled=True)]
    pallas_call x1 -> x0, Pallas kernels: 4.15 us -> none  [ordered_copies(): pl.pallas_call(ordered_kernel, out_shape=jax.ShapeDtypeStruct((RING, dept...]
    all_to_all x2, starting transfers between devices: 11.9 us -> 9.31 us  [exchange(): return lax.all_to_all(value, axis, split_axis=0, concat_axis=0, tiled=True)]
    pallas_call x1, Pallas kernels: 4.3 us -> 5.89 us  [hessian_of(): pl.pallas_call(hessian_kernel, out_shape=jax.ShapeDtypeStruct((width, 2 *...]
  transfers between devices with their start and end apart: 4 -> 8, of which waited for: 1 -> 6; matrix products, arithmetic and copies ran while one was open for 2% -> 3% of each run, Pallas kernels for 3% -> 0%
where the time goes in v9:
time: 124 us; the launch traced here: 123 us
  blocking collectives  50.8 us (41%)
  starting transfers between devices  33.1 us (27%)
  waiting for transfers between devices  23.6 us (19%)
  Pallas kernels  9.26 us (7%)
  local copies, waits for them, and re-layouts  5.74 us (5%)
    all_gather x1, blocking collectives, on_device(): rows = lax.all_gather(attended, 'zh', axis=0, tiled=True)  32.7 us
    all_gather x1, blocking collectives, on_device(): lax.all_gather(chunk, ('zl', 'zh'), axis=0, tiled=True, axis_index_groups...  18 us
    ppermute x4, starting transfers between devices, shift(): lax.ppermute(value, axis, [(i, (i + by) % RING) for i in range(RING)])  15.1 us
    ppermute x4, waiting for transfers between devices, shift(): lax.ppermute(value, axis, [(i, (i + by) % RING) for i in range(RING)])  12.8 us
    all_to_all x2, waiting for transfers between devices, exchange(): return lax.all_to_all(value, axis, split_axis=0, concat_axis=0, tiled=True)  10.8 us
    all_to_all x2, starting transfers between devices, exchange(): return lax.all_to_all(value, axis, split_axis=0, concat_axis=0, tiled=True)  9.31 us
    ppermute x1, starting transfers between devices, swap_cores(): return lax.ppermute(value, 'core', [(0, 1), (1, 0)])  7.19 us
    pallas_call x1, Pallas kernels, hessian_of(): pl.pallas_call(hessian_kernel, out_shape=jax.ShapeDtypeStruct((width, 2 *...  5.89 us
  transfers between devices with their start and end apart: 8, of which 6 were waited for; matrix products, arithmetic and copies ran while one was open for 3% of the time, Pallas kernels for 0%

profile of v9, /device:TPU:1, one launch (start us, length us, event | category | flops | bytes accessed | tf_op | source)
XLA Modules:
  0.0 123.3 jit_solution(15284724146774762181)
XLA Ops:
  0.7 1.5 %pack.1 = bf16[4,272,128]{2,1,0:T(8,128)(2,1)} custom-call(s32[1]{0:T(128)} %bitcast.2.g_ref, bf16[128,1024]{1,0:T(8,128)(2,1)} %k_ref.1, bf16[128,1024]{1,0:T(8,128)(2,1)} %v_ref.1, s32[1,128]{1,0:T(1,128)} %bitcast.8), custom_call_target="tpu_custom_call" | custom-call | tf_op jit(solution)/shard_map/pack/pallas_call | solution.py:37
  2.2 4.8 %all-to-all-start = ((bf16[4,272,128]{2,1,0:T(8,128)(2,1)}), bf16[4,272,128]{2,1,0:T(8,128)(2,1)S(1)}, u32[]{:S(2)}, u32[]{:S(2)}) async-start(bf16[4,272,128]{2,1,0:T(8,128)(2,1)} %pack.1), calls=%async_computation | async-start | bytes 557056 | tf_op jit(solution)/shard_map/all_to_all | solution.py:159
  7.0 0.8 copy.9.p_ref
  7.8 1.0 copy.7
  8.9 3.7 %all-to-all-done.kv_ref = bf16[4,272,128]{2,1,0:T(8,128)(2,1)S(1)} async-done(((bf16[4,272,128]{2,1,0:T(8,128)(2,1)}), bf16[4,272,128]{2,1,0:T(8,128)(2,1)S(1)}, u32[]{:S(2)}, u32[]{:S(2)}) %all-to-all-start) | async-done | bytes 278560 | tf_op jit(solution)/shard_map/all_to_all | solution.py:159
  12.6 1.9 %attend.1 = bf16[128,512]{1,0:T(8,128)(2,1)} custom-call(bf16[4,128,128]{2,1,0:T(8,128)(2,1)S(1)} %bitcast.6, bf16[4,272,128]{2,1,0:T(8,128)(2,1)S(1)} %all-to-all-done.kv_ref, s32[128,1]{1,0:T(8,128)S(1)} %copy.9.p_ref), custom_call_target="tpu_custom_call" | custom-call | tf_op jit(solution)/shard_map/attend/pallas_call | solution.py:81
  14.5 1.6 %collective-permute-start = (bf16[128,512]{1,0:T(8,128)(2,1)}, bf16[128,512]{1,0:T(8,128)(2,1)S(1)}, u32[]{:S(2)}, u32[]{:S(2)}) collective-permute-start(bf16[128,512]{1,0:T(8,128)(2,1)} %attend.1), channel_id=1, source_target_pairs={{0,0},{1,32},{2,64},{3,96},{4,256},{5,288},{6,320},{7,352},{8,384}... | collective-permute-start | bytes 393224 | tf_op jit(solution)/shard_map/ppermute | solution.py:167
  16.0 32.7 %all_gather.6 = bf16[512,512]{1,0:T(8,128)(2,1)S(1)} all-gather(bf16[128,512]{1,0:T(8,128)(2,1)} %attend.1), channel_id=1, replica_groups=mesh['zl'=4,'y'=4,'core'=2,'zh'=4,'x'=4] {'zh'}, dimensions={0}, use_global_device_ids=true | all-gather | bytes 655360 | tf_op jit(solution)/shard_map/all_gather | solution.py:180
  48.8 18.0 %all_gather.7 = bf16[512,512]{1,0:T(8,128)(2,1)S(1)} all-gather(bf16[128,512]{1,0:T(8,128)(2,1)S(1)} %collective-permute-done), channel_id=1, replica_groups={{0,256,384,128},{132,388,260,4},{392,136,8,264},{268,12,140,396},{1,257..., dimensions={0}, use_global_device_ids=true | all-gather | bytes 655360 | tf_op jit(solution)/shard_map/all_gather | solution.py:183
  66.8 1.5 %broadcast_in_dim.10 = bf16[4,512,512]{2,1,0:T(8,128)(2,1)} broadcast(bf16[512,512]{1,0:T(8,128)(2,1)S(1)} %all_gather.7), dimensions={1,2} | broadcast | bytes 2621440 | tf_op jit(solution)/shard_map/broadcast_in_dim | solution.py:151
  68.3 4.5 %all-to-all-start.1 = ((bf16[4,512,512]{2,1,0:T(8,128)(2,1)}), bf16[4,512,512]{2,1,0:T(8,128)(2,1)S(1)}, u32[]{:S(2)}, u32[]{:S(2)}) async-start(bf16[4,512,512]{2,1,0:T(8,128)(2,1)} %broadcast_in_dim.10), calls=%async_computation.1 | async-start | bytes 4194304 | tf_op jit(solution)/shard_map/all_to_all | solution.py:159
  72.7 4.5 %collective-permute-start.2 = (bf16[512,512]{1,0:T(8,128)(2,1)S(1)}, bf16[512,512]{1,0:T(8,128)(2,1)S(1)}, u32[]{:S(2)}, u32[]{:S(2)}) collective-permute-start(bf16[512,512]{1,0:T(8,128)(2,1)S(1)} %all_gather.6), channel_id=1, source_target_pairs={{0,1},{1,2},{2,3},{3,0},{4,5},{5,6},{6,7},{7,4},{8,9},{9,10},{10,1... | collective-permute-start | bytes 1572872 | tf_op jit(solution)/shard_map/ppermute | solution.py:136
  77.2 3.1 %collective-permute-start.1 = (bf16[512,512]{1,0:T(8,128)(2,1)S(1)}, bf16[512,512]{1,0:T(8,128)(2,1)}, u32[]{:S(2)}, u32[]{:S(2)}) collective-permute-start(bf16[512,512]{1,0:T(8,128)(2,1)S(1)} %all_gather.6), channel_id=1, source_target_pairs={{0,3},{1,0},{2,1},{3,2},{4,7},{5,4},{6,5},{7,6},{8,11},{9,8},{10,9... | collective-permute-start | bytes 1572872 | tf_op jit(solution)/shard_map/ppermute | solution.py:136
  80.3 4.9 %collective-permute-done.2 = bf16[512,512]{1,0:T(8,128)(2,1)S(1)} collective-permute-done((bf16[512,512]{1,0:T(8,128)(2,1)S(1)}, bf16[512,512]{1,0:T(8,128)(2,1)S(1)}, u32[]{:S(2)}, u32[]{:S(2)}) %collective-permute-start.2) | collective-permute-done | bytes 524320 | tf_op jit(solution)/shard_map/ppermute | solution.py:136
  85.3 2.4 %collective-permute-done.1 = bf16[512,512]{1,0:T(8,128)(2,1)} collective-permute-done((bf16[512,512]{1,0:T(8,128)(2,1)S(1)}, bf16[512,512]{1,0:T(8,128)(2,1)}, u32[]{:S(2)}, u32[]{:S(2)}) %collective-permute-start.1) | collective-permute-done | bytes 524320 | tf_op jit(solution)/shard_map/ppermute | solution.py:136
  87.7 7.1 %all-to-all-done.1.near_ref = bf16[4,512,512]{2,1,0:T(8,128)(2,1)S(1)} async-done(((bf16[4,512,512]{2,1,0:T(8,128)(2,1)}), bf16[4,512,512]{2,1,0:T(8,128)(2,1)S(1)}, u32[]{:S(2)}, u32[]{:S(2)}) %all-to-all-start.1) | async-done | bytes 2097184 | tf_op jit(solution)/shard_map/all_to_all | solution.py:159
  94.7 7.2 %collective-permute-start.5 = (bf16[4,512,512]{2,1,0:T(8,128)(2,1)S(1)}, bf16[4,512,512]{2,1,0:T(8,128)(2,1)}, u32[]{:S(2)}, u32[]{:S(2)}) collective-permute-start(bf16[4,512,512]{2,1,0:T(8,128)(2,1)S(1)} %all-to-all-done.1.near_ref), channel_id=1, source_target_pairs={{0,16},{16,0},{1,17},{17,1},{2,18},{18,2},{3,19},{19,3},{4,20},{20... | collective-permute-start | bytes 6291464 | tf_op jit(solution)/shard_map/ppermute | solution.py:155
  102.0 4.5 %collective-permute-start.4 = (bf16[256,512]{1,0:T(8,128)(2,1)S(1)}, bf16[256,512]{1,0:T(8,128)(2,1)S(1)}, u32[]{:S(2)}, u32[]{:S(2)}) collective-permute-start(bf16[256,512]{1,0:T(8,128)(2,1)S(1)} %slice.9), channel_id=1, source_target_pairs={{0,1},{1,2},{2,3},{3,0},{4,5},{5,6},{6,7},{7,4},{8,9},{9,10},{10,1... | collective-permute-start | bytes 786440 | tf_op jit(solution)/shard_map/ppermute | solution.py:136
  106.5 1.0 slice.8
  107.4 3.1 %collective-permute-start.3 = (bf16[256,512]{1,0:T(8,128)(2,1)S(1)}, bf16[256,512]{1,0:T(8,128)(2,1)S(1)}, u32[]{:S(2)}, u32[]{:S(2)}) collective-permute-start(bf16[256,512]{1,0:T(8,128)(2,1)S(1)} %slice.8), channel_id=1, source_target_pairs={{0,3},{1,0},{2,1},{3,2},{4,7},{5,4},{6,5},{7,6},{8,11},{9,8},{10,9... | collective-permute-start | bytes 786440 | tf_op jit(solution)/shard_map/ppermute | solution.py:136
  110.7 1.1 constant_dynamic-update-slice_fusion.3
  111.8 2.4 %collective-permute-done.4 = bf16[256,512]{1,0:T(8,128)(2,1)S(1)} collective-permute-done((bf16[256,512]{1,0:T(8,128)(2,1)S(1)}, bf16[256,512]{1,0:T(8,128)(2,1)S(1)}, u32[]{:S(2)}, u32[]{:S(2)}) %collective-permute-start.4) | collective-permute-done | bytes 262176 | tf_op jit(solution)/shard_map/ppermute | solution.py:136
  114.2 3.1 %collective-permute-done.3 = bf16[256,512]{1,0:T(8,128)(2,1)S(1)} collective-permute-done((bf16[256,512]{1,0:T(8,128)(2,1)S(1)}, bf16[256,512]{1,0:T(8,128)(2,1)S(1)}, u32[]{:S(2)}, u32[]{:S(2)}) %collective-permute-start.3) | collective-permute-done | bytes 262176 | tf_op jit(solution)/shard_map/ppermute | solution.py:136
  117.4 5.9 %hessian.1 = f32[512,1024]{1,0:T(8,128)} custom-call(s32[1]{0:T(128)} %bitcast.5.s_ref, bf16[2048,512]{1,0:T(8,128)(2,1)S(1)} %constant_dynamic-update-slice_fusion.rows_ref, bf16[4,512,512]{2,1,0:T(8,128)(2,1)S(1)} %all-to-all-done.1.near_ref, bf16[4,512,512]{2,1,0:T(8,128)(2,1)} %collective-permute-done.5.far_ref), custom_call_target="tpu_custom_call" | custom-call | tf_op jit(solution)/shard_map/hessian/pallas_call | solution.py:115
  (9 shorter events, 0.4 us)
Async XLA Ops:
  2.2 10.5 %all-to-all-start = ((bf16[4,272,128]{2,1,0:T(8,128)(2,1)}), bf16[4,272,128]{2,1,0:T(8,128)(2,1)S(1)}, u32[]{:S(2)}, u32[]{:S(2)}) async-start(bf16[4,272,128]{2,1,0:T(8,128)(2,1)} %pack.1), calls=%async_computation | async-start | bytes 557056 | tf_op jit(solution)/shard_map/all_to_all | solution.py:159
  14.5 34.3 %collective-permute-start = (bf16[128,512]{1,0:T(8,128)(2,1)}, bf16[128,512]{1,0:T(8,128)(2,1)S(1)}, u32[]{:S(2)}, u32[]{:S(2)}) collective-permute-start(bf16[128,512]{1,0:T(8,128)(2,1)} %attend.1), channel_id=1, source_target_pairs={{0,0},{1,32},{2,64},{3,96},{4,256},{5,288},{6,320},{7,352},{8,384}... | collective-permute-start | bytes 393224 | tf_op jit(solution)/shard_map/ppermute | solution.py:167
  68.3 26.5 %all-to-all-start.1 = ((bf16[4,512,512]{2,1,0:T(8,128)(2,1)}), bf16[4,512,512]{2,1,0:T(8,128)(2,1)S(1)}, u32[]{:S(2)}, u32[]{:S(2)}) async-start(bf16[4,512,512]{2,1,0:T(8,128)(2,1)} %broadcast_in_dim.10), calls=%async_computation.1 | async-start | bytes 4194304 | tf_op jit(solution)/shard_map/all_to_all | solution.py:159
  72.7 12.5 %collective-permute-start.2 = (bf16[512,512]{1,0:T(8,128)(2,1)S(1)}, bf16[512,512]{1,0:T(8,128)(2,1)S(1)}, u32[]{:S(2)}, u32[]{:S(2)}) collective-permute-start(bf16[512,512]{1,0:T(8,128)(2,1)S(1)} %all_gather.6), channel_id=1, source_target_pairs={{0,1},{1,2},{2,3},{3,0},{4,5},{5,6},{6,7},{7,4},{8,9},{9,10},{10,1... | collective-permute-start | bytes 1572872 | tf_op jit(solution)/shard_map/ppermute | solution.py:136
  77.2 10.4 %collective-permute-start.1 = (bf16[512,512]{1,0:T(8,128)(2,1)S(1)}, bf16[512,512]{1,0:T(8,128)(2,1)}, u32[]{:S(2)}, u32[]{:S(2)}) collective-permute-start(bf16[512,512]{1,0:T(8,128)(2,1)S(1)} %all_gather.6), channel_id=1, source_target_pairs={{0,3},{1,0},{2,1},{3,2},{4,7},{5,4},{6,5},{7,6},{8,11},{9,8},{10,9... | collective-permute-start | bytes 1572872 | tf_op jit(solution)/shard_map/ppermute | solution.py:136
  94.7 22.6 %collective-permute-start.5 = (bf16[4,512,512]{2,1,0:T(8,128)(2,1)S(1)}, bf16[4,512,512]{2,1,0:T(8,128)(2,1)}, u32[]{:S(2)}, u32[]{:S(2)}) collective-permute-start(bf16[4,512,512]{2,1,0:T(8,128)(2,1)S(1)} %all-to-all-done.1.near_ref), channel_id=1, source_target_pairs={{0,16},{16,0},{1,17},{17,1},{2,18},{18,2},{3,19},{19,3},{4,20},{20... | collective-permute-start | bytes 6291464 | tf_op jit(solution)/shard_map/ppermute | solution.py:155
  102.0 12.3 %collective-permute-start.4 = (bf16[256,512]{1,0:T(8,128)(2,1)S(1)}, bf16[256,512]{1,0:T(8,128)(2,1)S(1)}, u32[]{:S(2)}, u32[]{:S(2)}) collective-permute-start(bf16[256,512]{1,0:T(8,128)(2,1)S(1)} %slice.9), channel_id=1, source_target_pairs={{0,1},{1,2},{2,3},{3,0},{4,5},{5,6},{6,7},{7,4},{8,9},{9,10},{10,1... | collective-permute-start | bytes 786440 | tf_op jit(solution)/shard_map/ppermute | solution.py:136
  107.4 9.9 %collective-permute-start.3 = (bf16[256,512]{1,0:T(8,128)(2,1)S(1)}, bf16[256,512]{1,0:T(8,128)(2,1)S(1)}, u32[]{:S(2)}, u32[]{:S(2)}) collective-permute-start(bf16[256,512]{1,0:T(8,128)(2,1)S(1)} %slice.8), channel_id=1, source_target_pairs={{0,3},{1,0},{2,1},{3,2},{4,7},{5,4},{6,5},{7,6},{8,11},{9,8},{10,9... | collective-permute-start | bytes 786440 | tf_op jit(solution)/shard_map/ppermute | solution.py:136

commit v10 on v8

--- a/solution.py
+++ b/solution.py
@@ -125,24 +125,22 @@
     )(*args)
 
 
-def turn(value, axis, by):
-    at = lambda core, i: core * RING + i if axis == "x" else i * 2 + core
-    axes = ("core", axis) if axis == "x" else (axis, "core")
-    steps = ((0, by), (1, -by))
-    pairs = [(at(c, i), at(c, (i + d) % RING)) for c, d in steps for i in range(RING)]
-    return lax.ppermute(value, axes, pairs)
+def shift(value, axis, by):
+    return lax.ppermute(value, axis, [(i, (i + by) % RING) for i in range(RING)])
 
 
-def joined(axis, own, got, across):
+def joined(axis, pieces):
     me = lax.axis_index(axis)
-    ahead = jnp.where(lax.axis_index("core") == 0, RING - 1, 1)
-    depth, width = own.shape
-    slots = (me, me + ahead, me - ahead, me + 2, me + 2)
-    whole = jnp.zeros((RING * depth, width), own.dtype)
-    for slot, piece, shift in zip(slots, (own, *got, *across), (0, 0, 0, 0, depth // 2)):
-        start = (slot & (RING - 1)) * depth + shift
+    depth, width = pieces[0].shape
+    whole = jnp.zeros((RING * depth, width), pieces[0].dtype)
+    for ahead, piece in enumerate(pieces):
+        start = ((me + ahead) & (RING - 1)) * depth
         whole = lax.dynamic_update_slice(whole, piece, (start, 0))
     return whole
+
+
+def copies(value):
+    return jnp.broadcast_to(value[None], (RING,) + value.shape)
 
 
 def swap_cores(value):
@@ -176,17 +174,12 @@
     landed = [[place * RING + group for place in LANDING[group]] for group in range(RING)]
     cols = lax.all_gather(chunk, ("zl", "zh"), axis=0, tiled=True, axis_index_groups=landed)
     cols, rows = lax.optimization_barrier((cols, rows))
-    ways = ((rows, "x"), (cols, "y"))
-    got = [[turn(v, axis, by) for v, axis in ways] for by in (1, -1)]
-    half = rows.shape[0] // 2
-    cut = lax.optimization_barrier([[v[:half] for v in got[0]], [v[half:] for v in got[1]]])
-    across = [[turn(v, "xy"[k], by) for k, v in enumerate(c)] for c, by in zip(cut, (1, -1))]
-    rows, near = (
-        joined("xy"[k], v, (got[0][k], got[1][k]), (across[0][k], across[1][k]))
-        for k, v in enumerate((rows, cols))
-    )
-    near, rows = lax.optimization_barrier((near, rows))
+    near = exchange(copies(cols), "y")
+    pieces = [shift(rows, "x", -ahead) for ahead in (2, 1, 3)]
+    near, opposite, after, before = lax.optimization_barrier((near, *pieces))
     far = swap_cores(near)
+    rows = joined("x", (rows, after, opposite, before))
+    near, far = (v.reshape(-1, v.shape[2]) for v in (near, far))
     core = lax.axis_index("core").astype(jnp.int32).reshape(1)
     hessian = hessian_half(core, rows, near)
     hessian = hessian_half(1 - core, rows, far, hessian)

time: 127 us -> 115 us (0.906)
  starting transfers between devices: 38.2 us -> 29 us
  waiting for transfers between devices: 24.8 us -> 17.5 us
  local copies, waits for them, and re-layouts: 2.61 us -> 6.39 us
    ppermute x8 -> x3, starting transfers between devices: 23.9 us -> 11.6 us  [shift(): lax.ppermute(value, axis, [(i, (i + by) % RING) for i in range(RING)])]
    ppermute x8 -> x3, waiting for transfers between devices: 19.8 us -> 13.8 us  [shift(): lax.ppermute(value, axis, [(i, (i + by) % RING) for i in range(RING)])]
    all_to_all x1 -> x2, starting transfers between devices: 4.84 us -> 8.75 us  [exchange(): return lax.all_to_all(value, axis, split_axis=0, concat_axis=0, tiled=True)]
    unnamed x1 -> x5, local copies, waits for them, and re-layouts: 1.02 us -> 2.66 us
    broadcast_in_dim x0 -> x2, local copies, waits for them, and re-layouts: none -> 1.62 us  [the longest x1 1.48 us: copies(): return jnp.broadcast_to(value[None], (RING,) + value.shape)]
    all_to_all x1 -> x2, waiting for transfers between devices: 3.69 us -> 3.69 us  [exchange(): return lax.all_to_all(value, axis, split_axis=0, concat_axis=0, tiled=True)]
  transfers between devices with their start and end apart: 11 -> 7, of which waited for: 8 -> 4; matrix products, arithmetic and copies ran while one was open for 2% -> 3% of each run, Pallas kernels for 2% -> 2%
where the time goes in v10:
time: 115 us; the launch traced here: 114 us
  blocking collectives  51.4 us (45%)
  starting transfers between devices  29 us (25%)
  waiting for transfers between devices  17.5 us (15%)
  Pallas kernels  9.42 us (8%)
  local copies, waits for them, and re-layouts  6.39 us (6%)
    all_gather x1, blocking collectives, on_device(): rows = lax.all_gather(attended, 'zh', axis=0, tiled=True)  32.7 us
    all_gather x1, blocking collectives, on_device(): lax.all_gather(chunk, ('zl', 'zh'), axis=0, tiled=True, axis_index_groups...  18.7 us
    ppermute x3, waiting for transfers between devices, shift(): lax.ppermute(value, axis, [(i, (i + by) % RING) for i in range(RING)])  13.8 us
    ppermute x3, starting transfers between devices, shift(): lax.ppermute(value, axis, [(i, (i + by) % RING) for i in range(RING)])  11.6 us
    all_to_all x2, starting transfers between devices, exchange(): return lax.all_to_all(value, axis, split_axis=0, concat_axis=0, tiled=True)  8.75 us
    ppermute x1, starting transfers between devices, swap_cores(): return lax.ppermute(value, 'core', [(0, 1), (1, 0)])  7.1 us
    pallas_call x2, Pallas kernels, hessian_half(): pl.pallas_call(half_kernel, out_shape=jax.ShapeDtypeStruct((width, 2 * ha...  6.04 us
    all_to_all x2, waiting for transfers between devices, exchange(): return lax.all_to_all(value, axis, split_axis=0, concat_axis=0, tiled=True)  3.69 us
  transfers between devices with their start and end apart: 7, of which 4 were waited for; matrix products, arithmetic and copies ran while one was open for 3% of the time, Pallas kernels for 2%

profile of v10, /device:TPU:1, one launch (start us, length us, event | category | flops | bytes accessed | tf_op | source)
XLA Modules:
  0.0 114.4 jit_solution(7469092264701989482)
XLA Ops:
  0.7 1.5 %pack.1 = bf16[4,272,128]{2,1,0:T(8,128)(2,1)} custom-call(s32[1]{0:T(128)} %bitcast.2.g_ref, bf16[128,1024]{1,0:T(8,128)(2,1)} %k_ref.1, bf16[128,1024]{1,0:T(8,128)(2,1)} %v_ref.1, s32[1,128]{1,0:T(1,128)} %bitcast.11), custom_call_target="tpu_custom_call" | custom-call | tf_op jit(solution)/shard_map/pack/pallas_call | solution.py:37
  2.2 4.8 %all-to-all-start = ((bf16[4,272,128]{2,1,0:T(8,128)(2,1)}), bf16[4,272,128]{2,1,0:T(8,128)(2,1)S(1)}, u32[]{:S(2)}, u32[]{:S(2)}) async-start(bf16[4,272,128]{2,1,0:T(8,128)(2,1)} %pack.1), calls=%async_computation | async-start | bytes 557056 | tf_op jit(solution)/shard_map/all_to_all | solution.py:151
  7.0 1.0 copy.8
  8.2 0.8 copy.10.p_ref
  9.0 3.7 %all-to-all-done.kv_ref = bf16[4,272,128]{2,1,0:T(8,128)(2,1)S(1)} async-done(((bf16[4,272,128]{2,1,0:T(8,128)(2,1)}), bf16[4,272,128]{2,1,0:T(8,128)(2,1)S(1)}, u32[]{:S(2)}, u32[]{:S(2)}) %all-to-all-start) | async-done | bytes 278560 | tf_op jit(solution)/shard_map/all_to_all | solution.py:151
  12.6 1.8 %attend.1 = bf16[128,512]{1,0:T(8,128)(2,1)} custom-call(bf16[4,128,128]{2,1,0:T(8,128)(2,1)S(1)} %bitcast.9, bf16[4,272,128]{2,1,0:T(8,128)(2,1)S(1)} %all-to-all-done.kv_ref, s32[128,1]{1,0:T(8,128)S(1)} %copy.10.p_ref), custom_call_target="tpu_custom_call" | custom-call | tf_op jit(solution)/shard_map/attend/pallas_call | solution.py:81
  14.5 1.6 %collective-permute-start = (bf16[128,512]{1,0:T(8,128)(2,1)}, bf16[128,512]{1,0:T(8,128)(2,1)S(1)}, u32[]{:S(2)}, u32[]{:S(2)}) collective-permute-start(bf16[128,512]{1,0:T(8,128)(2,1)} %attend.1), channel_id=1, source_target_pairs={{0,0},{1,32},{2,64},{3,96},{4,256},{5,288},{6,320},{7,352},{8,384}... | collective-permute-start | bytes 393224 | tf_op jit(solution)/shard_map/ppermute | solution.py:159
  16.0 32.7 %all_gather.6 = bf16[512,512]{1,0:T(8,128)(2,1)S(1)} all-gather(bf16[128,512]{1,0:T(8,128)(2,1)} %attend.1), channel_id=1, replica_groups=mesh['zl'=4,'y'=4,'core'=2,'zh'=4,'x'=4] {'zh'}, dimensions={0}, use_global_device_ids=true | all-gather | bytes 655360 | tf_op jit(solution)/shard_map/all_gather | solution.py:172
  48.8 18.7 %all_gather.7 = bf16[512,512]{1,0:T(8,128)(2,1)S(1)} all-gather(bf16[128,512]{1,0:T(8,128)(2,1)S(1)} %collective-permute-done), channel_id=1, replica_groups={{0,256,384,128},{132,388,260,4},{392,136,8,264},{268,12,140,396},{1,257..., dimensions={0}, use_global_device_ids=true | all-gather | bytes 655360 | tf_op jit(solution)/shard_map/all_gather | solution.py:175
  67.4 1.5 %broadcast_in_dim.10 = bf16[4,512,512]{2,1,0:T(8,128)(2,1)} broadcast(bf16[512,512]{1,0:T(8,128)(2,1)S(1)} %all_gather.7), dimensions={1,2} | broadcast | bytes 2621440 | tf_op jit(solution)/shard_map/broadcast_in_dim | solution.py:143
  68.9 3.9 %all-to-all-start.1 = ((bf16[4,512,512]{2,1,0:T(8,128)(2,1)}), bf16[4,512,512]{2,1,0:T(8,128)(2,1)S(1)}, u32[]{:S(2)}, u32[]{:S(2)}) async-start(bf16[4,512,512]{2,1,0:T(8,128)(2,1)} %broadcast_in_dim.10), calls=%async_computation.1 | async-start | bytes 4194304 | tf_op jit(solution)/shard_map/all_to_all | solution.py:151
  72.8 6.3 %collective-permute-start.1 = (bf16[512,512]{1,0:T(8,128)(2,1)S(1)}, bf16[512,512]{1,0:T(8,128)(2,1)S(1)}, u32[]{:S(2)}, u32[]{:S(2)}) collective-permute-start(bf16[512,512]{1,0:T(8,128)(2,1)S(1)} %all_gather.6), channel_id=1, source_target_pairs={{0,2},{1,3},{2,0},{3,1},{4,6},{5,7},{6,4},{7,5},{8,10},{9,11},{10,... | collective-permute-start | bytes 1572872 | tf_op jit(solution)/shard_map/ppermute | solution.py:129
  79.1 1.9 %collective-permute-start.2 = (bf16[512,512]{1,0:T(8,128)(2,1)S(1)}, bf16[512,512]{1,0:T(8,128)(2,1)S(1)}, u32[]{:S(2)}, u32[]{:S(2)}) collective-permute-start(bf16[512,512]{1,0:T(8,128)(2,1)S(1)} %all_gather.6), channel_id=1, source_target_pairs={{0,3},{1,0},{2,1},{3,2},{4,7},{5,4},{6,5},{7,6},{8,11},{9,8},{10,9... | collective-permute-start | bytes 1572872 | tf_op jit(solution)/shard_map/ppermute | solution.py:129
  81.1 3.4 %collective-permute-start.3 = (bf16[512,512]{1,0:T(8,128)(2,1)S(1)}, bf16[512,512]{1,0:T(8,128)(2,1)}, u32[]{:S(2)}, u32[]{:S(2)}) collective-permute-start(bf16[512,512]{1,0:T(8,128)(2,1)S(1)} %all_gather.6), channel_id=1, source_target_pairs={{0,1},{1,2},{2,3},{3,0},{4,5},{5,6},{6,7},{7,4},{8,9},{9,10},{10,1... | collective-permute-start | bytes 1572872 | tf_op jit(solution)/shard_map/ppermute | solution.py:129
  84.4 1.3 %collective-permute-done.1 = bf16[512,512]{1,0:T(8,128)(2,1)S(1)} collective-permute-done((bf16[512,512]{1,0:T(8,128)(2,1)S(1)}, bf16[512,512]{1,0:T(8,128)(2,1)S(1)}, u32[]{:S(2)}, u32[]{:S(2)}) %collective-permute-start.1) | collective-permute-done | bytes 524320 | tf_op jit(solution)/shard_map/ppermute | solution.py:129
  85.7 12.4 %collective-permute-done.2 = bf16[512,512]{1,0:T(8,128)(2,1)S(1)} collective-permute-done((bf16[512,512]{1,0:T(8,128)(2,1)S(1)}, bf16[512,512]{1,0:T(8,128)(2,1)S(1)}, u32[]{:S(2)}, u32[]{:S(2)}) %collective-permute-start.2) | collective-permute-done | bytes 524320 | tf_op jit(solution)/shard_map/ppermute | solution.py:129
  98.1 0.8 copy-done
  98.9 0.2 collective-permute-done.3
  99.0 7.1 %collective-permute-start.4 = (bf16[4,512,512]{2,1,0:T(8,128)(2,1)S(1)}, bf16[4,512,512]{2,1,0:T(8,128)(2,1)}, u32[]{:S(2)}, u32[]{:S(2)}) collective-permute-start(bf16[4,512,512]{2,1,0:T(8,128)(2,1)S(1)} %all-to-all-done.1), channel_id=1, source_target_pairs={{0,16},{16,0},{1,17},{17,1},{2,18},{18,2},{3,19},{19,3},{4,20},{20... | collective-permute-start | bytes 6291464 | tf_op jit(solution)/shard_map/ppermute | solution.py:147
  106.2 0.1 broadcast_in_dim.4
  106.4 0.8 copy-done.1
  107.3 1.1 constant_dynamic-update-slice_fusion.rows_ref
  108.4 2.5 %hessian_half.2.rest_0_ = f32[512,1024]{1,0:T(8,128)} custom-call(s32[1]{0:T(128)} %bitcast.5.s_ref, bf16[2048,512]{1,0:T(8,128)(2,1)S(1)} %constant_dynamic-update-slice_fusion.rows_ref, bf16[2048,512]{1,0:T(8,128)(2,1)S(1)} %bitcast.8), custom_call_target="tpu_custom_call" | custom-call | tf_op jit(solution)/shard_map/hessian_half/pallas_call | solution.py:113
  110.9 3.5 %hessian_half.3 = f32[512,1024]{1,0:T(8,128)} custom-call(s32[1]{0:T(128)S(6)} %sub.8.s_ref, bf16[2048,512]{1,0:T(8,128)(2,1)S(1)} %constant_dynamic-update-slice_fusion.rows_ref, bf16[2048,512]{1,0:T(8,128)(2,1)} %bitcast.6.cols_ref, f32[512,1024]{1,0:T(8,128)} %hessian_half.2.rest_0_), custom_call_target="tpu_custom_call", output_to_operand_aliasing={{}: (3, {})} | custom-call | tf_op jit(solution)/shard_map/hessian_half/pallas_call | solution.py:113
  (9 shorter events, 0.3 us)
Async XLA Ops:
  2.2 10.5 %all-to-all-start = ((bf16[4,272,128]{2,1,0:T(8,128)(2,1)}), bf16[4,272,128]{2,1,0:T(8,128)(2,1)S(1)}, u32[]{:S(2)}, u32[]{:S(2)}) async-start(bf16[4,272,128]{2,1,0:T(8,128)(2,1)} %pack.1), calls=%async_computation | async-start | bytes 557056 | tf_op jit(solution)/shard_map/all_to_all | solution.py:151
  14.5 34.3 %collective-permute-start = (bf16[128,512]{1,0:T(8,128)(2,1)}, bf16[128,512]{1,0:T(8,128)(2,1)S(1)}, u32[]{:S(2)}, u32[]{:S(2)}) collective-permute-start(bf16[128,512]{1,0:T(8,128)(2,1)} %attend.1), channel_id=1, source_target_pairs={{0,0},{1,32},{2,64},{3,96},{4,256},{5,288},{6,320},{7,352},{8,384}... | collective-permute-start | bytes 393224 | tf_op jit(solution)/shard_map/ppermute | solution.py:159
  68.9 30.1 %all-to-all-start.1 = ((bf16[4,512,512]{2,1,0:T(8,128)(2,1)}), bf16[4,512,512]{2,1,0:T(8,128)(2,1)S(1)}, u32[]{:S(2)}, u32[]{:S(2)}) async-start(bf16[4,512,512]{2,1,0:T(8,128)(2,1)} %broadcast_in_dim.10), calls=%async_computation.1 | async-start | bytes 4194304 | tf_op jit(solution)/shard_map/all_to_all | solution.py:151
  72.8 12.9 %collective-permute-start.1 = (bf16[512,512]{1,0:T(8,128)(2,1)S(1)}, bf16[512,512]{1,0:T(8,128)(2,1)S(1)}, u32[]{:S(2)}, u32[]{:S(2)}) collective-permute-start(bf16[512,512]{1,0:T(8,128)(2,1)S(1)} %all_gather.6), channel_id=1, source_target_pairs={{0,2},{1,3},{2,0},{3,1},{4,6},{5,7},{6,4},{7,5},{8,10},{9,11},{10,... | collective-permute-start | bytes 1572872 | tf_op jit(solution)/shard_map/ppermute | solution.py:129
  79.1 18.9 %collective-permute-start.2 = (bf16[512,512]{1,0:T(8,128)(2,1)S(1)}, bf16[512,512]{1,0:T(8,128)(2,1)S(1)}, u32[]{:S(2)}, u32[]{:S(2)}) collective-permute-start(bf16[512,512]{1,0:T(8,128)(2,1)S(1)} %all_gather.6), channel_id=1, source_target_pairs={{0,3},{1,0},{2,1},{3,2},{4,7},{5,4},{6,5},{7,6},{8,11},{9,8},{10,9... | collective-permute-start | bytes 1572872 | tf_op jit(solution)/shard_map/ppermute | solution.py:129
  81.1 18.0 %collective-permute-start.3 = (bf16[512,512]{1,0:T(8,128)(2,1)S(1)}, bf16[512,512]{1,0:T(8,128)(2,1)}, u32[]{:S(2)}, u32[]{:S(2)}) collective-permute-start(bf16[512,512]{1,0:T(8,128)(2,1)S(1)} %all_gather.6), channel_id=1, source_target_pairs={{0,1},{1,2},{2,3},{3,0},{4,5},{5,6},{6,7},{7,4},{8,9},{9,10},{10,1... | collective-permute-start | bytes 1572872 | tf_op jit(solution)/shard_map/ppermute | solution.py:129
  98.1 0.8 copy-start
  99.0 11.8 %collective-permute-start.4 = (bf16[4,512,512]{2,1,0:T(8,128)(2,1)S(1)}, bf16[4,512,512]{2,1,0:T(8,128)(2,1)}, u32[]{:S(2)}, u32[]{:S(2)}) collective-permute-start(bf16[4,512,512]{2,1,0:T(8,128)(2,1)S(1)} %all-to-all-done.1), channel_id=1, source_target_pairs={{0,16},{16,0},{1,17},{17,1},{2,18},{18,2},{3,19},{19,3},{4,20},{20... | collective-permute-start | bytes 6291464 | tf_op jit(solution)/shard_map/ppermute | solution.py:147
  106.2 1.0 copy-start.1

commit v11 on v10

--- a/solution.py
+++ b/solution.py
@@ -176,9 +176,10 @@
     cols, rows = lax.optimization_barrier((cols, rows))
     near = exchange(copies(cols), "y")
     pieces = [shift(rows, "x", -ahead) for ahead in (2, 1, 3)]
-    near, opposite, after, before = lax.optimization_barrier((near, *pieces))
+    opposite, after, before = pieces
+    rows = joined("x", (rows, after, opposite, before))
+    near, rows = lax.optimization_barrier((near, rows))
     far = swap_cores(near)
-    rows = joined("x", (rows, after, opposite, before))
     near, far = (v.reshape(-1, v.shape[2]) for v in (near, far))
     core = lax.axis_index("core").astype(jnp.int32).reshape(1)
     hessian = hessian_half(core, rows, near)

time: 115 us -> 117 us (1.017)
  waiting for transfers between devices: 17.5 us -> 21 us
    ppermute x3, waiting for transfers between devices: 13.8 us -> 16.9 us  [shift(): lax.ppermute(value, axis, [(i, (i + by) % RING) for i in range(RING)])]
    unnamed x5 -> x1, local copies, waits for them, and re-layouts: 2.66 us -> 1.02 us
  transfers between devices with their start and end apart: 7 -> 7, of which waited for: 4 -> 5; matrix products, arithmetic and copies ran while one was open for 3% -> 4% of each run, Pallas kernels for 2% -> 3%
where the time goes in v11:
time: 117 us
  blocking collectives  51.4 us (44%)
  starting transfers between devices  28.3 us (24%)
  waiting for transfers between devices  21 us (18%)
  Pallas kernels  9.41 us (8%)
  local copies, waits for them, and re-layouts  5.77 us (5%)
    all_gather x1, blocking collectives, on_device(): rows = lax.all_gather(attended, 'zh', axis=0, tiled=True)  32.7 us
    all_gather x1, blocking collectives, on_device(): lax.all_gather(chunk, ('zl', 'zh'), axis=0, tiled=True, axis_index_groups...  18.7 us
    ppermute x3, waiting for transfers between devices, shift(): lax.ppermute(value, axis, [(i, (i + by) % RING) for i in range(RING)])  16.9 us
    ppermute x3, starting transfers between devices, shift(): lax.ppermute(value, axis, [(i, (i + by) % RING) for i in range(RING)])  11.3 us
    all_to_all x2, starting transfers between devices, exchange(): return lax.all_to_all(value, axis, split_axis=0, concat_axis=0, tiled=True)  9.3 us
    ppermute x1, starting transfers between devices, swap_cores(): return lax.ppermute(value, 'core', [(0, 1), (1, 0)])  6.19 us
    pallas_call x2, Pallas kernels, hessian_half(): pl.pallas_call(half_kernel, out_shape=jax.ShapeDtypeStruct((width, 2 * ha...  6.04 us
    all_to_all x2, waiting for transfers between devices, exchange(): return lax.all_to_all(value, axis, split_axis=0, concat_axis=0, tiled=True)  3.69 us
  transfers between devices with their start and end apart: 7, of which 5 were waited for; matrix products, arithmetic and copies ran while one was open for 4% of the time, Pallas kernels for 3%

profile of v11, /device:TPU:1, one launch (start us, length us, event | category | flops | bytes accessed | tf_op | source)
XLA Modules:
  0.0 116.7 jit_solution(13405034345932941773)
XLA Ops:
  0.7 1.5 %pack.1 = bf16[4,272,128]{2,1,0:T(8,128)(2,1)} custom-call(s32[1]{0:T(128)} %bitcast.2.g_ref, bf16[128,1024]{1,0:T(8,128)(2,1)} %k_ref.1, bf16[128,1024]{1,0:T(8,128)(2,1)} %v_ref.1, s32[1,128]{1,0:T(1,128)} %bitcast.11), custom_call_target="tpu_custom_call" | custom-call | tf_op jit(solution)/shard_map/pack/pallas_call | solution.py:37
  2.2 4.8 %all-to-all-start = ((bf16[4,272,128]{2,1,0:T(8,128)(2,1)}), bf16[4,272,128]{2,1,0:T(8,128)(2,1)S(1)}, u32[]{:S(2)}, u32[]{:S(2)}) async-start(bf16[4,272,128]{2,1,0:T(8,128)(2,1)} %pack.1), calls=%async_computation | async-start | bytes 557056 | tf_op jit(solution)/shard_map/all_to_all | solution.py:151
  7.0 1.0 copy.8
  8.2 0.8 copy.10.p_ref
  9.0 3.7 %all-to-all-done.kv_ref = bf16[4,272,128]{2,1,0:T(8,128)(2,1)S(1)} async-done(((bf16[4,272,128]{2,1,0:T(8,128)(2,1)}), bf16[4,272,128]{2,1,0:T(8,128)(2,1)S(1)}, u32[]{:S(2)}, u32[]{:S(2)}) %all-to-all-start) | async-done | bytes 278560 | tf_op jit(solution)/shard_map/all_to_all | solution.py:151
  12.6 1.8 %attend.1 = bf16[128,512]{1,0:T(8,128)(2,1)} custom-call(bf16[4,128,128]{2,1,0:T(8,128)(2,1)S(1)} %bitcast.9, bf16[4,272,128]{2,1,0:T(8,128)(2,1)S(1)} %all-to-all-done.kv_ref, s32[128,1]{1,0:T(8,128)S(1)} %copy.10.p_ref), custom_call_target="tpu_custom_call" | custom-call | tf_op jit(solution)/shard_map/attend/pallas_call | solution.py:81
  14.5 1.6 %collective-permute-start = (bf16[128,512]{1,0:T(8,128)(2,1)}, bf16[128,512]{1,0:T(8,128)(2,1)S(1)}, u32[]{:S(2)}, u32[]{:S(2)}) collective-permute-start(bf16[128,512]{1,0:T(8,128)(2,1)} %attend.1), channel_id=1, source_target_pairs={{0,0},{1,32},{2,64},{3,96},{4,256},{5,288},{6,320},{7,352},{8,384}... | collective-permute-start | bytes 393224 | tf_op jit(solution)/shard_map/ppermute | solution.py:159
  16.0 32.7 %all_gather.6 = bf16[512,512]{1,0:T(8,128)(2,1)S(1)} all-gather(bf16[128,512]{1,0:T(8,128)(2,1)} %attend.1), channel_id=1, replica_groups=mesh['zl'=4,'y'=4,'core'=2,'zh'=4,'x'=4] {'zh'}, dimensions={0}, use_global_device_ids=true | all-gather | bytes 655360 | tf_op jit(solution)/shard_map/all_gather | solution.py:172
  48.8 18.7 %all_gather.7 = bf16[512,512]{1,0:T(8,128)(2,1)S(1)} all-gather(bf16[128,512]{1,0:T(8,128)(2,1)S(1)} %collective-permute-done), channel_id=1, replica_groups={{0,256,384,128},{132,388,260,4},{392,136,8,264},{268,12,140,396},{1,257..., dimensions={0}, use_global_device_ids=true | all-gather | bytes 655360 | tf_op jit(solution)/shard_map/all_gather | solution.py:175
  67.4 1.5 %broadcast_in_dim.4 = bf16[4,512,512]{2,1,0:T(8,128)(2,1)} broadcast(bf16[512,512]{1,0:T(8,128)(2,1)S(1)} %all_gather.7), dimensions={1,2} | broadcast | bytes 2621440 | tf_op jit(solution)/shard_map/broadcast_in_dim | solution.py:143
  68.9 4.5 %all-to-all-start.1 = ((bf16[4,512,512]{2,1,0:T(8,128)(2,1)}), bf16[4,512,512]{2,1,0:T(8,128)(2,1)}, u32[]{:S(2)}, u32[]{:S(2)}) async-start(bf16[4,512,512]{2,1,0:T(8,128)(2,1)} %broadcast_in_dim.4), calls=%async_computation.1 | async-start | bytes 4194304 | tf_op jit(solution)/shard_map/all_to_all | solution.py:151
  73.4 5.9 %collective-permute-start.1 = (bf16[512,512]{1,0:T(8,128)(2,1)S(1)}, bf16[512,512]{1,0:T(8,128)(2,1)}, u32[]{:S(2)}, u32[]{:S(2)}) collective-permute-start(bf16[512,512]{1,0:T(8,128)(2,1)S(1)} %all_gather.6), channel_id=1, source_target_pairs={{0,3},{1,0},{2,1},{3,2},{4,7},{5,4},{6,5},{7,6},{8,11},{9,8},{10,9... | collective-permute-start | bytes 1572872 | tf_op jit(solution)/shard_map/ppermute | solution.py:129
  79.3 2.6 %collective-permute-start.2 = (bf16[512,512]{1,0:T(8,128)(2,1)S(1)}, bf16[512,512]{1,0:T(8,128)(2,1)}, u32[]{:S(2)}, u32[]{:S(2)}) collective-permute-start(bf16[512,512]{1,0:T(8,128)(2,1)S(1)} %all_gather.6), channel_id=1, source_target_pairs={{0,2},{1,3},{2,0},{3,1},{4,6},{5,7},{6,4},{7,5},{8,10},{9,11},{10,... | collective-permute-start | bytes 1572872 | tf_op jit(solution)/shard_map/ppermute | solution.py:129
  81.9 2.8 %collective-permute-start.3 = (bf16[512,512]{1,0:T(8,128)(2,1)S(1)}, bf16[512,512]{1,0:T(8,128)(2,1)S(1)}, u32[]{:S(2)}, u32[]{:S(2)}) collective-permute-start(bf16[512,512]{1,0:T(8,128)(2,1)S(1)} %all_gather.6), channel_id=1, source_target_pairs={{0,1},{1,2},{2,3},{3,0},{4,5},{5,6},{6,7},{7,4},{8,9},{9,10},{10,1... | collective-permute-start | bytes 1572872 | tf_op jit(solution)/shard_map/ppermute | solution.py:129
  84.7 0.1 broadcast_in_dim.10
  84.9 2.8 %collective-permute-done.1 = bf16[512,512]{1,0:T(8,128)(2,1)} collective-permute-done((bf16[512,512]{1,0:T(8,128)(2,1)S(1)}, bf16[512,512]{1,0:T(8,128)(2,1)}, u32[]{:S(2)}, u32[]{:S(2)}) %collective-permute-start.1) | collective-permute-done | bytes 524320 | tf_op jit(solution)/shard_map/ppermute | solution.py:129
  87.7 1.1 constant_dynamic-update-slice_fusion.2
  88.8 2.1 %collective-permute-done.2 = bf16[512,512]{1,0:T(8,128)(2,1)} collective-permute-done((bf16[512,512]{1,0:T(8,128)(2,1)S(1)}, bf16[512,512]{1,0:T(8,128)(2,1)}, u32[]{:S(2)}, u32[]{:S(2)}) %collective-permute-start.2) | collective-permute-done | bytes 524320 | tf_op jit(solution)/shard_map/ppermute | solution.py:129
  90.9 1.1 constant_dynamic-update-slice_fusion.1
  92.0 12.0 %collective-permute-done.3 = bf16[512,512]{1,0:T(8,128)(2,1)S(1)} collective-permute-done((bf16[512,512]{1,0:T(8,128)(2,1)S(1)}, bf16[512,512]{1,0:T(8,128)(2,1)S(1)}, u32[]{:S(2)}, u32[]{:S(2)}) %collective-permute-start.3) | collective-permute-done | bytes 524320 | tf_op jit(solution)/shard_map/ppermute | solution.py:129
  104.0 6.2 %collective-permute-start.4 = (bf16[4,512,512]{2,1,0:T(8,128)(2,1)}, bf16[4,512,512]{2,1,0:T(8,128)(2,1)S(1)}, u32[]{:S(2)}, u32[]{:S(2)}) collective-permute-start(bf16[4,512,512]{2,1,0:T(8,128)(2,1)} %all-to-all-done.1), channel_id=1, source_target_pairs={{0,16},{16,0},{1,17},{17,1},{2,18},{18,2},{3,19},{19,3},{4,20},{20... | collective-permute-start | bytes 6291464 | tf_op jit(solution)/shard_map/ppermute | solution.py:147
  110.2 3.6 %hessian_half.2.rest_0_ = f32[512,1024]{1,0:T(8,128)} custom-call(s32[1]{0:T(128)} %bitcast.5.s_ref, bf16[2048,512]{1,0:T(8,128)(2,1)S(1)} %constant_dynamic-update-slice_fusion.rows_ref, bf16[2048,512]{1,0:T(8,128)(2,1)} %bitcast.7.cols_ref), custom_call_target="tpu_custom_call" | custom-call | tf_op jit(solution)/shard_map/hessian_half/pallas_call | solution.py:113
  113.8 0.4 collective-permute-done.4
  114.2 2.5 %hessian_half.3 = f32[512,1024]{1,0:T(8,128)} custom-call(s32[1]{0:T(128)S(6)} %sub.8.s_ref, bf16[2048,512]{1,0:T(8,128)(2,1)S(1)} %constant_dynamic-update-slice_fusion.rows_ref, bf16[2048,512]{1,0:T(8,128)(2,1)S(1)} %bitcast.8, f32[512,1024]{1,0:T(8,128)} %hessian_half.2.rest_0_), custom_call_target="tpu_custom_call", output_to_operand_aliasing={{}: (3, {})} | custom-call | tf_op jit(solution)/shard_map/hessian_half/pallas_call | solution.py:113
  (5 shorter events, 0.2 us)
Async XLA Ops:
  2.2 10.5 %all-to-all-start = ((bf16[4,272,128]{2,1,0:T(8,128)(2,1)}), bf16[4,272,128]{2,1,0:T(8,128)(2,1)S(1)}, u32[]{:S(2)}, u32[]{:S(2)}) async-start(bf16[4,272,128]{2,1,0:T(8,128)(2,1)} %pack.1), calls=%async_computation | async-start | bytes 557056 | tf_op jit(solution)/shard_map/all_to_all | solution.py:151
  14.5 34.3 %collective-permute-start = (bf16[128,512]{1,0:T(8,128)(2,1)}, bf16[128,512]{1,0:T(8,128)(2,1)S(1)}, u32[]{:S(2)}, u32[]{:S(2)}) collective-permute-start(bf16[128,512]{1,0:T(8,128)(2,1)} %attend.1), channel_id=1, source_target_pairs={{0,0},{1,32},{2,64},{3,96},{4,256},{5,288},{6,320},{7,352},{8,384}... | collective-permute-start | bytes 393224 | tf_op jit(solution)/shard_map/ppermute | solution.py:159
  68.9 35.1 %all-to-all-start.1 = ((bf16[4,512,512]{2,1,0:T(8,128)(2,1)}), bf16[4,512,512]{2,1,0:T(8,128)(2,1)}, u32[]{:S(2)}, u32[]{:S(2)}) async-start(bf16[4,512,512]{2,1,0:T(8,128)(2,1)} %broadcast_in_dim.4), calls=%async_computation.1 | async-start | bytes 4194304 | tf_op jit(solution)/shard_map/all_to_all | solution.py:151
  73.4 14.3 %collective-permute-start.1 = (bf16[512,512]{1,0:T(8,128)(2,1)S(1)}, bf16[512,512]{1,0:T(8,128)(2,1)}, u32[]{:S(2)}, u32[]{:S(2)}) collective-permute-start(bf16[512,512]{1,0:T(8,128)(2,1)S(1)} %all_gather.6), channel_id=1, source_target_pairs={{0,3},{1,0},{2,1},{3,2},{4,7},{5,4},{6,5},{7,6},{8,11},{9,8},{10,9... | collective-permute-start | bytes 1572872 | tf_op jit(solution)/shard_map/ppermute | solution.py:129
  79.3 11.6 %collective-permute-start.2 = (bf16[512,512]{1,0:T(8,128)(2,1)S(1)}, bf16[512,512]{1,0:T(8,128)(2,1)}, u32[]{:S(2)}, u32[]{:S(2)}) collective-permute-start(bf16[512,512]{1,0:T(8,128)(2,1)S(1)} %all_gather.6), channel_id=1, source_target_pairs={{0,2},{1,3},{2,0},{3,1},{4,6},{5,7},{6,4},{7,5},{8,10},{9,11},{10,... | collective-permute-start | bytes 1572872 | tf_op jit(solution)/shard_map/ppermute | solution.py:129
  81.9 22.0 %collective-permute-start.3 = (bf16[512,512]{1,0:T(8,128)(2,1)S(1)}, bf16[512,512]{1,0:T(8,128)(2,1)S(1)}, u32[]{:S(2)}, u32[]{:S(2)}) collective-permute-start(bf16[512,512]{1,0:T(8,128)(2,1)S(1)} %all_gather.6), channel_id=1, source_target_pairs={{0,1},{1,2},{2,3},{3,0},{4,5},{5,6},{6,7},{7,4},{8,9},{9,10},{10,1... | collective-permute-start | bytes 1572872 | tf_op jit(solution)/shard_map/ppermute | solution.py:129
  104.0 10.2 %collective-permute-start.4 = (bf16[4,512,512]{2,1,0:T(8,128)(2,1)}, bf16[4,512,512]{2,1,0:T(8,128)(2,1)S(1)}, u32[]{:S(2)}, u32[]{:S(2)}) collective-permute-start(bf16[4,512,512]{2,1,0:T(8,128)(2,1)} %all-to-all-done.1), channel_id=1, source_target_pairs={{0,16},{16,0},{1,17},{17,1},{2,18},{18,2},{3,19},{19,3},{4,20},{20... | collective-permute-start | bytes 6291464 | tf_op jit(solution)/shard_map/ppermute | solution.py:147

commit v12 on v11

--- a/solution.py
+++ b/solution.py
@@ -133,9 +133,9 @@
     me = lax.axis_index(axis)
     depth, width = pieces[0].shape
     whole = jnp.zeros((RING * depth, width), pieces[0].dtype)
-    for ahead, piece in enumerate(pieces):
+    for ahead in (0, 2, 1, 3):
         start = ((me + ahead) & (RING - 1)) * depth
-        whole = lax.dynamic_update_slice(whole, piece, (start, 0))
+        whole = lax.dynamic_update_slice(whole, pieces[ahead], (start, 0))
     return whole
 
 

time: 117 us -> 114 us (0.974)
  waiting for transfers between devices: 21 us -> 16.4 us
  starting transfers between devices: 28.3 us -> 29.9 us
    ppermute x3, waiting for transfers between devices: 16.9 us -> 12.3 us  [shift(): lax.ppermute(value, axis, [(i, (i + by) % RING) for i in range(RING)])]
  transfers between devices with their start and end apart: 7 -> 7, of which waited for: 5 -> 4; matrix products, arithmetic and copies ran while one was open for 4% -> 4% of each run, Pallas kernels for 3% -> 3%
where the time goes in v12:
time: 114 us
  blocking collectives  51.4 us (45%)
  starting transfers between devices  29.9 us (26%)
  waiting for transfers between devices  16.4 us (14%)
  Pallas kernels  9.41 us (8%)
  local copies, waits for them, and re-layouts  5.78 us (5%)
    all_gather x1, blocking collectives, on_device(): rows = lax.all_gather(attended, 'zh', axis=0, tiled=True)  32.7 us
    all_gather x1, blocking collectives, on_device(): lax.all_gather(chunk, ('zl', 'zh'), axis=0, tiled=True, axis_index_groups...  18.7 us
    ppermute x3, waiting for transfers between devices, shift(): lax.ppermute(value, axis, [(i, (i + by) % RING) for i in range(RING)])  12.3 us
    ppermute x3, starting transfers between devices, shift(): lax.ppermute(value, axis, [(i, (i + by) % RING) for i in range(RING)])  11.9 us
    all_to_all x2, starting transfers between devices, exchange(): return lax.all_to_all(value, axis, split_axis=0, concat_axis=0, tiled=True)  9.3 us
    ppermute x1, starting transfers between devices, swap_cores(): return lax.ppermute(value, 'core', [(0, 1), (1, 0)])  7.12 us
    pallas_call x2, Pallas kernels, hessian_half(): pl.pallas_call(half_kernel, out_shape=jax.ShapeDtypeStruct((width, 2 * ha...  6.04 us
    all_to_all x2, waiting for transfers between devices, exchange(): return lax.all_to_all(value, axis, split_axis=0, concat_axis=0, tiled=True)  3.69 us
  transfers between devices with their start and end apart: 7, of which 4 were waited for; matrix products, arithmetic and copies ran while one was open for 4% of the time, Pallas kernels for 3%

profile of v12, /device:TPU:1, one launch (start us, length us, event | category | flops | bytes accessed | tf_op | source)
XLA Modules:
  0.0 113.6 jit_solution(15881700592718553114)
XLA Ops:
  0.7 1.5 %pack.1 = bf16[4,272,128]{2,1,0:T(8,128)(2,1)} custom-call(s32[1]{0:T(128)} %bitcast.2.g_ref, bf16[128,1024]{1,0:T(8,128)(2,1)} %k_ref.1, bf16[128,1024]{1,0:T(8,128)(2,1)} %v_ref.1, s32[1,128]{1,0:T(1,128)} %bitcast.11), custom_call_target="tpu_custom_call" | custom-call | tf_op jit(solution)/shard_map/pack/pallas_call | solution.py:37
  2.2 4.8 %all-to-all-start = ((bf16[4,272,128]{2,1,0:T(8,128)(2,1)}), bf16[4,272,128]{2,1,0:T(8,128)(2,1)S(1)}, u32[]{:S(2)}, u32[]{:S(2)}) async-start(bf16[4,272,128]{2,1,0:T(8,128)(2,1)} %pack.1), calls=%async_computation | async-start | bytes 557056 | tf_op jit(solution)/shard_map/all_to_all | solution.py:151
  7.0 1.0 copy.8
  8.0 0.1 copy.9
  8.2 0.8 copy.10.p_ref
  9.0 3.7 %all-to-all-done.kv_ref = bf16[4,272,128]{2,1,0:T(8,128)(2,1)S(1)} async-done(((bf16[4,272,128]{2,1,0:T(8,128)(2,1)}), bf16[4,272,128]{2,1,0:T(8,128)(2,1)S(1)}, u32[]{:S(2)}, u32[]{:S(2)}) %all-to-all-start) | async-done | bytes 278560 | tf_op jit(solution)/shard_map/all_to_all | solution.py:151
  12.6 1.8 %attend.1 = bf16[128,512]{1,0:T(8,128)(2,1)} custom-call(bf16[4,128,128]{2,1,0:T(8,128)(2,1)S(1)} %bitcast.9, bf16[4,272,128]{2,1,0:T(8,128)(2,1)S(1)} %all-to-all-done.kv_ref, s32[128,1]{1,0:T(8,128)S(1)} %copy.10.p_ref), custom_call_target="tpu_custom_call" | custom-call | tf_op jit(solution)/shard_map/attend/pallas_call | solution.py:81
  14.5 1.6 %collective-permute-start = (bf16[128,512]{1,0:T(8,128)(2,1)}, bf16[128,512]{1,0:T(8,128)(2,1)S(1)}, u32[]{:S(2)}, u32[]{:S(2)}) collective-permute-start(bf16[128,512]{1,0:T(8,128)(2,1)} %attend.1), channel_id=1, source_target_pairs={{0,0},{1,32},{2,64},{3,96},{4,256},{5,288},{6,320},{7,352},{8,384}... | collective-permute-start | bytes 393224 | tf_op jit(solution)/shard_map/ppermute | solution.py:159
  16.0 32.7 %all_gather.6 = bf16[512,512]{1,0:T(8,128)(2,1)S(1)} all-gather(bf16[128,512]{1,0:T(8,128)(2,1)} %attend.1), channel_id=1, replica_groups=mesh['zl'=4,'y'=4,'core'=2,'zh'=4,'x'=4] {'zh'}, dimensions={0}, use_global_device_ids=true | all-gather | bytes 655360 | tf_op jit(solution)/shard_map/all_gather | solution.py:172
  48.8 18.7 %all_gather.7 = bf16[512,512]{1,0:T(8,128)(2,1)S(1)} all-gather(bf16[128,512]{1,0:T(8,128)(2,1)S(1)} %collective-permute-done), channel_id=1, replica_groups={{0,256,384,128},{132,388,260,4},{392,136,8,264},{268,12,140,396},{1,257..., dimensions={0}, use_global_device_ids=true | all-gather | bytes 655360 | tf_op jit(solution)/shard_map/all_gather | solution.py:175
  67.4 1.5 %broadcast_in_dim.4 = bf16[4,512,512]{2,1,0:T(8,128)(2,1)} broadcast(bf16[512,512]{1,0:T(8,128)(2,1)S(1)} %all_gather.7), dimensions={1,2} | broadcast | bytes 2621440 | tf_op jit(solution)/shard_map/broadcast_in_dim | solution.py:143
  68.9 4.5 %all-to-all-start.1 = ((bf16[4,512,512]{2,1,0:T(8,128)(2,1)}), bf16[4,512,512]{2,1,0:T(8,128)(2,1)}, u32[]{:S(2)}, u32[]{:S(2)}) async-start(bf16[4,512,512]{2,1,0:T(8,128)(2,1)} %broadcast_in_dim.4), calls=%async_computation.1 | async-start | bytes 4194304 | tf_op jit(solution)/shard_map/all_to_all | solution.py:151
  73.4 6.6 %collective-permute-start.1 = (bf16[512,512]{1,0:T(8,128)(2,1)S(1)}, bf16[512,512]{1,0:T(8,128)(2,1)}, u32[]{:S(2)}, u32[]{:S(2)}) collective-permute-start(bf16[512,512]{1,0:T(8,128)(2,1)S(1)} %all_gather.6), channel_id=1, source_target_pairs={{0,2},{1,3},{2,0},{3,1},{4,6},{5,7},{6,4},{7,5},{8,10},{9,11},{10,... | collective-permute-start | bytes 1572872 | tf_op jit(solution)/shard_map/ppermute | solution.py:129
  80.0 1.9 %collective-permute-start.2 = (bf16[512,512]{1,0:T(8,128)(2,1)S(1)}, bf16[512,512]{1,0:T(8,128)(2,1)}, u32[]{:S(2)}, u32[]{:S(2)}) collective-permute-start(bf16[512,512]{1,0:T(8,128)(2,1)S(1)} %all_gather.6), channel_id=1, source_target_pairs={{0,3},{1,0},{2,1},{3,2},{4,7},{5,4},{6,5},{7,6},{8,11},{9,8},{10,9... | collective-permute-start | bytes 1572872 | tf_op jit(solution)/shard_map/ppermute | solution.py:129
  81.9 3.4 %collective-permute-start.3 = (bf16[512,512]{1,0:T(8,128)(2,1)S(1)}, bf16[512,512]{1,0:T(8,128)(2,1)S(1)}, u32[]{:S(2)}, u32[]{:S(2)}) collective-permute-start(bf16[512,512]{1,0:T(8,128)(2,1)S(1)} %all_gather.6), channel_id=1, source_target_pairs={{0,1},{1,2},{2,3},{3,0},{4,5},{5,6},{6,7},{7,4},{8,9},{9,10},{10,1... | collective-permute-start | bytes 1572872 | tf_op jit(solution)/shard_map/ppermute | solution.py:129
  85.3 0.1 broadcast_in_dim.10
  85.5 1.1 %collective-permute-done.1 = bf16[512,512]{1,0:T(8,128)(2,1)} collective-permute-done((bf16[512,512]{1,0:T(8,128)(2,1)S(1)}, bf16[512,512]{1,0:T(8,128)(2,1)}, u32[]{:S(2)}, u32[]{:S(2)}) %collective-permute-start.1) | collective-permute-done | bytes 524320 | tf_op jit(solution)/shard_map/ppermute | solution.py:129
  86.7 1.1 constant_dynamic-update-slice_fusion.2
  87.7 11.2 %collective-permute-done.2 = bf16[512,512]{1,0:T(8,128)(2,1)} collective-permute-done((bf16[512,512]{1,0:T(8,128)(2,1)S(1)}, bf16[512,512]{1,0:T(8,128)(2,1)}, u32[]{:S(2)}, u32[]{:S(2)}) %collective-permute-start.2) | collective-permute-done | bytes 524320 | tf_op jit(solution)/shard_map/ppermute | solution.py:129
  98.9 1.1 constant_dynamic-update-slice_fusion.1
  100.1 7.1 %collective-permute-start.4 = (bf16[4,512,512]{2,1,0:T(8,128)(2,1)}, bf16[4,512,512]{2,1,0:T(8,128)(2,1)S(1)}, u32[]{:S(2)}, u32[]{:S(2)}) collective-permute-start(bf16[4,512,512]{2,1,0:T(8,128)(2,1)} %all-to-all-done.1), channel_id=1, source_target_pairs={{0,16},{16,0},{1,17},{17,1},{2,18},{18,2},{3,19},{19,3},{4,20},{20... | collective-permute-start | bytes 6291464 | tf_op jit(solution)/shard_map/ppermute | solution.py:147
  107.2 3.6 %hessian_half.2.rest_0_ = f32[512,1024]{1,0:T(8,128)} custom-call(s32[1]{0:T(128)} %bitcast.5.s_ref, bf16[2048,512]{1,0:T(8,128)(2,1)S(1)} %constant_dynamic-update-slice_fusion.rows_ref, bf16[2048,512]{1,0:T(8,128)(2,1)} %bitcast.7.cols_ref), custom_call_target="tpu_custom_call" | custom-call | tf_op jit(solution)/shard_map/hessian_half/pallas_call | solution.py:113
  110.8 0.4 collective-permute-done.4
  111.2 2.5 %hessian_half.3 = f32[512,1024]{1,0:T(8,128)} custom-call(s32[1]{0:T(128)S(6)} %sub.8.s_ref, bf16[2048,512]{1,0:T(8,128)(2,1)S(1)} %constant_dynamic-update-slice_fusion.rows_ref, bf16[2048,512]{1,0:T(8,128)(2,1)S(1)} %bitcast.8, f32[512,1024]{1,0:T(8,128)} %hessian_half.2.rest_0_), custom_call_target="tpu_custom_call", output_to_operand_aliasing={{}: (3, {})} | custom-call | tf_op jit(solution)/shard_map/hessian_half/pallas_call | solution.py:113
  (5 shorter events, 0.1 us)
Async XLA Ops:
  2.2 10.5 %all-to-all-start = ((bf16[4,272,128]{2,1,0:T(8,128)(2,1)}), bf16[4,272,128]{2,1,0:T(8,128)(2,1)S(1)}, u32[]{:S(2)}, u32[]{:S(2)}) async-start(bf16[4,272,128]{2,1,0:T(8,128)(2,1)} %pack.1), calls=%async_computation | async-start | bytes 557056 | tf_op jit(solution)/shard_map/all_to_all | solution.py:151
  14.5 34.3 %collective-permute-start = (bf16[128,512]{1,0:T(8,128)(2,1)}, bf16[128,512]{1,0:T(8,128)(2,1)S(1)}, u32[]{:S(2)}, u32[]{:S(2)}) collective-permute-start(bf16[128,512]{1,0:T(8,128)(2,1)} %attend.1), channel_id=1, source_target_pairs={{0,0},{1,32},{2,64},{3,96},{4,256},{5,288},{6,320},{7,352},{8,384}... | collective-permute-start | bytes 393224 | tf_op jit(solution)/shard_map/ppermute | solution.py:159
  68.9 31.2 %all-to-all-start.1 = ((bf16[4,512,512]{2,1,0:T(8,128)(2,1)}), bf16[4,512,512]{2,1,0:T(8,128)(2,1)}, u32[]{:S(2)}, u32[]{:S(2)}) async-start(bf16[4,512,512]{2,1,0:T(8,128)(2,1)} %broadcast_in_dim.4), calls=%async_computation.1 | async-start | bytes 4194304 | tf_op jit(solution)/shard_map/all_to_all | solution.py:151
  73.4 13.3 %collective-permute-start.1 = (bf16[512,512]{1,0:T(8,128)(2,1)S(1)}, bf16[512,512]{1,0:T(8,128)(2,1)}, u32[]{:S(2)}, u32[]{:S(2)}) collective-permute-start(bf16[512,512]{1,0:T(8,128)(2,1)S(1)} %all_gather.6), channel_id=1, source_target_pairs={{0,2},{1,3},{2,0},{3,1},{4,6},{5,7},{6,4},{7,5},{8,10},{9,11},{10,... | collective-permute-start | bytes 1572872 | tf_op jit(solution)/shard_map/ppermute | solution.py:129
  80.0 18.9 %collective-permute-start.2 = (bf16[512,512]{1,0:T(8,128)(2,1)S(1)}, bf16[512,512]{1,0:T(8,128)(2,1)}, u32[]{:S(2)}, u32[]{:S(2)}) collective-permute-start(bf16[512,512]{1,0:T(8,128)(2,1)S(1)} %all_gather.6), channel_id=1, source_target_pairs={{0,3},{1,0},{2,1},{3,2},{4,7},{5,4},{6,5},{7,6},{8,11},{9,8},{10,9... | collective-permute-start | bytes 1572872 | tf_op jit(solution)/shard_map/ppermute | solution.py:129
  81.9 18.1 %collective-permute-start.3 = (bf16[512,512]{1,0:T(8,128)(2,1)S(1)}, bf16[512,512]{1,0:T(8,128)(2,1)S(1)}, u32[]{:S(2)}, u32[]{:S(2)}) collective-permute-start(bf16[512,512]{1,0:T(8,128)(2,1)S(1)} %all_gather.6), channel_id=1, source_target_pairs={{0,1},{1,2},{2,3},{3,0},{4,5},{5,6},{6,7},{7,4},{8,9},{9,10},{10,1... | collective-permute-start | bytes 1572872 | tf_op jit(solution)/shard_map/ppermute | solution.py:129
  100.1 11.1 %collective-permute-start.4 = (bf16[4,512,512]{2,1,0:T(8,128)(2,1)}, bf16[4,512,512]{2,1,0:T(8,128)(2,1)S(1)}, u32[]{:S(2)}, u32[]{:S(2)}) collective-permute-start(bf16[4,512,512]{2,1,0:T(8,128)(2,1)} %all-to-all-done.1), channel_id=1, source_target_pairs={{0,16},{16,0},{1,17},{17,1},{2,18},{18,2},{3,19},{19,3},{4,20},{20... | collective-permute-start | bytes 6291464 | tf_op jit(solution)/shard_map/ppermute | solution.py:147

commit v13 on v12

--- a/solution.py
+++ b/solution.py
@@ -87,6 +87,7 @@
 
 
 LANDING = ((0, 2, 3, 1), (1, 3, 2, 0), (3, 1, 0, 2), (2, 0, 1, 3))
+TAKEN = tuple(tuple(line.index(k) for k in range(RING)) for line in LANDING)
 CONTRACT = (((0,), (0,)), ((), ()))
 
 
@@ -129,8 +130,13 @@
     return lax.ppermute(value, axis, [(i, (i + by) % RING) for i in range(RING)])
 
 
-def joined(axis, pieces):
-    me = lax.axis_index(axis)
+def shift_landed(value, ahead):
+    at = lambda group, slot: LANDING[group][slot % RING] * RING + group
+    pairs = [(at(g, k + ahead), at(g, k)) for g in range(RING) for k in range(RING)]
+    return lax.ppermute(value, ("zl", "zh"), pairs)
+
+
+def joined(me, pieces):
     depth, width = pieces[0].shape
     whole = jnp.zeros((RING * depth, width), pieces[0].dtype)
     for ahead in (0, 2, 1, 3):
@@ -171,13 +177,14 @@
     chunk = swap(attended)
     rows = lax.all_gather(attended, "zh", axis=0, tiled=True)
     chunk, rows = lax.optimization_barrier((chunk, rows))
-    landed = [[place * RING + group for place in LANDING[group]] for group in range(RING)]
-    cols = lax.all_gather(chunk, ("zl", "zh"), axis=0, tiled=True, axis_index_groups=landed)
-    cols, rows = lax.optimization_barrier((cols, rows))
+    spot = jnp.asarray(TAKEN, jnp.int32)[lax.axis_index("zh"), lax.axis_index("zl")]
+    landed = [chunk] + [shift_landed(chunk, ahead) for ahead in range(1, RING)]
+    opposite = shift(rows, "x", -2)
+    landed, opposite = lax.optimization_barrier((landed, opposite))
+    cols = joined(spot, landed)
     near = exchange(copies(cols), "y")
-    pieces = [shift(rows, "x", -ahead) for ahead in (2, 1, 3)]
-    opposite, after, before = pieces
-    rows = joined("x", (rows, after, opposite, before))
+    after, before = shift(rows, "x", -1), shift(rows, "x", 1)
+    rows = joined(lax.axis_index("x"), (rows, after, opposite, before))
     near, rows = lax.optimization_barrier((near, rows))
     far = swap_cores(near)
     near, far = (v.reshape(-1, v.shape[2]) for v in (near, far))

time: 114 us -> 118 us (1.035)
  starting transfers between devices: 29.9 us -> 48.8 us
  blocking collectives: 51.4 us -> 32.7 us
  between operations: 0.77 us -> 3.45 us
  local copies, waits for them, and re-layouts: 5.78 us -> 7.16 us
  waiting for transfers between devices: 16.4 us -> 15.2 us
    ppermute x0 -> x3, starting transfers between devices: none -> 20.3 us  [shift_landed(): return lax.ppermute(value, ('zl', 'zh'), pairs)]
    all_gather x1 -> x0, blocking collectives: 18.7 us -> none  [on_device(): lax.all_gather(chunk, ('zl', 'zh'), axis=0, tiled=True, axis_index_groups...]
    ppermute x3, waiting for transfers between devices: 12.3 us -> 6.83 us  [shift(): lax.ppermute(value, axis, [(i, (i + by) % RING) for i in range(RING)])]
    ppermute x3, starting transfers between devices: 11.9 us -> 7.2 us  [shift(): lax.ppermute(value, axis, [(i, (i + by) % RING) for i in range(RING)])]
    all_to_all x2, waiting for transfers between devices: 3.69 us -> 7.91 us  [exchange(): return lax.all_to_all(value, axis, split_axis=0, concat_axis=0, tiled=True)]
    ppermute x1, starting transfers between devices: 7.12 us -> 10.5 us  [swap_cores(): return lax.ppermute(value, 'core', [(0, 1), (1, 0)])]
    dynamic_slice x0 -> x1, local copies, waits for them, and re-layouts: none -> 1.27 us  [on_device(): jnp.asarray(TAKEN, jnp.int32)[lax.axis_index('zh'), lax.axis_index('zl')]]
  transfers between devices with their start and end apart: 7 -> 10, of which waited for: 4 -> 5; matrix products, arithmetic and copies ran while one was open for 4% -> 5% of each run, Pallas kernels for 3% -> 3%
where the time goes in v13:
time: 118 us; the launch traced here: 117 us
  starting transfers between devices  48.8 us (41%)
  blocking collectives  32.7 us (28%)
  waiting for transfers between devices  15.2 us (13%)
  Pallas kernels  9.42 us (8%)
  local copies, waits for them, and re-layouts  7.16 us (6%)
  between operations  3.45 us (3%)
    all_gather x1, blocking collectives, on_device(): rows = lax.all_gather(attended, 'zh', axis=0, tiled=True)  32.7 us
    ppermute x3, starting transfers between devices, shift_landed(): return lax.ppermute(value, ('zl', 'zh'), pairs)  20.3 us
    ppermute x1, starting transfers between devices, swap_cores(): return lax.ppermute(value, 'core', [(0, 1), (1, 0)])  10.5 us
    all_to_all x2, starting transfers between devices, exchange(): return lax.all_to_all(value, axis, split_axis=0, concat_axis=0, tiled=True)  9.28 us
    all_to_all x2, waiting for transfers between devices, exchange(): return lax.all_to_all(value, axis, split_axis=0, concat_axis=0, tiled=True)  7.91 us
    ppermute x3, starting transfers between devices, shift(): lax.ppermute(value, axis, [(i, (i + by) % RING) for i in range(RING)])  7.2 us
    ppermute x3, waiting for transfers between devices, shift(): lax.ppermute(value, axis, [(i, (i + by) % RING) for i in range(RING)])  6.83 us
    pallas_call x2, Pallas kernels, hessian_half(): pl.pallas_call(half_kernel, out_shape=jax.ShapeDtypeStruct((width, 2 * ha...  6.05 us
  transfers between devices with their start and end apart: 10, of which 5 were waited for; matrix products, arithmetic and copies ran while one was open for 5% of the time, Pallas kernels for 3%

profile of v13, /device:TPU:1, one launch (start us, length us, event | category | flops | bytes accessed | tf_op | source)
XLA Modules:
  0.0 116.7 jit_solution(17419662908598098340)
XLA Ops:
  0.7 1.5 %pack.1 = bf16[4,272,128]{2,1,0:T(8,128)(2,1)} custom-call(s32[1]{0:T(128)} %bitcast.2.g_ref, bf16[128,1024]{1,0:T(8,128)(2,1)} %k_ref.1, bf16[128,1024]{1,0:T(8,128)(2,1)} %v_ref.1, s32[1,128]{1,0:T(1,128)} %bitcast.15), custom_call_target="tpu_custom_call" | custom-call | tf_op jit(solution)/shard_map/pack/pallas_call | solution.py:37
  2.2 4.8 %all-to-all-start = ((bf16[4,272,128]{2,1,0:T(8,128)(2,1)}), bf16[4,272,128]{2,1,0:T(8,128)(2,1)S(1)}, u32[]{:S(2)}, u32[]{:S(2)}) async-start(bf16[4,272,128]{2,1,0:T(8,128)(2,1)} %pack.1), calls=%async_computation | async-start | bytes 557056 | tf_op jit(solution)/shard_map/all_to_all | solution.py:157
  7.0 1.0 copy.9
  9.0 3.7 %all-to-all-done.kv_ref = bf16[4,272,128]{2,1,0:T(8,128)(2,1)S(1)} async-done(((bf16[4,272,128]{2,1,0:T(8,128)(2,1)}), bf16[4,272,128]{2,1,0:T(8,128)(2,1)S(1)}, u32[]{:S(2)}, u32[]{:S(2)}) %all-to-all-start) | async-done | bytes 278560 | tf_op jit(solution)/shard_map/all_to_all | solution.py:157
  12.6 1.8 %attend.1 = bf16[128,512]{1,0:T(8,128)(2,1)} custom-call(bf16[4,128,128]{2,1,0:T(8,128)(2,1)S(1)} %bitcast.13, bf16[4,272,128]{2,1,0:T(8,128)(2,1)S(1)} %all-to-all-done.kv_ref, s32[128,1]{1,0:T(8,128)S(1)} %copy.11.p_ref), custom_call_target="tpu_custom_call" | custom-call | tf_op jit(solution)/shard_map/attend/pallas_call | solution.py:81
  14.5 1.6 %collective-permute-start = (bf16[128,512]{1,0:T(8,128)(2,1)}, bf16[128,512]{1,0:T(8,128)(2,1)S(1)}, u32[]{:S(2)}, u32[]{:S(2)}) collective-permute-start(bf16[128,512]{1,0:T(8,128)(2,1)} %attend.1), channel_id=1, source_target_pairs={{0,0},{1,32},{2,64},{3,96},{4,256},{5,288},{6,320},{7,352},{8,384}... | collective-permute-start | bytes 393224 | tf_op jit(solution)/shard_map/ppermute | solution.py:165
  16.0 32.7 %all_gather.3 = bf16[512,512]{1,0:T(8,128)(2,1)S(1)} all-gather(bf16[128,512]{1,0:T(8,128)(2,1)} %attend.1), channel_id=1, replica_groups=mesh['zl'=4,'y'=4,'core'=2,'zh'=4,'x'=4] {'zh'}, dimensions={0}, use_global_device_ids=true | all-gather | bytes 655360 | tf_op jit(solution)/shard_map/all_gather | solution.py:178
  48.7 1.9 %collective-permute-start.4 = (bf16[512,512]{1,0:T(8,128)(2,1)S(1)}, bf16[512,512]{1,0:T(8,128)(2,1)S(1)}, u32[]{:S(2)}, u32[]{:S(2)}) collective-permute-start(bf16[512,512]{1,0:T(8,128)(2,1)S(1)} %all_gather.3), channel_id=1, source_target_pairs={{0,2},{1,3},{2,0},{3,1},{4,6},{5,7},{6,4},{7,5},{8,10},{9,11},{10,... | collective-permute-start | bytes 1572872 | tf_op jit(solution)/shard_map/ppermute | solution.py:130
  50.6 9.2 %collective-permute-start.1 = (bf16[128,512]{1,0:T(8,128)(2,1)S(1)}, bf16[128,512]{1,0:T(8,128)(2,1)S(1)}, u32[]{:S(2)}, u32[]{:S(2)}) collective-permute-start(bf16[128,512]{1,0:T(8,128)(2,1)S(1)} %collective-permute-done), channel_id=1, source_target_pairs={{256,0},{384,256},{128,384},{0,128},{388,132},{260,388},{4,260},{1... | collective-permute-start | bytes 393224 | tf_op jit(solution)/shard_map/ppermute | solution.py:136
  59.8 9.2 %collective-permute-start.2 = (bf16[128,512]{1,0:T(8,128)(2,1)S(1)}, bf16[128,512]{1,0:T(8,128)(2,1)S(1)}, u32[]{:S(2)}, u32[]{:S(2)}) collective-permute-start(bf16[128,512]{1,0:T(8,128)(2,1)S(1)} %collective-permute-done), channel_id=1, source_target_pairs={{384,0},{128,256},{0,384},{256,128},{260,132},{4,388},{132,260},{3... | collective-permute-start | bytes 393224 | tf_op jit(solution)/shard_map/ppermute | solution.py:136
  69.0 1.9 %collective-permute-start.3 = (bf16[128,512]{1,0:T(8,128)(2,1)S(1)}, bf16[128,512]{1,0:T(8,128)(2,1)S(1)}, u32[]{:S(2)}, u32[]{:S(2)}) collective-permute-start(bf16[128,512]{1,0:T(8,128)(2,1)S(1)} %collective-permute-done), channel_id=1, source_target_pairs={{128,0},{0,256},{256,384},{384,128},{4,132},{132,388},{388,260},{2... | collective-permute-start | bytes 393224 | tf_op jit(solution)/shard_map/ppermute | solution.py:136
  71.0 1.3 %dynamic_slice.3 = s32[1,1]{1,0:T(1,128)} dynamic-slice(s32[4,4]{1,0:T(4,128)} %constant.81.clone, s32[]{:T(128)S(6)} %select_n.36, s32[]{:T(128)S(6)} %select_n.37), dynamic_slice_sizes={1,1} | dynamic-slice | bytes 12 | tf_op jit(solution)/shard_map/dynamic_slice | solution.py:180
  75.0 1.5 %broadcast_in_dim.13 = bf16[4,512,512]{2,1,0:T(8,128)(2,1)} broadcast(bf16[512,512]{1,0:T(8,128)(2,1)S(1)} %constant_dynamic-update-slice_fusion.4), dimensions={1,2} | broadcast | bytes 2621440 | tf_op jit(solution)/shard_map/broadcast_in_dim | solution.py:149
  76.5 4.4 %all-to-all-start.1 = ((bf16[4,512,512]{2,1,0:T(8,128)(2,1)}), bf16[4,512,512]{2,1,0:T(8,128)(2,1)}, u32[]{:S(2)}, u32[]{:S(2)}) async-start(bf16[4,512,512]{2,1,0:T(8,128)(2,1)} %broadcast_in_dim.13), calls=%async_computation.1 | async-start | bytes 4194304 | tf_op jit(solution)/shard_map/all_to_all | solution.py:157
  80.9 1.9 %collective-permute-start.5 = (bf16[512,512]{1,0:T(8,128)(2,1)S(1)}, bf16[512,512]{1,0:T(8,128)(2,1)}, u32[]{:S(2)}, u32[]{:S(2)}) collective-permute-start(bf16[512,512]{1,0:T(8,128)(2,1)S(1)} %all_gather.3), channel_id=1, source_target_pairs={{0,3},{1,0},{2,1},{3,2},{4,7},{5,4},{6,5},{7,6},{8,11},{9,8},{10,9... | collective-permute-start | bytes 1572872 | tf_op jit(solution)/shard_map/ppermute | solution.py:130
  82.9 3.4 %collective-permute-start.6 = (bf16[512,512]{1,0:T(8,128)(2,1)S(1)}, bf16[512,512]{1,0:T(8,128)(2,1)}, u32[]{:S(2)}, u32[]{:S(2)}) collective-permute-start(bf16[512,512]{1,0:T(8,128)(2,1)S(1)} %all_gather.3), channel_id=1, source_target_pairs={{0,1},{1,2},{2,3},{3,0},{4,5},{5,6},{6,7},{7,4},{8,9},{9,10},{10,1... | collective-permute-start | bytes 1572872 | tf_op jit(solution)/shard_map/ppermute | solution.py:130
  86.5 4.5 %collective-permute-done.5 = bf16[512,512]{1,0:T(8,128)(2,1)} collective-permute-done((bf16[512,512]{1,0:T(8,128)(2,1)S(1)}, bf16[512,512]{1,0:T(8,128)(2,1)}, u32[]{:S(2)}, u32[]{:S(2)}) %collective-permute-start.5) | collective-permute-done | bytes 524320 | tf_op jit(solution)/shard_map/ppermute | solution.py:130
  91.0 1.1 constant_dynamic-update-slice_fusion.1
  92.1 2.4 %collective-permute-done.6 = bf16[512,512]{1,0:T(8,128)(2,1)} collective-permute-done((bf16[512,512]{1,0:T(8,128)(2,1)S(1)}, bf16[512,512]{1,0:T(8,128)(2,1)}, u32[]{:S(2)}, u32[]{:S(2)}) %collective-permute-start.6) | collective-permute-done | bytes 524320 | tf_op jit(solution)/shard_map/ppermute | solution.py:130
  94.4 1.1 constant_dynamic-update-slice_fusion.rows_ref
  95.5 4.2 %all-to-all-done.1 = bf16[4,512,512]{2,1,0:T(8,128)(2,1)} async-done(((bf16[4,512,512]{2,1,0:T(8,128)(2,1)}), bf16[4,512,512]{2,1,0:T(8,128)(2,1)}, u32[]{:S(2)}, u32[]{:S(2)}) %all-to-all-start.1) | async-done | bytes 2097184 | tf_op jit(solution)/shard_map/all_to_all | solution.py:157
  99.7 10.5 %collective-permute-start.7 = (bf16[4,512,512]{2,1,0:T(8,128)(2,1)}, bf16[4,512,512]{2,1,0:T(8,128)(2,1)S(1)}, u32[]{:S(2)}, u32[]{:S(2)}) collective-permute-start(bf16[4,512,512]{2,1,0:T(8,128)(2,1)} %all-to-all-done.1), channel_id=1, source_target_pairs={{0,16},{16,0},{1,17},{17,1},{2,18},{18,2},{3,19},{19,3},{4,20},{20... | collective-permute-start | bytes 6291464 | tf_op jit(solution)/shard_map/ppermute | solution.py:153
  110.2 3.6 %hessian_half.2.rest_0_ = f32[512,1024]{1,0:T(8,128)} custom-call(s32[1]{0:T(128)} %bitcast.5.s_ref, bf16[2048,512]{1,0:T(8,128)(2,1)S(1)} %constant_dynamic-update-slice_fusion.rows_ref, bf16[2048,512]{1,0:T(8,128)(2,1)} %bitcast.11.cols_ref), custom_call_target="tpu_custom_call" | custom-call | tf_op jit(solution)/shard_map/hessian_half/pallas_call | solution.py:114
  114.2 2.5 %hessian_half.3 = f32[512,1024]{1,0:T(8,128)} custom-call(s32[1]{0:T(128)S(6)} %sub.8.s_ref, bf16[2048,512]{1,0:T(8,128)(2,1)S(1)} %constant_dynamic-update-slice_fusion.rows_ref, bf16[2048,512]{1,0:T(8,128)(2,1)S(1)} %bitcast.12, f32[512,1024]{1,0:T(8,128)} %hessian_half.2.rest_0_), custom_call_target="tpu_custom_call", output_to_operand_aliasing={{}: (3, {})} | custom-call | tf_op jit(solution)/shard_map/hessian_half/pallas_call | solution.py:114
  (16 shorter events, 1.7 us)
Async XLA Ops:
  2.2 10.5 %all-to-all-start = ((bf16[4,272,128]{2,1,0:T(8,128)(2,1)}), bf16[4,272,128]{2,1,0:T(8,128)(2,1)S(1)}, u32[]{:S(2)}, u32[]{:S(2)}) async-start(bf16[4,272,128]{2,1,0:T(8,128)(2,1)} %pack.1), calls=%async_computation | async-start | bytes 557056 | tf_op jit(solution)/shard_map/all_to_all | solution.py:157
  14.5 34.2 %collective-permute-start = (bf16[128,512]{1,0:T(8,128)(2,1)}, bf16[128,512]{1,0:T(8,128)(2,1)S(1)}, u32[]{:S(2)}, u32[]{:S(2)}) collective-permute-start(bf16[128,512]{1,0:T(8,128)(2,1)} %attend.1), channel_id=1, source_target_pairs={{0,0},{1,32},{2,64},{3,96},{4,256},{5,288},{6,320},{7,352},{8,384}... | collective-permute-start | bytes 393224 | tf_op jit(solution)/shard_map/ppermute | solution.py:165
  48.7 26.1 %collective-permute-start.4 = (bf16[512,512]{1,0:T(8,128)(2,1)S(1)}, bf16[512,512]{1,0:T(8,128)(2,1)S(1)}, u32[]{:S(2)}, u32[]{:S(2)}) collective-permute-start(bf16[512,512]{1,0:T(8,128)(2,1)S(1)} %all_gather.3), channel_id=1, source_target_pairs={{0,2},{1,3},{2,0},{3,1},{4,6},{5,7},{6,4},{7,5},{8,10},{9,11},{10,... | collective-permute-start | bytes 1572872 | tf_op jit(solution)/shard_map/ppermute | solution.py:130
  50.6 24.2 %collective-permute-start.1 = (bf16[128,512]{1,0:T(8,128)(2,1)S(1)}, bf16[128,512]{1,0:T(8,128)(2,1)S(1)}, u32[]{:S(2)}, u32[]{:S(2)}) collective-permute-start(bf16[128,512]{1,0:T(8,128)(2,1)S(1)} %collective-permute-done), channel_id=1, source_target_pairs={{256,0},{384,256},{128,384},{0,128},{388,132},{260,388},{4,260},{1... | collective-permute-start | bytes 393224 | tf_op jit(solution)/shard_map/ppermute | solution.py:136
  59.8 15.0 %collective-permute-start.2 = (bf16[128,512]{1,0:T(8,128)(2,1)S(1)}, bf16[128,512]{1,0:T(8,128)(2,1)S(1)}, u32[]{:S(2)}, u32[]{:S(2)}) collective-permute-start(bf16[128,512]{1,0:T(8,128)(2,1)S(1)} %collective-permute-done), channel_id=1, source_target_pairs={{384,0},{128,256},{0,384},{256,128},{260,132},{4,388},{132,260},{3... | collective-permute-start | bytes 393224 | tf_op jit(solution)/shard_map/ppermute | solution.py:136
  69.0 5.8 %collective-permute-start.3 = (bf16[128,512]{1,0:T(8,128)(2,1)S(1)}, bf16[128,512]{1,0:T(8,128)(2,1)S(1)}, u32[]{:S(2)}, u32[]{:S(2)}) collective-permute-start(bf16[128,512]{1,0:T(8,128)(2,1)S(1)} %collective-permute-done), channel_id=1, source_target_pairs={{128,0},{0,256},{256,384},{384,128},{4,132},{132,388},{388,260},{2... | collective-permute-start | bytes 393224 | tf_op jit(solution)/shard_map/ppermute | solution.py:136
  76.5 23.2 %all-to-all-start.1 = ((bf16[4,512,512]{2,1,0:T(8,128)(2,1)}), bf16[4,512,512]{2,1,0:T(8,128)(2,1)}, u32[]{:S(2)}, u32[]{:S(2)}) async-start(bf16[4,512,512]{2,1,0:T(8,128)(2,1)} %broadcast_in_dim.13), calls=%async_computation.1 | async-start | bytes 4194304 | tf_op jit(solution)/shard_map/all_to_all | solution.py:157
  80.9 10.0 %collective-permute-start.5 = (bf16[512,512]{1,0:T(8,128)(2,1)S(1)}, bf16[512,512]{1,0:T(8,128)(2,1)}, u32[]{:S(2)}, u32[]{:S(2)}) collective-permute-start(bf16[512,512]{1,0:T(8,128)(2,1)S(1)} %all_gather.3), channel_id=1, source_target_pairs={{0,3},{1,0},{2,1},{3,2},{4,7},{5,4},{6,5},{7,6},{8,11},{9,8},{10,9... | collective-permute-start | bytes 1572872 | tf_op jit(solution)/shard_map/ppermute | solution.py:130
  82.9 11.5 %collective-permute-start.6 = (bf16[512,512]{1,0:T(8,128)(2,1)S(1)}, bf16[512,512]{1,0:T(8,128)(2,1)}, u32[]{:S(2)}, u32[]{:S(2)}) collective-permute-start(bf16[512,512]{1,0:T(8,128)(2,1)S(1)} %all_gather.3), channel_id=1, source_target_pairs={{0,1},{1,2},{2,3},{3,0},{4,5},{5,6},{6,7},{7,4},{8,9},{9,10},{10,1... | collective-permute-start | bytes 1572872 | tf_op jit(solution)/shard_map/ppermute | solution.py:130
  99.7 14.5 %collective-permute-start.7 = (bf16[4,512,512]{2,1,0:T(8,128)(2,1)}, bf16[4,512,512]{2,1,0:T(8,128)(2,1)S(1)}, u32[]{:S(2)}, u32[]{:S(2)}) collective-permute-start(bf16[4,512,512]{2,1,0:T(8,128)(2,1)} %all-to-all-done.1), channel_id=1, source_target_pairs={{0,16},{16,0},{1,17},{17,1},{2,18},{18,2},{3,19},{19,3},{4,20},{20... | collective-permute-start | bytes 6291464 | tf_op jit(solution)/shard_map/ppermute | solution.py:153

commit v14 on v11

--- a/solution.py
+++ b/solution.py
@@ -129,11 +129,16 @@
     return lax.ppermute(value, axis, [(i, (i + by) % RING) for i in range(RING)])
 
 
-def joined(axis, pieces):
-    me = lax.axis_index(axis)
-    depth, width = pieces[0].shape
-    whole = jnp.zeros((RING * depth, width), pieces[0].dtype)
-    for ahead, piece in enumerate(pieces):
+def turn(value, by):
+    steps = ((0, by), (1, -by))
+    pairs = [(c * RING + i, c * RING + (i + d) % RING) for c, d in steps for i in range(RING)]
+    return lax.ppermute(value, ("core", "x"), pairs)
+
+
+def joined(me, pieces):
+    depth, width = pieces[0][1].shape
+    whole = jnp.zeros((RING * depth, width), pieces[0][1].dtype)
+    for ahead, piece in pieces:
         start = ((me + ahead) & (RING - 1)) * depth
         whole = lax.dynamic_update_slice(whole, piece, (start, 0))
     return whole
@@ -175,9 +180,11 @@
     cols = lax.all_gather(chunk, ("zl", "zh"), axis=0, tiled=True, axis_index_groups=landed)
     cols, rows = lax.optimization_barrier((cols, rows))
     near = exchange(copies(cols), "y")
-    pieces = [shift(rows, "x", -ahead) for ahead in (2, 1, 3)]
-    opposite, after, before = pieces
-    rows = joined("x", (rows, after, opposite, before))
+    opposite = shift(rows, "x", -2)
+    one, two = turn(rows, -1), turn(rows, 1)
+    step = jnp.where(lax.axis_index("core") == 0, 1, RING - 1)
+    pieces = ((0, rows), (2, opposite), (step, one), (-step, two))
+    rows = joined(lax.axis_index("x"), pieces)
     near, rows = lax.optimization_barrier((near, rows))
     far = swap_cores(near)
     near, far = (v.reshape(-1, v.shape[2]) for v in (near, far))

time: 117 us -> 115 us (0.983)
  waiting for transfers between devices: 21 us -> 16.8 us
  starting transfers between devices: 28.3 us -> 29.7 us
    ppermute x3 -> x1, waiting for transfers between devices: 16.9 us -> 0.04 us  [shift(): lax.ppermute(value, axis, [(i, (i + by) % RING) for i in range(RING)])]
    ppermute x0 -> x2, waiting for transfers between devices: none -> 12.6 us  [turn(): return lax.ppermute(value, ('core', 'x'), pairs)]
    ppermute x0 -> x2, starting transfers between devices: none -> 6.49 us  [turn(): return lax.ppermute(value, ('core', 'x'), pairs)]
    ppermute x3 -> x1, starting transfers between devices: 11.3 us -> 6.63 us  [shift(): lax.ppermute(value, axis, [(i, (i + by) % RING) for i in range(RING)])]
  transfers between devices with their start and end apart: 7 -> 7, of which waited for: 5 -> 4; matrix products, arithmetic and copies ran while one was open for 4% -> 4% of each run, Pallas kernels for 3% -> 3%
where the time goes in v14:
time: 115 us; the launch traced here: 114 us
  blocking collectives  51.4 us (45%)
  starting transfers between devices  29.7 us (26%)
  waiting for transfers between devices  16.8 us (15%)
  Pallas kernels  9.42 us (8%)
  local copies, waits for them, and re-layouts  5.78 us (5%)
    all_gather x1, blocking collectives, on_device(): rows = lax.all_gather(attended, 'zh', axis=0, tiled=True)  32.7 us
    all_gather x1, blocking collectives, on_device(): lax.all_gather(chunk, ('zl', 'zh'), axis=0, tiled=True, axis_index_groups...  18.7 us
    ppermute x2, waiting for transfers between devices, turn(): return lax.ppermute(value, ('core', 'x'), pairs)  12.6 us
    all_to_all x2, starting transfers between devices, exchange(): return lax.all_to_all(value, axis, split_axis=0, concat_axis=0, tiled=True)  9.3 us
    ppermute x1, starting transfers between devices, shift(): lax.ppermute(value, axis, [(i, (i + by) % RING) for i in range(RING)])  6.63 us
    ppermute x2, starting transfers between devices, turn(): return lax.ppermute(value, ('core', 'x'), pairs)  6.49 us
    pallas_call x2, Pallas kernels, hessian_half(): pl.pallas_call(half_kernel, out_shape=jax.ShapeDtypeStruct((width, 2 * ha...  6.04 us
    ppermute x1, starting transfers between devices, swap_cores(): return lax.ppermute(value, 'core', [(0, 1), (1, 0)])  5.69 us
  transfers between devices with their start and end apart: 7, of which 4 were waited for; matrix products, arithmetic and copies ran while one was open for 4% of the time, Pallas kernels for 3%

profile of v14, /device:TPU:1, one launch (start us, length us, event | category | flops | bytes accessed | tf_op | source)
XLA Modules:
  0.0 113.8 jit_solution(15838628122904475992)
XLA Ops:
  0.7 1.5 %pack.1 = bf16[4,272,128]{2,1,0:T(8,128)(2,1)} custom-call(s32[1]{0:T(128)} %bitcast.2.g_ref, bf16[128,1024]{1,0:T(8,128)(2,1)} %k_ref.1, bf16[128,1024]{1,0:T(8,128)(2,1)} %v_ref.1, s32[1,128]{1,0:T(1,128)} %bitcast.11), custom_call_target="tpu_custom_call" | custom-call | tf_op jit(solution)/shard_map/pack/pallas_call | solution.py:37
  2.2 4.8 %all-to-all-start = ((bf16[4,272,128]{2,1,0:T(8,128)(2,1)}), bf16[4,272,128]{2,1,0:T(8,128)(2,1)S(1)}, u32[]{:S(2)}, u32[]{:S(2)}) async-start(bf16[4,272,128]{2,1,0:T(8,128)(2,1)} %pack.1), calls=%async_computation | async-start | bytes 557056 | tf_op jit(solution)/shard_map/all_to_all | solution.py:156
  7.0 1.0 copy.8
  8.0 0.1 copy.9
  8.2 0.8 copy.10.p_ref
  9.0 3.7 %all-to-all-done.kv_ref = bf16[4,272,128]{2,1,0:T(8,128)(2,1)S(1)} async-done(((bf16[4,272,128]{2,1,0:T(8,128)(2,1)}), bf16[4,272,128]{2,1,0:T(8,128)(2,1)S(1)}, u32[]{:S(2)}, u32[]{:S(2)}) %all-to-all-start) | async-done | bytes 278560 | tf_op jit(solution)/shard_map/all_to_all | solution.py:156
  12.6 1.8 %attend.1 = bf16[128,512]{1,0:T(8,128)(2,1)} custom-call(bf16[4,128,128]{2,1,0:T(8,128)(2,1)S(1)} %bitcast.9, bf16[4,272,128]{2,1,0:T(8,128)(2,1)S(1)} %all-to-all-done.kv_ref, s32[128,1]{1,0:T(8,128)S(1)} %copy.10.p_ref), custom_call_target="tpu_custom_call" | custom-call | tf_op jit(solution)/shard_map/attend/pallas_call | solution.py:81
  14.5 1.6 %collective-permute-start = (bf16[128,512]{1,0:T(8,128)(2,1)}, bf16[128,512]{1,0:T(8,128)(2,1)S(1)}, u32[]{:S(2)}, u32[]{:S(2)}) collective-permute-start(bf16[128,512]{1,0:T(8,128)(2,1)} %attend.1), channel_id=1, source_target_pairs={{0,0},{1,32},{2,64},{3,96},{4,256},{5,288},{6,320},{7,352},{8,384}... | collective-permute-start | bytes 393224 | tf_op jit(solution)/shard_map/ppermute | solution.py:164
  16.0 32.7 %all_gather.6 = bf16[512,512]{1,0:T(8,128)(2,1)S(1)} all-gather(bf16[128,512]{1,0:T(8,128)(2,1)} %attend.1), channel_id=1, replica_groups=mesh['zl'=4,'y'=4,'core'=2,'zh'=4,'x'=4] {'zh'}, dimensions={0}, use_global_device_ids=true | all-gather | bytes 655360 | tf_op jit(solution)/shard_map/all_gather | solution.py:177
  48.8 18.7 %all_gather.7 = bf16[512,512]{1,0:T(8,128)(2,1)S(1)} all-gather(bf16[128,512]{1,0:T(8,128)(2,1)S(1)} %collective-permute-done), channel_id=1, replica_groups={{0,256,384,128},{132,388,260,4},{392,136,8,264},{268,12,140,396},{1,257..., dimensions={0}, use_global_device_ids=true | all-gather | bytes 655360 | tf_op jit(solution)/shard_map/all_gather | solution.py:180
  67.4 1.5 %broadcast_in_dim.4 = bf16[4,512,512]{2,1,0:T(8,128)(2,1)} broadcast(bf16[512,512]{1,0:T(8,128)(2,1)S(1)} %all_gather.7), dimensions={1,2} | broadcast | bytes 2621440 | tf_op jit(solution)/shard_map/broadcast_in_dim | solution.py:148
  68.9 4.5 %all-to-all-start.1 = ((bf16[4,512,512]{2,1,0:T(8,128)(2,1)}), bf16[4,512,512]{2,1,0:T(8,128)(2,1)}, u32[]{:S(2)}, u32[]{:S(2)}) async-start(bf16[4,512,512]{2,1,0:T(8,128)(2,1)} %broadcast_in_dim.4), calls=%async_computation.1 | async-start | bytes 4194304 | tf_op jit(solution)/shard_map/all_to_all | solution.py:156
  73.4 6.6 %collective-permute-start.1 = (bf16[512,512]{1,0:T(8,128)(2,1)S(1)}, bf16[512,512]{1,0:T(8,128)(2,1)}, u32[]{:S(2)}, u32[]{:S(2)}) collective-permute-start(bf16[512,512]{1,0:T(8,128)(2,1)S(1)} %all_gather.6), channel_id=1, source_target_pairs={{0,2},{1,3},{2,0},{3,1},{4,6},{5,7},{6,4},{7,5},{8,10},{9,11},{10,... | collective-permute-start | bytes 1572872 | tf_op jit(solution)/shard_map/ppermute | solution.py:129
  80.0 1.9 %collective-permute-start.2 = (bf16[512,512]{1,0:T(8,128)(2,1)S(1)}, bf16[512,512]{1,0:T(8,128)(2,1)}, u32[]{:S(2)}, u32[]{:S(2)}) collective-permute-start(bf16[512,512]{1,0:T(8,128)(2,1)S(1)} %all_gather.6), channel_id=1, source_target_pairs={{0,3},{1,0},{2,1},{3,2},{16,17},{17,18},{18,19},{19,16},{4,7},{5,4... | collective-permute-start | bytes 1572872 | tf_op jit(solution)/shard_map/ppermute | solution.py:135
  81.9 4.6 %collective-permute-start.3 = (bf16[512,512]{1,0:T(8,128)(2,1)S(1)}, bf16[512,512]{1,0:T(8,128)(2,1)S(1)}, u32[]{:S(2)}, u32[]{:S(2)}) collective-permute-start(bf16[512,512]{1,0:T(8,128)(2,1)S(1)} %all_gather.6), channel_id=1, source_target_pairs={{0,1},{1,2},{2,3},{3,0},{16,19},{17,16},{18,17},{19,18},{4,5},{5,6... | collective-permute-start | bytes 1572872 | tf_op jit(solution)/shard_map/ppermute | solution.py:135
  86.5 0.1 broadcast_in_dim.10
  86.8 1.1 constant_dynamic-update-slice_fusion.2
  87.8 8.2 %collective-permute-done.2 = bf16[512,512]{1,0:T(8,128)(2,1)} collective-permute-done((bf16[512,512]{1,0:T(8,128)(2,1)S(1)}, bf16[512,512]{1,0:T(8,128)(2,1)}, u32[]{:S(2)}, u32[]{:S(2)}) %collective-permute-start.2) | collective-permute-done | bytes 524320 | tf_op jit(solution)/shard_map/ppermute | solution.py:135
  96.1 1.1 constant_dynamic-update-slice_fusion.1
  97.1 4.4 %collective-permute-done.3 = bf16[512,512]{1,0:T(8,128)(2,1)S(1)} collective-permute-done((bf16[512,512]{1,0:T(8,128)(2,1)S(1)}, bf16[512,512]{1,0:T(8,128)(2,1)S(1)}, u32[]{:S(2)}, u32[]{:S(2)}) %collective-permute-start.3) | collective-permute-done | bytes 524320 | tf_op jit(solution)/shard_map/ppermute | solution.py:135
  101.6 5.7 %collective-permute-start.4 = (bf16[4,512,512]{2,1,0:T(8,128)(2,1)}, bf16[4,512,512]{2,1,0:T(8,128)(2,1)S(1)}, u32[]{:S(2)}, u32[]{:S(2)}) collective-permute-start(bf16[4,512,512]{2,1,0:T(8,128)(2,1)} %all-to-all-done.1), channel_id=1, source_target_pairs={{0,16},{16,0},{1,17},{17,1},{2,18},{18,2},{3,19},{19,3},{4,20},{20... | collective-permute-start | bytes 6291464 | tf_op jit(solution)/shard_map/ppermute | solution.py:152
  107.3 3.6 %hessian_half.2.rest_0_ = f32[512,1024]{1,0:T(8,128)} custom-call(s32[1]{0:T(128)} %bitcast.5.s_ref, bf16[2048,512]{1,0:T(8,128)(2,1)S(1)} %constant_dynamic-update-slice_fusion.rows_ref, bf16[2048,512]{1,0:T(8,128)(2,1)} %bitcast.7.cols_ref), custom_call_target="tpu_custom_call" | custom-call | tf_op jit(solution)/shard_map/hessian_half/pallas_call | solution.py:113
  110.9 0.4 collective-permute-done.4
  111.3 2.5 %hessian_half.3 = f32[512,1024]{1,0:T(8,128)} custom-call(s32[1]{0:T(128)S(6)} %sub.8.s_ref, bf16[2048,512]{1,0:T(8,128)(2,1)S(1)} %constant_dynamic-update-slice_fusion.rows_ref, bf16[2048,512]{1,0:T(8,128)(2,1)S(1)} %bitcast.8, f32[512,1024]{1,0:T(8,128)} %hessian_half.2.rest_0_), custom_call_target="tpu_custom_call", output_to_operand_aliasing={{}: (3, {})} | custom-call | tf_op jit(solution)/shard_map/hessian_half/pallas_call | solution.py:113
  (5 shorter events, 0.1 us)
Async XLA Ops:
  2.2 10.5 %all-to-all-start = ((bf16[4,272,128]{2,1,0:T(8,128)(2,1)}), bf16[4,272,128]{2,1,0:T(8,128)(2,1)S(1)}, u32[]{:S(2)}, u32[]{:S(2)}) async-start(bf16[4,272,128]{2,1,0:T(8,128)(2,1)} %pack.1), calls=%async_computation | async-start | bytes 557056 | tf_op jit(solution)/shard_map/all_to_all | solution.py:156
  14.5 34.3 %collective-permute-start = (bf16[128,512]{1,0:T(8,128)(2,1)}, bf16[128,512]{1,0:T(8,128)(2,1)S(1)}, u32[]{:S(2)}, u32[]{:S(2)}) collective-permute-start(bf16[128,512]{1,0:T(8,128)(2,1)} %attend.1), channel_id=1, source_target_pairs={{0,0},{1,32},{2,64},{3,96},{4,256},{5,288},{6,320},{7,352},{8,384}... | collective-permute-start | bytes 393224 | tf_op jit(solution)/shard_map/ppermute | solution.py:164
  68.9 32.7 %all-to-all-start.1 = ((bf16[4,512,512]{2,1,0:T(8,128)(2,1)}), bf16[4,512,512]{2,1,0:T(8,128)(2,1)}, u32[]{:S(2)}, u32[]{:S(2)}) async-start(bf16[4,512,512]{2,1,0:T(8,128)(2,1)} %broadcast_in_dim.4), calls=%async_computation.1 | async-start | bytes 4194304 | tf_op jit(solution)/shard_map/all_to_all | solution.py:156
  73.4 13.4 %collective-permute-start.1 = (bf16[512,512]{1,0:T(8,128)(2,1)S(1)}, bf16[512,512]{1,0:T(8,128)(2,1)}, u32[]{:S(2)}, u32[]{:S(2)}) collective-permute-start(bf16[512,512]{1,0:T(8,128)(2,1)S(1)} %all_gather.6), channel_id=1, source_target_pairs={{0,2},{1,3},{2,0},{3,1},{4,6},{5,7},{6,4},{7,5},{8,10},{9,11},{10,... | collective-permute-start | bytes 1572872 | tf_op jit(solution)/shard_map/ppermute | solution.py:129
  80.0 16.1 %collective-permute-start.2 = (bf16[512,512]{1,0:T(8,128)(2,1)S(1)}, bf16[512,512]{1,0:T(8,128)(2,1)}, u32[]{:S(2)}, u32[]{:S(2)}) collective-permute-start(bf16[512,512]{1,0:T(8,128)(2,1)S(1)} %all_gather.6), channel_id=1, source_target_pairs={{0,3},{1,0},{2,1},{3,2},{16,17},{17,18},{18,19},{19,16},{4,7},{5,4... | collective-permute-start | bytes 1572872 | tf_op jit(solution)/shard_map/ppermute | solution.py:135
  81.9 19.6 %collective-permute-start.3 = (bf16[512,512]{1,0:T(8,128)(2,1)S(1)}, bf16[512,512]{1,0:T(8,128)(2,1)S(1)}, u32[]{:S(2)}, u32[]{:S(2)}) collective-permute-start(bf16[512,512]{1,0:T(8,128)(2,1)S(1)} %all_gather.6), channel_id=1, source_target_pairs={{0,1},{1,2},{2,3},{3,0},{16,19},{17,16},{18,17},{19,18},{4,5},{5,6... | collective-permute-start | bytes 1572872 | tf_op jit(solution)/shard_map/ppermute | solution.py:135
  101.6 9.7 %collective-permute-start.4 = (bf16[4,512,512]{2,1,0:T(8,128)(2,1)}, bf16[4,512,512]{2,1,0:T(8,128)(2,1)S(1)}, u32[]{:S(2)}, u32[]{:S(2)}) collective-permute-start(bf16[4,512,512]{2,1,0:T(8,128)(2,1)} %all-to-all-done.1), channel_id=1, source_target_pairs={{0,16},{16,0},{1,17},{17,1},{2,18},{18,2},{3,19},{19,3},{4,20},{20... | collective-permute-start | bytes 6291464 | tf_op jit(solution)/shard_map/ppermute | solution.py:152

commit v15 on v12

--- a/solution.py
+++ b/solution.py
@@ -129,14 +129,9 @@
     return lax.ppermute(value, axis, [(i, (i + by) % RING) for i in range(RING)])
 
 
-def joined(axis, pieces):
-    me = lax.axis_index(axis)
-    depth, width = pieces[0].shape
-    whole = jnp.zeros((RING * depth, width), pieces[0].dtype)
-    for ahead in (0, 2, 1, 3):
-        start = ((me + ahead) & (RING - 1)) * depth
-        whole = lax.dynamic_update_slice(whole, pieces[ahead], (start, 0))
-    return whole
+def placed(whole, axis, ahead, piece):
+    start = ((lax.axis_index(axis) + ahead) & (RING - 1)) * piece.shape[0]
+    return lax.dynamic_update_slice(whole, piece, (start, 0))
 
 
 def copies(value):
@@ -177,8 +172,11 @@
     near = exchange(copies(cols), "y")
     pieces = [shift(rows, "x", -ahead) for ahead in (2, 1, 3)]
     opposite, after, before = pieces
-    rows = joined("x", (rows, after, opposite, before))
-    near, rows = lax.optimization_barrier((near, rows))
+    whole = jnp.zeros((RING * rows.shape[0], rows.shape[1]), rows.dtype)
+    for ahead, piece in ((0, rows), (2, opposite), (1, after)):
+        whole = placed(whole, "x", ahead, piece)
+    near, whole, before = lax.optimization_barrier((near, whole, before))
+    rows = placed(whole, "x", 3, before)
     far = swap_cores(near)
     near, far = (v.reshape(-1, v.shape[2]) for v in (near, far))
     core = lax.axis_index("core").astype(jnp.int32).reshape(1)

time: 114 us -> 116 us (1.018)
  no operation moved by 1% of the time
where the time goes in v15:
time: 116 us; the launch traced here: 115 us
  blocking collectives  51.4 us (44%)
  starting transfers between devices  29.8 us (26%)
  waiting for transfers between devices  16.6 us (14%)
  Pallas kernels  10.5 us (9%)
  local copies, waits for them, and re-layouts  5.78 us (5%)
    all_gather x1, blocking collectives, on_device(): rows = lax.all_gather(attended, 'zh', axis=0, tiled=True)  32.7 us
    all_gather x1, blocking collectives, on_device(): lax.all_gather(chunk, ('zl', 'zh'), axis=0, tiled=True, axis_index_groups...  18.7 us
    ppermute x3, waiting for transfers between devices, shift(): lax.ppermute(value, axis, [(i, (i + by) % RING) for i in range(RING)])  12.5 us
    ppermute x3, starting transfers between devices, shift(): lax.ppermute(value, axis, [(i, (i + by) % RING) for i in range(RING)])  11.9 us
    all_to_all x2, starting transfers between devices, exchange(): return lax.all_to_all(value, axis, split_axis=0, concat_axis=0, tiled=True)  9.3 us
    pallas_call x2, Pallas kernels, hessian_half(): pl.pallas_call(half_kernel, out_shape=jax.ShapeDtypeStruct((width, 2 * ha...  7.11 us
    ppermute x1, starting transfers between devices, swap_cores(): return lax.ppermute(value, 'core', [(0, 1), (1, 0)])  7.09 us
    all_to_all x2, waiting for transfers between devices, exchange(): return lax.all_to_all(value, axis, split_axis=0, concat_axis=0, tiled=True)  3.69 us
  transfers between devices with their start and end apart: 7, of which 4 were waited for; matrix products, arithmetic and copies ran while one was open for 4% of the time, Pallas kernels for 3%

profile of v15, /device:TPU:1, one launch (start us, length us, event | category | flops | bytes accessed | tf_op | source)
XLA Modules:
  0.0 114.9 jit_solution(5037642092849025653)
XLA Ops:
  0.7 1.5 %pack.1 = bf16[4,272,128]{2,1,0:T(8,128)(2,1)} custom-call(s32[1]{0:T(128)} %bitcast.2.g_ref, bf16[128,1024]{1,0:T(8,128)(2,1)} %k_ref.1, bf16[128,1024]{1,0:T(8,128)(2,1)} %v_ref.1, s32[1,128]{1,0:T(1,128)} %bitcast.10), custom_call_target="tpu_custom_call" | custom-call | tf_op jit(solution)/shard_map/pack/pallas_call | solution.py:37
  2.2 4.8 %all-to-all-start = ((bf16[4,272,128]{2,1,0:T(8,128)(2,1)}), bf16[4,272,128]{2,1,0:T(8,128)(2,1)S(1)}, u32[]{:S(2)}, u32[]{:S(2)}) async-start(bf16[4,272,128]{2,1,0:T(8,128)(2,1)} %pack.1), calls=%async_computation | async-start | bytes 557056 | tf_op jit(solution)/shard_map/all_to_all | solution.py:146
  7.0 1.0 copy.8
  8.0 0.1 copy.9
  8.2 0.8 copy.10.p_ref
  9.0 3.7 %all-to-all-done.kv_ref = bf16[4,272,128]{2,1,0:T(8,128)(2,1)S(1)} async-done(((bf16[4,272,128]{2,1,0:T(8,128)(2,1)}), bf16[4,272,128]{2,1,0:T(8,128)(2,1)S(1)}, u32[]{:S(2)}, u32[]{:S(2)}) %all-to-all-start) | async-done | bytes 278560 | tf_op jit(solution)/shard_map/all_to_all | solution.py:146
  12.6 1.8 %attend.1 = bf16[128,512]{1,0:T(8,128)(2,1)} custom-call(bf16[4,128,128]{2,1,0:T(8,128)(2,1)S(1)} %bitcast.8, bf16[4,272,128]{2,1,0:T(8,128)(2,1)S(1)} %all-to-all-done.kv_ref, s32[128,1]{1,0:T(8,128)S(1)} %copy.10.p_ref), custom_call_target="tpu_custom_call" | custom-call | tf_op jit(solution)/shard_map/attend/pallas_call | solution.py:81
  14.5 1.6 %collective-permute-start = (bf16[128,512]{1,0:T(8,128)(2,1)}, bf16[128,512]{1,0:T(8,128)(2,1)S(1)}, u32[]{:S(2)}, u32[]{:S(2)}) collective-permute-start(bf16[128,512]{1,0:T(8,128)(2,1)} %attend.1), channel_id=1, source_target_pairs={{0,0},{1,32},{2,64},{3,96},{4,256},{5,288},{6,320},{7,352},{8,384}... | collective-permute-start | bytes 393224 | tf_op jit(solution)/shard_map/ppermute | solution.py:154
  16.0 32.7 %all_gather.6 = bf16[512,512]{1,0:T(8,128)(2,1)S(1)} all-gather(bf16[128,512]{1,0:T(8,128)(2,1)} %attend.1), channel_id=1, replica_groups=mesh['zl'=4,'y'=4,'core'=2,'zh'=4,'x'=4] {'zh'}, dimensions={0}, use_global_device_ids=true | all-gather | bytes 655360 | tf_op jit(solution)/shard_map/all_gather | solution.py:167
  48.8 18.7 %all_gather.7 = bf16[512,512]{1,0:T(8,128)(2,1)S(1)} all-gather(bf16[128,512]{1,0:T(8,128)(2,1)S(1)} %collective-permute-done), channel_id=1, replica_groups={{0,256,384,128},{132,388,260,4},{392,136,8,264},{268,12,140,396},{1,257..., dimensions={0}, use_global_device_ids=true | all-gather | bytes 655360 | tf_op jit(solution)/shard_map/all_gather | solution.py:170
  67.4 1.5 %broadcast_in_dim.4 = bf16[4,512,512]{2,1,0:T(8,128)(2,1)} broadcast(bf16[512,512]{1,0:T(8,128)(2,1)S(1)} %all_gather.7), dimensions={1,2} | broadcast | bytes 2621440 | tf_op jit(solution)/shard_map/broadcast_in_dim | solution.py:138
  68.9 4.5 %all-to-all-start.1 = ((bf16[4,512,512]{2,1,0:T(8,128)(2,1)}), bf16[4,512,512]{2,1,0:T(8,128)(2,1)}, u32[]{:S(2)}, u32[]{:S(2)}) async-start(bf16[4,512,512]{2,1,0:T(8,128)(2,1)} %broadcast_in_dim.4), calls=%async_computation.1 | async-start | bytes 4194304 | tf_op jit(solution)/shard_map/all_to_all | solution.py:146
  73.4 6.6 %collective-permute-start.1 = (bf16[512,512]{1,0:T(8,128)(2,1)S(1)}, bf16[512,512]{1,0:T(8,128)(2,1)}, u32[]{:S(2)}, u32[]{:S(2)}) collective-permute-start(bf16[512,512]{1,0:T(8,128)(2,1)S(1)} %all_gather.6), channel_id=1, source_target_pairs={{0,2},{1,3},{2,0},{3,1},{4,6},{5,7},{6,4},{7,5},{8,10},{9,11},{10,... | collective-permute-start | bytes 1572872 | tf_op jit(solution)/shard_map/ppermute | solution.py:129
  80.0 1.9 %collective-permute-start.2 = (bf16[512,512]{1,0:T(8,128)(2,1)S(1)}, bf16[512,512]{1,0:T(8,128)(2,1)}, u32[]{:S(2)}, u32[]{:S(2)}) collective-permute-start(bf16[512,512]{1,0:T(8,128)(2,1)S(1)} %all_gather.6), channel_id=1, source_target_pairs={{0,3},{1,0},{2,1},{3,2},{4,7},{5,4},{6,5},{7,6},{8,11},{9,8},{10,9... | collective-permute-start | bytes 1572872 | tf_op jit(solution)/shard_map/ppermute | solution.py:129
  81.9 3.4 %collective-permute-start.3 = (bf16[512,512]{1,0:T(8,128)(2,1)S(1)}, bf16[512,512]{1,0:T(8,128)(2,1)S(1)}, u32[]{:S(2)}, u32[]{:S(2)}) collective-permute-start(bf16[512,512]{1,0:T(8,128)(2,1)S(1)} %all_gather.6), channel_id=1, source_target_pairs={{0,1},{1,2},{2,3},{3,0},{4,5},{5,6},{6,7},{7,4},{8,9},{9,10},{10,1... | collective-permute-start | bytes 1572872 | tf_op jit(solution)/shard_map/ppermute | solution.py:129
  85.3 0.1 broadcast_in_dim.10
  85.5 1.2 %collective-permute-done.1 = bf16[512,512]{1,0:T(8,128)(2,1)} collective-permute-done((bf16[512,512]{1,0:T(8,128)(2,1)S(1)}, bf16[512,512]{1,0:T(8,128)(2,1)}, u32[]{:S(2)}, u32[]{:S(2)}) %collective-permute-start.1) | collective-permute-done | bytes 524320 | tf_op jit(solution)/shard_map/ppermute | solution.py:129
  86.7 1.1 constant_dynamic-update-slice_fusion.2
  87.7 11.3 %collective-permute-done.2 = bf16[512,512]{1,0:T(8,128)(2,1)} collective-permute-done((bf16[512,512]{1,0:T(8,128)(2,1)S(1)}, bf16[512,512]{1,0:T(8,128)(2,1)}, u32[]{:S(2)}, u32[]{:S(2)}) %collective-permute-start.2) | collective-permute-done | bytes 524320 | tf_op jit(solution)/shard_map/ppermute | solution.py:129
  99.0 1.1 constant_dynamic-update-slice_fusion.1
  100.1 7.1 %collective-permute-start.4 = (bf16[4,512,512]{2,1,0:T(8,128)(2,1)}, bf16[4,512,512]{2,1,0:T(8,128)(2,1)}, u32[]{:S(2)}, u32[]{:S(2)}) collective-permute-start(bf16[4,512,512]{2,1,0:T(8,128)(2,1)} %all-to-all-done.1), channel_id=1, source_target_pairs={{0,16},{16,0},{1,17},{17,1},{2,18},{18,2},{3,19},{19,3},{4,20},{20... | collective-permute-start | bytes 6291464 | tf_op jit(solution)/shard_map/ppermute | solution.py:142
  107.3 3.6 %hessian_half.2.rest_0_ = f32[512,1024]{1,0:T(8,128)} custom-call(s32[1]{0:T(128)} %bitcast.5.s_ref, bf16[2048,512]{1,0:T(8,128)(2,1)S(1)} %constant_dynamic-update-slice_fusion.rows_ref, bf16[2048,512]{1,0:T(8,128)(2,1)} %bitcast.7.cols_ref), custom_call_target="tpu_custom_call" | custom-call | tf_op jit(solution)/shard_map/hessian_half/pallas_call | solution.py:113
  110.8 0.5 collective-permute-done.4
  111.3 3.5 %hessian_half.3 = f32[512,1024]{1,0:T(8,128)} custom-call(s32[1]{0:T(128)S(6)} %sub.8.s_ref, bf16[2048,512]{1,0:T(8,128)(2,1)S(1)} %constant_dynamic-update-slice_fusion.rows_ref, bf16[2048,512]{1,0:T(8,128)(2,1)} %bitcast.6.cols_ref, f32[512,1024]{1,0:T(8,128)} %hessian_half.2.rest_0_), custom_call_target="tpu_custom_call", output_to_operand_aliasing={{}: (3, {})} | custom-call | tf_op jit(solution)/shard_map/hessian_half/pallas_call | solution.py:113
  (5 shorter events, 0.1 us)
Async XLA Ops:
  2.2 10.5 %all-to-all-start = ((bf16[4,272,128]{2,1,0:T(8,128)(2,1)}), bf16[4,272,128]{2,1,0:T(8,128)(2,1)S(1)}, u32[]{:S(2)}, u32[]{:S(2)}) async-start(bf16[4,272,128]{2,1,0:T(8,128)(2,1)} %pack.1), calls=%async_computation | async-start | bytes 557056 | tf_op jit(solution)/shard_map/all_to_all | solution.py:146
  14.5 34.3 %collective-permute-start = (bf16[128,512]{1,0:T(8,128)(2,1)}, bf16[128,512]{1,0:T(8,128)(2,1)S(1)}, u32[]{:S(2)}, u32[]{:S(2)}) collective-permute-start(bf16[128,512]{1,0:T(8,128)(2,1)} %attend.1), channel_id=1, source_target_pairs={{0,0},{1,32},{2,64},{3,96},{4,256},{5,288},{6,320},{7,352},{8,384}... | collective-permute-start | bytes 393224 | tf_op jit(solution)/shard_map/ppermute | solution.py:154
  68.9 31.2 %all-to-all-start.1 = ((bf16[4,512,512]{2,1,0:T(8,128)(2,1)}), bf16[4,512,512]{2,1,0:T(8,128)(2,1)}, u32[]{:S(2)}, u32[]{:S(2)}) async-start(bf16[4,512,512]{2,1,0:T(8,128)(2,1)} %broadcast_in_dim.4), calls=%async_computation.1 | async-start | bytes 4194304 | tf_op jit(solution)/shard_map/all_to_all | solution.py:146
  73.4 13.3 %collective-permute-start.1 = (bf16[512,512]{1,0:T(8,128)(2,1)S(1)}, bf16[512,512]{1,0:T(8,128)(2,1)}, u32[]{:S(2)}, u32[]{:S(2)}) collective-permute-start(bf16[512,512]{1,0:T(8,128)(2,1)S(1)} %all_gather.6), channel_id=1, source_target_pairs={{0,2},{1,3},{2,0},{3,1},{4,6},{5,7},{6,4},{7,5},{8,10},{9,11},{10,... | collective-permute-start | bytes 1572872 | tf_op jit(solution)/shard_map/ppermute | solution.py:129
  80.0 19.0 %collective-permute-start.2 = (bf16[512,512]{1,0:T(8,128)(2,1)S(1)}, bf16[512,512]{1,0:T(8,128)(2,1)}, u32[]{:S(2)}, u32[]{:S(2)}) collective-permute-start(bf16[512,512]{1,0:T(8,128)(2,1)S(1)} %all_gather.6), channel_id=1, source_target_pairs={{0,3},{1,0},{2,1},{3,2},{4,7},{5,4},{6,5},{7,6},{8,11},{9,8},{10,9... | collective-permute-start | bytes 1572872 | tf_op jit(solution)/shard_map/ppermute | solution.py:129
  81.9 18.2 %collective-permute-start.3 = (bf16[512,512]{1,0:T(8,128)(2,1)S(1)}, bf16[512,512]{1,0:T(8,128)(2,1)S(1)}, u32[]{:S(2)}, u32[]{:S(2)}) collective-permute-start(bf16[512,512]{1,0:T(8,128)(2,1)S(1)} %all_gather.6), channel_id=1, source_target_pairs={{0,1},{1,2},{2,3},{3,0},{4,5},{5,6},{6,7},{7,4},{8,9},{9,10},{10,1... | collective-permute-start | bytes 1572872 | tf_op jit(solution)/shard_map/ppermute | solution.py:129
  100.1 11.2 %collective-permute-start.4 = (bf16[4,512,512]{2,1,0:T(8,128)(2,1)}, bf16[4,512,512]{2,1,0:T(8,128)(2,1)}, u32[]{:S(2)}, u32[]{:S(2)}) collective-permute-start(bf16[4,512,512]{2,1,0:T(8,128)(2,1)} %all-to-all-done.1), channel_id=1, source_target_pairs={{0,16},{16,0},{1,17},{17,1},{2,18},{18,2},{3,19},{19,3},{4,20},{20... | collective-permute-start | bytes 6291464 | tf_op jit(solution)/shard_map/ppermute | solution.py:142
